TPU v7x, 32 devices: a whole 2x2x4 slice. The times are simulated.
32 devices in a mesh: dp: 4 (over y, core), expert: 8 (over z, x).
Axes of the slice: x: 2, y: 2, z: 4, core: 2. Of those that a mesh axis runs over, the one named last changes fastest.
Arguments:
- tokens: bfloat16 [2, 2048, 1024], P(None, ('dp', 'expert')), may hold values from -6 to 6
- cotangent: bfloat16 [2, 2048, 1024], P(None, ('dp', 'expert')), may hold values from -6 to 6
- segments: int32 [2, 32, 64], P(None, ('dp', 'expert')), may hold values from 0 to 3, never falling along the last dimension, each value on 1 to 32 neighbouring positions
- value_picks: int32 [2, 2048, 4, 2], P(None, ('dp', 'expert')), may hold values from 0 to 4, all different within a row
- output_picks: int32 [2, 2048, 4, 2], P(None, ('dp', 'expert')), may hold values from 0 to 4, all different within a row
- expert_picks: int32 [2, 2048, 16], P(None, ('dp', 'expert')), may hold values from 0 to 127, all different within a row; in each aligned block of 64 rows (0 to 63, 64 to 127, ..., all dimensions but the last counted through in order) at most 16 rows name the same one
- attn_gain: bfloat16 [1024], P('dp'), may hold values from 0.5 to 2
- query_weight: bfloat16 [1024, 512], P('dp'), may hold values from -0.1875 to 0.1875
- key_weight: bfloat16 [1024, 512], P('dp'), may hold values from -0.1875 to 0.1875
- value_weight: bfloat16 [1024, 2560], P('dp'), may hold values from -0.1875 to 0.1875
- output_expert_weight: bfloat16 [1024, 2560], P('dp'), may hold values from -1 to 1
- value_select: bfloat16 [1024, 20], P('dp'), may hold values from -0.125 to 0.125
- output_select: bfloat16 [1024, 20], P('dp'), may hold values from -0.125 to 0.125
- moe_gain: bfloat16 [1024], P('dp'), may hold values from 0.5 to 2
- router_weight: bfloat16 [1024, 128], P('dp'), may hold values from -0.09375 to 0.09375
- up_weight: bfloat16 [128, 1024, 128], P('expert', 'dp'), may hold values from -0.1875 to 0.1875
- down_weight: bfloat16 [128, 128, 1024], P('expert', None, 'dp'), may hold values from -0.25 to 0.25
Outputs:
- output: float32 [2, 2048, 1024], P(None, ('dp', 'expert'))
- grad_tokens: float32 [2, 2048, 1024], P(None, ('dp', 'expert'))
- grad_attn_gain: float32 [1024], P(('dp', 'expert'))
- grad_query_weight: float32 [1024, 512], P(('dp', 'expert'))
- grad_key_weight: float32 [1024, 512], P(('dp', 'expert'))
- grad_value_weight: float32 [1024, 2560], P(('dp', 'expert'))
- grad_output_weight: float32 [1024, 2560], P(('dp', 'expert'))
- grad_value_select: float32 [1024, 20], P(('dp', 'expert'))
- grad_output_select: float32 [1024, 20], P(('dp', 'expert'))
- grad_moe_gain: float32 [1024], P(('dp', 'expert'))
- grad_router_weight: float32 [1024, 128], P(('dp', 'expert'))
- grad_up_weight: float32 [128, 1024, 128], P('expert', 'dp')
- grad_down_weight: float32 [128, 128, 1024], P('expert', None, 'dp')
Inputs may be any that keep to these rules, and one draw needn't show every extreme that they name: `expert_picks`: each token names 16 different experts. Among the 64 tokens of one row of one micro-batch no expert is named more than 16 times, and in some rows an expert is named exactly 16 times. `value_picks`: for each token and head, 2 different experts. `output_picks`: for each token and head, 2 different experts. `segments`: along each row of 64 tokens the numbers never fall; a segment spans at most half a row.
All inputs are finite; a program needn't handle non-finite values.
Results may differ from a plain program's by a relative error of at most 0.013.
The roundings to bfloat16 on the way count: a program that leaves them out, or rounds other values in their place, can miss the bound.
Values may be sent and summed in bfloat16 or wider, within the bound.
No kernel may reach another device: no remote copies, remote signals or barrier semaphores. Data moves between devices by JAX's collectives and lax.ppermute only.
A program may use at most 192 MiB of HBM per device.

v0:
```python
import jax
import jax.numpy as jnp
from jax import lax
from jax.sharding import PartitionSpec as P

H = 4
DH = 128
EA = 5
TOP = 16
EXPERTS = 128
CAP = 16


EPSILON = 1e-05
MASKED = -1e30


def matmul(matrix_a, matrix_b):
    return jnp.dot(matrix_a, matrix_b, preferred_element_type=jnp.float32)


def product_rows(matrix_a, matrix_b):
    return lax.dot_general(
        matrix_a, matrix_b, (((0,), (0,)), ((), ())), preferred_element_type=jnp.float32
    )


def matmul_cols(matrix_a, matrix_b):
    return lax.dot_general(
        matrix_a, matrix_b, (((1,), (1,)), ((), ())), preferred_element_type=jnp.float32
    )


def norm_forward(layer_inputs, norm_gain):
    centered = layer_inputs - jnp.mean(layer_inputs, axis=-1, keepdims=True)
    inverse_std = lax.rsqrt(jnp.mean(centered * centered, axis=-1, keepdims=True) + EPSILON)
    unit_rows = centered * inverse_std
    return (unit_rows * norm_gain, unit_rows, inverse_std)


def norm_backward(grad_normed, norm_gain, unit_rows, inverse_std):
    grad_gain = jnp.sum(grad_normed * unit_rows, axis=0)
    grad_unit = grad_normed * norm_gain
    grad_input = inverse_std * (
        grad_unit
        - jnp.mean(grad_unit, axis=-1, keepdims=True)
        - unit_rows * jnp.mean(grad_unit * unit_rows, axis=-1, keepdims=True)
    )
    return (grad_input, grad_gain)


def pick_mask(chosen, number):
    matches = chosen[..., None] == jnp.arange(number, dtype=jnp.int32)
    return jnp.sum(matches.astype(jnp.float32), axis=-2)


def add_trees(first_tree, second_tree):
    if first_tree is None:
        return second_tree
    return tuple(
        (first_part + second_part for first_part, second_part in zip(first_tree, second_tree))
    )


def per_device(
    tokens,
    cotangent,
    segments,
    value_picks,
    output_picks,
    expert_picks,
    attn_gain,
    query_weight,
    key_weight,
    value_weight,
    output_expert_weight,
    value_select,
    output_select,
    moe_gain,
    router_weight,
    up_weight,
    down_weight,
):
    micro_count = tokens.shape[0]
    length = tokens.shape[1]
    width = tokens.shape[2]
    owners = lax.axis_size("expert")
    local_experts = EXPERTS // owners
    mixed_width = H * EA * DH
    scale = DH ** (-0.5)
    positions = jnp.arange(length, dtype=jnp.int32)
    causal = positions[None, :] <= positions[:, None]
    expert_ids = jnp.arange(EXPERTS, dtype=jnp.int32)
    outputs = []
    grad_inputs = []
    attn_totals = None
    expert_totals = None
    for micro_step in range(micro_count):
        attn_full = (
            lax.all_gather(attn_gain, "dp", axis=0, tiled=True),
            lax.all_gather(query_weight, "dp", axis=0, tiled=True),
            lax.all_gather(key_weight, "dp", axis=0, tiled=True),
            lax.all_gather(value_weight, "dp", axis=0, tiled=True),
            lax.all_gather(output_expert_weight, "dp", axis=0, tiled=True),
            lax.all_gather(value_select, "dp", axis=0, tiled=True),
            lax.all_gather(output_select, "dp", axis=0, tiled=True),
            lax.all_gather(moe_gain, "dp", axis=0, tiled=True),
            lax.all_gather(router_weight, "dp", axis=0, tiled=True),
        )
        gain_one = attn_full[0].astype(jnp.float32)
        query_full = attn_full[1]
        key_full = attn_full[2]
        value_full = attn_full[3]
        output_full = attn_full[4]
        select_value = attn_full[5]
        select_output = attn_full[6]
        gain_two = attn_full[7].astype(jnp.float32)
        router_full = attn_full[8]
        up_full, down_full = (
            lax.all_gather(up_weight, "dp", axis=1, tiled=True),
            lax.all_gather(down_weight, "dp", axis=2, tiled=True),
        )
        inputs_bf = tokens[micro_step]
        inputs_f = inputs_bf.astype(jnp.float32)
        normed_one, unit_one, inverse_one = norm_forward(inputs_f, gain_one)
        normed_brain_float = normed_one.astype(jnp.bfloat16)
        queries = matmul(normed_brain_float, query_full).astype(jnp.bfloat16).reshape(length, H, DH)
        keys_all = matmul(normed_brain_float, key_full).astype(jnp.bfloat16).reshape(length, H, DH)
        value_sig = jax.nn.sigmoid(matmul(normed_brain_float, select_value))
        output_sig = jax.nn.sigmoid(matmul(normed_brain_float, select_output))
        value_mask = pick_mask(value_picks[micro_step], EA).reshape(length, H * EA)
        output_mask = pick_mask(output_picks[micro_step], EA).reshape(length, H * EA)
        value_gate = (value_sig * value_mask).reshape(length, H, EA, 1)
        output_gate = (output_sig * output_mask).reshape(length, H, EA, 1)
        value_all = matmul(inputs_bf, value_full).reshape(length, H, EA, DH)
        values = jnp.sum(value_gate * value_all, axis=2).astype(jnp.bfloat16)
        row_segments = segments[micro_step, 0]
        allowed = (causal & (row_segments[:, None] == row_segments[None, :]))[None]
        raw_scores = jnp.einsum(
            "qhd,khd->hqk", queries, keys_all, preferred_element_type=jnp.float32
        )
        scaled = jnp.where(allowed, raw_scores * scale, MASKED)
        row_max = jnp.max(scaled, axis=-1, keepdims=True)
        expo = jnp.where(allowed, jnp.exp(scaled - row_max), 0.0)
        row_total = jnp.sum(expo, axis=-1, keepdims=True)
        probs = expo / row_total
        log_total = row_max + jnp.log(row_total)
        attended = jnp.einsum(
            "hqk,khd->qhd", probs.astype(jnp.bfloat16), values, preferred_element_type=jnp.float32
        )
        mixed_heads = (
            (output_gate * attended[:, :, None, :])
            .reshape(length, mixed_width)
            .astype(jnp.bfloat16)
        )
        residual_branch = matmul_cols(mixed_heads, output_full)
        resid = inputs_f + residual_branch
        resid_bf = resid.astype(jnp.bfloat16)
        normed_two, unit_two, inverse_two = norm_forward(resid, gain_two)
        normed_two_bf = normed_two.astype(jnp.bfloat16)
        router_gate = jax.nn.sigmoid(matmul(normed_two_bf, router_full))
        chosen = expert_picks[micro_step]
        matches = chosen[:, :, None] == expert_ids
        per_token = jnp.sum(matches.astype(jnp.int32), axis=1, dtype=jnp.int32)
        earlier = jnp.cumsum(per_token, axis=0, dtype=jnp.int32) - per_token
        slots = jnp.sum(jnp.where(matches, earlier[:, None, :], 0), axis=2, dtype=jnp.int32)
        pair_gate = jnp.sum(jnp.where(matches, router_gate[:, None, :], 0.0), axis=2)
        send_rows = (
            jnp.zeros((EXPERTS, CAP, width), jnp.bfloat16)
            .at[chosen, slots]
            .set(jnp.broadcast_to(resid_bf[:, None, :], (length, TOP, width)))
        )
        received = lax.all_to_all(
            send_rows, "expert", split_axis=0, concat_axis=0, tiled=True
        ).reshape(owners, local_experts, CAP, width)
        pre_act = jnp.einsum(
            "jecd,edf->jecf", received, up_full, preferred_element_type=jnp.float32
        )
        pre_sig = jax.nn.sigmoid(pre_act)
        hidden = (pre_act * pre_sig).astype(jnp.bfloat16)
        expert_out = (
            jnp.einsum("jecf,efd->jecd", hidden, down_full, preferred_element_type=jnp.float32)
            .astype(jnp.bfloat16)
            .reshape(EXPERTS, CAP, width)
        )
        returned = lax.all_to_all(expert_out, "expert", split_axis=0, concat_axis=0, tiled=True)
        pair_out = returned[chosen, slots]
        outputs.append(
            resid + jnp.sum(pair_gate[:, :, None] * pair_out.astype(jnp.float32), axis=1)
        )
        grad_out = cotangent[micro_step].astype(jnp.float32)
        gate_grad = jnp.sum(pair_out.astype(jnp.float32) * grad_out[:, None, :], axis=2)
        pair_grad = (pair_gate[:, :, None] * grad_out[:, None, :]).astype(jnp.bfloat16)
        send_grad = jnp.zeros((EXPERTS, CAP, width), jnp.bfloat16).at[chosen, slots].set(pair_grad)
        recv_grad = lax.all_to_all(
            send_grad, "expert", split_axis=0, concat_axis=0, tiled=True
        ).reshape(owners, local_experts, CAP, width)
        grad_down_part = jnp.einsum(
            "jecf,jecd->efd", hidden, recv_grad, preferred_element_type=jnp.float32
        )
        grad_hidden = jnp.einsum(
            "jecd,efd->jecf", recv_grad, down_full, preferred_element_type=jnp.float32
        )
        pre_grad = (grad_hidden * pre_sig * (1.0 + pre_act * (1.0 - pre_sig))).astype(jnp.bfloat16)
        grad_up_part = jnp.einsum(
            "jecd,jecf->edf", received, pre_grad, preferred_element_type=jnp.float32
        )
        grad_rows = (
            jnp.einsum("jecf,edf->jecd", pre_grad, up_full, preferred_element_type=jnp.float32)
            .astype(jnp.bfloat16)
            .reshape(EXPERTS, CAP, width)
        )
        back_rows = lax.all_to_all(grad_rows, "expert", split_axis=0, concat_axis=0, tiled=True)
        from_experts = jnp.sum(back_rows[chosen, slots].astype(jnp.float32), axis=1)
        router_sum = jnp.sum(jnp.where(matches, gate_grad[:, :, None], 0.0), axis=1)
        router_grad = (router_sum * router_gate * (1.0 - router_gate)).astype(jnp.bfloat16)
        grad_router_part = product_rows(normed_two_bf, router_grad)
        grad_normed_two = matmul_cols(router_grad, router_full)
        from_norm_two, grad_gain_two = norm_backward(
            grad_normed_two, gain_two, unit_two, inverse_two
        )
        resid_grad = grad_out + from_experts + from_norm_two
        branch_grad = resid_grad.astype(jnp.bfloat16)
        grad_output_part = product_rows(branch_grad, mixed_heads)
        mixed_grad = matmul(branch_grad, output_full).reshape(length, H, EA, DH)
        attended_grad = jnp.sum(output_gate * mixed_grad, axis=2).astype(jnp.bfloat16)
        out_gate_grad = (
            jnp.sum(mixed_grad * attended[:, :, None, :], axis=3).reshape(length, H * EA)
            * output_mask
        )
        output_logit_grad = (out_gate_grad * output_sig * (1.0 - output_sig)).astype(jnp.bfloat16)
        raw_again = jnp.einsum(
            "qhd,khd->hqk", queries, keys_all, preferred_element_type=jnp.float32
        )
        probs_again = jnp.where(allowed, jnp.exp(raw_again * scale - log_total), 0.0)
        values_grad = jnp.einsum(
            "hqk,qhd->khd",
            probs_again.astype(jnp.bfloat16),
            attended_grad,
            preferred_element_type=jnp.float32,
        )
        probs_grad = jnp.einsum(
            "qhd,khd->hqk", attended_grad, values, preferred_element_type=jnp.float32
        )
        delta_rows = jnp.sum(probs_again * probs_grad, axis=-1, keepdims=True)
        score_grad = (probs_again * (probs_grad - delta_rows) * scale).astype(jnp.bfloat16)
        queries_grad = (
            jnp.einsum("hqk,khd->qhd", score_grad, keys_all, preferred_element_type=jnp.float32)
            .astype(jnp.bfloat16)
            .reshape(length, H * DH)
        )
        keys_grad = (
            jnp.einsum("hqk,qhd->khd", score_grad, queries, preferred_element_type=jnp.float32)
            .astype(jnp.bfloat16)
            .reshape(length, H * DH)
        )
        value_all_grad = (
            (value_gate * values_grad[:, :, None, :])
            .reshape(length, mixed_width)
            .astype(jnp.bfloat16)
        )
        value_gate_grad = (
            jnp.sum(values_grad[:, :, None, :] * value_all, axis=3).reshape(length, H * EA)
            * value_mask
        )
        value_logits_gradient = (value_gate_grad * value_sig * (1.0 - value_sig)).astype(
            jnp.bfloat16
        )
        grad_query_part = product_rows(normed_brain_float, queries_grad)
        grad_key_part = product_rows(normed_brain_float, keys_grad)
        value_choice_grad_part = product_rows(normed_brain_float, value_logits_gradient)
        grad_osel_part = product_rows(normed_brain_float, output_logit_grad)
        grad_value_part = product_rows(inputs_bf, value_all_grad)
        grad_normed_one = (
            matmul_cols(queries_grad, query_full)
            + matmul_cols(keys_grad, key_full)
            + matmul_cols(value_logits_gradient, select_value)
            + matmul_cols(output_logit_grad, select_output)
        )
        from_norm_one, grad_gain_one = norm_backward(
            grad_normed_one, gain_one, unit_one, inverse_one
        )
        grad_inputs.append(resid_grad + matmul_cols(value_all_grad, value_full) + from_norm_one)
        attn_grads = (
            grad_gain_one,
            grad_query_part,
            grad_key_part,
            grad_value_part,
            grad_output_part,
            value_choice_grad_part,
            grad_osel_part,
            grad_gain_two,
            grad_router_part,
        )
        expert_grads = (grad_up_part, grad_down_part)
        attn_totals = add_trees(attn_totals, attn_grads)
        expert_totals = add_trees(expert_totals, expert_grads)
    attn_totals = (
        lax.psum_scatter(attn_totals[0], ("dp", "expert"), scatter_dimension=0, tiled=True),
        lax.psum_scatter(attn_totals[1], ("dp", "expert"), scatter_dimension=0, tiled=True),
        lax.psum_scatter(attn_totals[2], ("dp", "expert"), scatter_dimension=0, tiled=True),
        lax.psum_scatter(attn_totals[3], ("dp", "expert"), scatter_dimension=0, tiled=True),
        lax.psum_scatter(attn_totals[4], ("dp", "expert"), scatter_dimension=0, tiled=True),
        lax.psum_scatter(attn_totals[5], ("dp", "expert"), scatter_dimension=0, tiled=True),
        lax.psum_scatter(attn_totals[6], ("dp", "expert"), scatter_dimension=0, tiled=True),
        lax.psum_scatter(attn_totals[7], ("dp", "expert"), scatter_dimension=0, tiled=True),
        lax.psum_scatter(attn_totals[8], ("dp", "expert"), scatter_dimension=0, tiled=True),
    )
    expert_totals = (
        lax.psum_scatter(
            expert_totals[0].astype(jnp.bfloat16), "dp", scatter_dimension=1, tiled=True
        ).astype(jnp.float32),
        lax.psum_scatter(
            expert_totals[1].astype(jnp.bfloat16), "dp", scatter_dimension=2, tiled=True
        ).astype(jnp.float32),
    )
    return (
        jnp.stack(outputs),
        jnp.stack(grad_inputs),
        attn_totals[0],
        attn_totals[1],
        attn_totals[2],
        attn_totals[3],
        attn_totals[4],
        attn_totals[5],
        attn_totals[6],
        attn_totals[7],
        attn_totals[8],
        expert_totals[0],
        expert_totals[1],
    )


def solution(mesh):
    placed = (
        P(None, ("dp", "expert"), None),
        P(None, ("dp", "expert"), None),
        P(None, ("dp", "expert"), None),
        P(None, ("dp", "expert"), None, None),
        P(None, ("dp", "expert"), None, None),
        P(None, ("dp", "expert"), None),
        P("dp"),
        P("dp", None),
        P("dp", None),
        P("dp", None),
        P("dp", None),
        P("dp", None),
        P("dp", None),
        P("dp"),
        P("dp", None),
        P("expert", "dp", None),
        P("expert", None, "dp"),
    )
    return jax.shard_map(
        per_device,
        mesh=mesh,
        in_specs=placed,
        out_specs=(
            P(None, ("dp", "expert"), None),
            P(None, ("dp", "expert"), None),
            P(("dp", "expert")),
            P(("dp", "expert"), None),
            P(("dp", "expert"), None),
            P(("dp", "expert"), None),
            P(("dp", "expert"), None),
            P(("dp", "expert"), None),
            P(("dp", "expert"), None),
            P(("dp", "expert")),
            P(("dp", "expert"), None),
            P("expert", "dp", None),
            P("expert", None, "dp"),
        ),
        check_vma=False,
    )
```

profile of v0, /device:TPU:0, one launch (start us, length us, event | category | flops | bytes accessed | tf_op | source)
XLA Modules:
  0.0 2201.5 jit_solution(13041282316002492647)
XLA Ops:
  16.8 6.0 all-gather
  23.4 5.5 all_gather.46
  31.4 5.4 all_gather.45
  40.1 7.4 all-gather.11.cloned.1.call-done
  49.3 40.2 %all-gather.9.cloned.1.call-done = bf16[1024,2560]{1,0:T(8,128)(2,1)} async-done(((bf16[256,2560]{1,0:T(8,128)(2,1)}), bf16[1024,2560]{1,0:T(8,128)(2,1)}) %all-gather.9.cloned.1.call-update) | async-done | bytes 5242896 | tf_op jit(solution)/shard_map/all_gather | solution.py:103
  89.5 8.0 copy.213
  97.5 5.6 multiply_reduce_fusion.7
  104.4 27.0 %all-gather.15.cloned.1.call-done = bf16[1024,2560]{1,0:T(8,128)(2,1)} async-done(((bf16[256,2560]{1,0:T(8,128)(2,1)}), bf16[1024,2560]{1,0:T(8,128)(2,1)}) %all-gather.15.cloned.1.call-update) | async-done | bytes 5242896 | tf_op jit(solution)/shard_map/all_gather | solution.py:104
  137.5 8.6 scatter_custom_fusion
  146.1 5.7 all-to-all-start
  155.7 5.0 multiply_reduce_fusion.6
  161.9 5.1 fusion.288
  168.9 8.7 scatter_custom_fusion.1
  177.6 67.9 %all-to-all-done = bf16[128,16,1024]{2,1,0:T(8,128)(2,1)} async-done(((bf16[128,16,1024]{2,1,0:T(8,128)(2,1)}), bf16[128,16,1024]{2,1,0:T(8,128)(2,1)}, u32[]{:S(2)}, u32[]{:S(2)}) %all-to-all-start) | async-done | bytes 4194336 | tf_op jit(solution)/shard_map/all_to_all | solution.py:173
  255.4 32.2 %all-gather.19.cloned.1.call-done = bf16[16,128,1024]{2,1,0:T(8,128)(2,1)} async-done(((bf16[16,128,256]{2,1,0:T(8,128)(2,1)}), bf16[16,128,1024]{2,1,0:T(8,128)(2,1)}) %all-gather.19.cloned.1.call-update) | async-done | bytes 4194320 | tf_op jit(solution)/shard_map/all_gather | solution.py:121
  293.5 49.4 %all-to-all-done.2 = bf16[128,16,1024]{2,1,0:T(8,128)(2,1)} async-done(((bf16[128,16,1024]{2,1,0:T(8,128)(2,1)}), bf16[128,16,1024]{2,1,0:T(8,128)(2,1)}, u32[]{:S(2)}, u32[]{:S(2)}) %all-to-all-start.2) | async-done | bytes 4194336 | tf_op jit(solution)/shard_map/all_to_all | solution.py:173
  356.3 83.8 %all-to-all-done.1 = bf16[128,16,1024]{2,1,0:T(8,128)(2,1)} async-done(((bf16[128,16,1024]{2,1,0:T(8,128)(2,1)}), bf16[128,16,1024]{2,1,0:T(8,128)(2,1)}, u32[]{:S(2)}, u32[]{:S(2)}) %all-to-all-start.1) | async-done | bytes 4194336 | tf_op jit(solution)/shard_map/all_to_all | solution.py:186
  444.9 5.1 all-gather.1
  450.0 5.8 all_gather.52
  456.9 15.1 gather_fusion
  478.1 8.7 scatter_custom_fusion.2
  486.8 50.6 %all-to-all-done.3 = bf16[128,16,1024]{2,1,0:T(8,128)(2,1)} async-done(((bf16[128,16,1024]{2,1,0:T(8,128)(2,1)}), bf16[128,16,1024]{2,1,0:T(8,128)(2,1)}, u32[]{:S(2)}, u32[]{:S(2)}) %all-to-all-start.3) | async-done | bytes 4194336 | tf_op jit(solution)/shard_map/all_to_all | solution.py:186
  537.4 5.1 all-to-all-start.4
  542.9 15.3 gather_fusion.1
  562.4 8.6 scatter_custom_fusion.3
  571.0 64.0 %all-to-all-done.4 = bf16[128,16,1024]{2,1,0:T(8,128)(2,1)} async-done(((bf16[128,16,1024]{2,1,0:T(8,128)(2,1)}), bf16[128,16,1024]{2,1,0:T(8,128)(2,1)}, u32[]{:S(2)}, u32[]{:S(2)}) %all-to-all-start.4) | async-done | bytes 4194336 | tf_op jit(solution)/shard_map/all_to_all | solution.py:195
  639.7 5.0 fusion.90
  648.5 83.8 %all-to-all-done.6 = bf16[128,16,1024]{2,1,0:T(8,128)(2,1)} async-done(((bf16[128,16,1024]{2,1,0:T(8,128)(2,1)}), bf16[128,16,1024]{2,1,0:T(8,128)(2,1)}, u32[]{:S(2)}, u32[]{:S(2)}) %all-to-all-start.6) | async-done | bytes 4194336 | tf_op jit(solution)/shard_map/all_to_all | solution.py:195
  746.0 83.7 %all-to-all-done.5 = bf16[128,16,1024]{2,1,0:T(8,128)(2,1)} async-done(((bf16[128,16,1024]{2,1,0:T(8,128)(2,1)}), bf16[128,16,1024]{2,1,0:T(8,128)(2,1)}, u32[]{:S(2)}, u32[]{:S(2)}) %all-to-all-start.5) | async-done | bytes 4194336 | tf_op jit(solution)/shard_map/all_to_all | solution.py:213
  837.5 6.8 fusion.139
  844.3 15.1 gather_fusion.2
  861.0 66.0 %all-to-all-done.7 = bf16[128,16,1024]{2,1,0:T(8,128)(2,1)} async-done(((bf16[128,16,1024]{2,1,0:T(8,128)(2,1)}), bf16[128,16,1024]{2,1,0:T(8,128)(2,1)}, u32[]{:S(2)}, u32[]{:S(2)}) %all-to-all-start.7) | async-done | bytes 4194336 | tf_op jit(solution)/shard_map/all_to_all | solution.py:213
  927.0 15.1 gather_fusion.3
  974.5 8.2 fusion.3
  986.7 5.7 fusion.2
  1008.1 5.4 add_bitcast_fusion
  1013.5 11.5 copy.276
  1027.6 5.4 convolution_add_fusion
  1039.6 37.9 %all-reduce.2 = (f32[1024]{0:T(1024)S(1)}, f32[1024]{0:T(1024)S(1)}) all-reduce(f32[1024]{0:T(1024)S(1)} %add.280, f32[1024]{0:T(1024)S(1)} %add.288), channel_id=2, replica_groups=mesh['dp'=4,'expert'=8] {'dp','expert'}, use_global_device_ids=true, to_apply=%region_56.57.clone | all-reduce | flops 2048 | bytes 16384
  1087.7 16.5 reduce-scatter.30.cloned.1.call-done
  1105.5 130.8 %reduce-scatter.32.cloned.1.call-done = f32[32,20]{1,0:T(8,128)} async-done(((f32[1024,20]{1,0:T(8,128)}), f32[32,20]{1,0:T(8,128)}) %reduce-scatter.32.cloned.1.call-update) | async-done | bytes 2576
  1237.8 42.0 %reduce-scatter.24.cloned.1.call-done = bf16[16,256,128]{2,1,0:T(8,128)(2,1)} async-done(((bf16[16,1024,128]{2,1,0:T(8,128)(2,1)}), bf16[16,256,128]{2,1,0:T(8,128)(2,1)}) %reduce-scatter.24.cloned.1.call-update) | async-done | bytes 1048592 | tf_op jit(solution)/shard_map/reduce_scatter | solution.py:310
  1282.5 44.3 %reduce-scatter.26.cloned.1.call-done = bf16[16,128,256]{2,1,0:T(8,128)(2,1)} async-done(((bf16[16,128,1024]{2,1,0:T(8,128)(2,1)}), bf16[16,128,256]{2,1,0:T(8,128)(2,1)}) %reduce-scatter.26.cloned.1.call-update) | async-done | bytes 1048592 | tf_op jit(solution)/shard_map/reduce_scatter | solution.py:313
  1329.6 134.0 %reduce-scatter.22.cloned.1.call-done = f32[32,128]{1,0:T(8,128)} async-done(((f32[1024,128]{1,0:T(8,128)}), f32[32,128]{1,0:T(8,128)}) %reduce-scatter.22.cloned.1.call-update) | async-done | bytes 16400 | tf_op jit(solution)/shard_map/reduce_scatter | solution.py:307
  1463.6 136.8 %reduce-scatter.16.cloned.1.call-done = f32[32,512]{1,0:T(8,128)} async-done(((f32[1024,512]{1,0:T(8,128)}), f32[32,512]{1,0:T(8,128)}) %reduce-scatter.16.cloned.1.call-update) | async-done | bytes 65552 | tf_op jit(solution)/shard_map/reduce_scatter | solution.py:300
  1600.4 137.1 %reduce-scatter.18.cloned.1.call-done = f32[32,512]{1,0:T(8,128)} async-done(((f32[1024,512]{1,0:T(8,128)}), f32[32,512]{1,0:T(8,128)}) %reduce-scatter.18.cloned.1.call-update) | async-done | bytes 65552 | tf_op jit(solution)/shard_map/reduce_scatter | solution.py:301
  1737.5 227.5 %reduce-scatter.28.cloned.1.call-done = f32[32,2560]{1,0:T(8,128)} async-done(((f32[1024,2560]{1,0:T(8,128)}), f32[32,2560]{1,0:T(8,128)}) %reduce-scatter.28.cloned.1.call-update) | async-done | bytes 327696
  1964.9 229.6 %reduce-scatter.20.cloned.1.call-done = f32[32,2560]{1,0:T(8,128)} async-done(((f32[1024,2560]{1,0:T(8,128)}), f32[32,2560]{1,0:T(8,128)}) %reduce-scatter.20.cloned.1.call-update) | async-done | bytes 327696 | tf_op jit(solution)/shard_map/reduce_scatter | solution.py:303
  (496 shorter events, 187.0 us)
Async XLA Ops:
  7.3 30.5 %copy-start.125 = (s32[2,1,64]{2,1,0:T(1,128)S(1)}, s32[2,1,64]{2,1,0:T(1,128)}, u32[]{:S(2)}) copy-start(s32[2,1,64]{2,1,0:T(1,128)} %param.19) | copy-start | bytes 1540
  7.3 31.2 %all-gather.13.cloned.1.call-start = ((), (), s32[]{:S(2)}) async-start(), calls=%async_computation.19 | async-start | bytes 1310720 | tf_op jit(solution)/shard_map/all_gather | solution.py:102
  8.0 39.5 %all-gather.11.cloned.1.call-start = ((), (), s32[]{:S(2)}) async-start(), calls=%async_computation.18 | async-start | bytes 1310720 | tf_op jit(solution)/shard_map/all_gather | solution.py:101
  8.8 80.7 %all-gather.9.cloned.1.call-start = ((), (), s32[]{:S(2)}) async-start(), calls=%async_computation.17 | async-start | bytes 6553600 | tf_op jit(solution)/shard_map/all_gather | solution.py:103
  9.5 121.9 %all-gather.15.cloned.1.call-start = ((), (), s32[]{:S(2)}) async-start(), calls=%async_computation.20 | async-start | bytes 6553600 | tf_op jit(solution)/shard_map/all_gather | solution.py:104
  13.4 84.1 %copy-start.43 = (s32[1,64,16]{2,1,0:T(8,128)}, s32[1,64,16]{2,1,0:T(8,128)S(1)}, u32[]{:S(2)}) copy-start(s32[1,64,16]{2,1,0:T(8,128)S(1)} %copy.283) | copy-start | bytes 12292
  16.8 120.7 %copy-start.123 = (s32[1024]{0:T(1024)}, s32[1024]{0:T(1024)S(1)}, u32[]{:S(2)}) copy-start(s32[1024]{0:T(1024)S(1)} %reshape.629) | copy-start | bytes 12292
  29.0 123.5 %copy-start.32 = (bf16[1024,20]{0,1:T(8,128)(2,1)}, bf16[1024,20]{0,1:T(8,128)(2,1)S(1)}, u32[]{:S(2)}) copy-start(bf16[1024,20]{0,1:T(8,128)(2,1)S(1)} %all_gather.46) | copy-start | bytes 122884
  30.0 124.7 %copy-start.10 = (bf16[64,1024]{1,0:T(8,128)(2,1)}, bf16[64,1024]{1,0:T(8,128)(2,1)S(1)}, u32[]{:S(2)}) copy-start(bf16[64,1024]{1,0:T(8,128)(2,1)S(1)} %get-tuple-element.113) | copy-start | bytes 393220
  30.8 66.7 %copy-start.64 = (f32[64,4,5]{0,2,1:T(8,128)}, f32[64,4,5]{0,2,1:T(8,128)S(1)}, u32[]{:S(2)}) copy-start(f32[64,4,5]{0,2,1:T(8,128)S(1)} %mul.497) | copy-start | bytes 15364
  37.8 65.6 %copy-start.34 = (f32[64,4,5]{2,1,0:T(4,128)}, f32[64,4,5]{2,1,0:T(4,128)S(1)}, u32[]{:S(2)}) copy-start(f32[64,4,5]{2,1,0:T(4,128)S(1)} %copy.210) | copy-start | bytes 15364
  38.5 64.6 %copy-start.73 = (pred[64,64]{0,1:T(8,128)(4,1)}, pred[64,64]{0,1:T(8,128)(4,1)S(1)}, u32[]{:S(2)}) copy-start(pred[64,64]{0,1:T(8,128)(4,1)S(1)} %get-tuple-element.170) | copy-start | bytes 12292
  40.1 57.4 %copy-start.80 = (bf16[8,4,8,128]{3,2,1,0:T(8,128)(2,1)}, bf16[8,4,8,128]{3,2,1,0:T(8,128)(2,1)S(1)}, u32[]{:S(2)}) copy-start(bf16[8,4,8,128]{3,2,1,0:T(8,128)(2,1)S(1)} %fusion.117) | copy-start | bytes 196612
  49.0 48.5 %copy-start.78 = (bf16[8,4,8,128]{3,2,1,0:T(8,128)(2,1)}, bf16[8,4,8,128]{3,2,1,0:T(8,128)(2,1)S(1)}, u32[]{:S(2)}) copy-start(bf16[8,4,8,128]{3,2,1,0:T(8,128)(2,1)S(1)} %fusion.116) | copy-start | bytes 196612
  49.2 53.9 %copy-start.54 = (f32[4,64,64]{1,2,0:T(8,128)}, f32[4,64,64]{1,2,0:T(8,128)S(1)}, u32[]{:S(2)}) copy-start(f32[4,64,64]{1,2,0:T(8,128)S(1)} %get-tuple-element.148) | copy-start | bytes 196612
  49.2 53.9 %copy-start.104 = (f32[4,64]{1,0:T(4,128)}, f32[4,64]{1,0:T(4,128)S(1)}, u32[]{:S(2)}) copy-start(f32[4,64]{1,0:T(4,128)S(1)} %get-tuple-element.147) | copy-start | bytes 3076
  49.3 53.9 %copy-start.106 = (f32[4,64]{1,0:T(4,128)}, f32[4,64]{1,0:T(4,128)S(1)}, u32[]{:S(2)}) copy-start(f32[4,64]{1,0:T(4,128)S(1)} %fusion.182) | copy-start | bytes 3076
  103.7 33.8 %copy-start.36 = (f32[64,4,128]{2,1,0:T(4,128)}, f32[64,4,128]{2,1,0:T(4,128)S(1)}, u32[]{:S(2)}) copy-start(f32[64,4,128]{2,1,0:T(4,128)S(1)} %copy.217) | copy-start | bytes 393220
  104.4 33.1 %copy-start.22 = (bf16[64,2560]{1,0:T(8,128)(2,1)}, bf16[64,2560]{1,0:T(8,128)(2,1)S(1)}, u32[]{:S(2)}) copy-start(bf16[64,2560]{1,0:T(8,128)(2,1)S(1)} %convert_element_type.296) | copy-start | bytes 983044
  135.7 320.9 %copy-start.8 = (f32[64,1024]{1,0:T(8,128)}, f32[64,1024]{1,0:T(8,128)S(1)}, u32[]{:S(2)}) copy-start(f32[64,1024]{1,0:T(8,128)S(1)} %get-tuple-element.164) | copy-start | bytes 786436
  135.7 320.9 %copy-start.96 = (f32[64]{0:T(128)}, f32[64]{0:T(128)S(1)}, u32[]{:S(2)}) copy-start(f32[64]{0:T(128)S(1)} %broadcast_multiply_fusion.10) | copy-start | bytes 772
  146.1 99.4 %all-to-all-start = ((bf16[128,16,1024]{2,1,0:T(8,128)(2,1)}), bf16[128,16,1024]{2,1,0:T(8,128)(2,1)}, u32[]{:S(2)}, u32[]{:S(2)}) async-start(bf16[128,16,1024]{2,1,0:T(8,128)(2,1)} %bitcast.400), calls=%async_computation | async-start | bytes 8388608 | tf_op jit(solution)/shard_map/all_to_all | solution.py:173
  151.8 98.9 %all-gather.17.cloned.1.call-start = ((), (), s32[]{:S(2)}) async-start(), calls=%async_computation.21 | async-start | bytes 5242880 | tf_op jit(solution)/shard_map/all_gather | solution.py:120
  167.1 375.5 %copy-start.99 = (f32[64]{0:T(128)}, f32[64]{0:T(128)S(1)}, u32[]{:S(2)}) copy-start(f32[64]{0:T(128)S(1)} %broadcast_multiply_fusion.8) | copy-start | bytes 772
  245.5 97.3 %all-to-all-start.2 = ((bf16[128,16,1024]{2,1,0:T(8,128)(2,1)}), bf16[128,16,1024]{2,1,0:T(8,128)(2,1)}, u32[]{:S(2)}, u32[]{:S(2)}) async-start(bf16[128,16,1024]{2,1,0:T(8,128)(2,1)} %bitcast.404), calls=%async_computation.2 | async-start | bytes 8388608 | tf_op jit(solution)/shard_map/all_to_all | solution.py:173
  250.1 37.5 %all-gather.19.cloned.1.call-start = ((), (), s32[]{:S(2)}) async-start(), calls=%async_computation.22 | async-start | bytes 5242880 | tf_op jit(solution)/shard_map/all_gather | solution.py:121
  255.4 35.6 %copy-start.15 = (f32[8,16,16,128]{3,2,0,1:T(8,128)}, f32[8,16,16,128]{3,2,0,1:T(8,128)S(1)}, u32[]{:S(2)}) copy-start(f32[8,16,16,128]{3,2,0,1:T(8,128)S(1)} %fusion.50) | copy-start | bytes 3145732
  342.8 97.3 %all-to-all-start.1 = ((bf16[128,16,1024]{2,1,0:T(8,128)(2,1)}), bf16[128,16,1024]{2,1,0:T(8,128)(2,1)}, u32[]{:S(2)}, u32[]{:S(2)}) async-start(bf16[128,16,1024]{2,1,0:T(8,128)(2,1)} %bitcast.407), calls=%async_computation.1 | async-start | bytes 8388608 | tf_op jit(solution)/shard_map/all_to_all | solution.py:186
  440.1 97.3 %all-to-all-start.3 = ((bf16[128,16,1024]{2,1,0:T(8,128)(2,1)}), bf16[128,16,1024]{2,1,0:T(8,128)(2,1)}, u32[]{:S(2)}, u32[]{:S(2)}) async-start(bf16[128,16,1024]{2,1,0:T(8,128)(2,1)} %bitcast.402), calls=%async_computation.3 | async-start | bytes 8388608 | tf_op jit(solution)/shard_map/all_to_all | solution.py:186
  537.4 97.6 %all-to-all-start.4 = ((bf16[128,16,1024]{2,1,0:T(8,128)(2,1)}), bf16[128,16,1024]{2,1,0:T(8,128)(2,1)}, u32[]{:S(2)}, u32[]{:S(2)}) async-start(bf16[128,16,1024]{2,1,0:T(8,128)(2,1)} %bitcast.403), calls=%async_computation.4 | async-start | bytes 8388608 | tf_op jit(solution)/shard_map/all_to_all | solution.py:195
  635.0 97.2 %all-to-all-start.6 = ((bf16[128,16,1024]{2,1,0:T(8,128)(2,1)}), bf16[128,16,1024]{2,1,0:T(8,128)(2,1)}, u32[]{:S(2)}, u32[]{:S(2)}) async-start(bf16[128,16,1024]{2,1,0:T(8,128)(2,1)} %bitcast.405), calls=%async_computation.6 | async-start | bytes 8388608 | tf_op jit(solution)/shard_map/all_to_all | solution.py:195
  732.3 97.4 %all-to-all-start.5 = ((bf16[128,16,1024]{2,1,0:T(8,128)(2,1)}), bf16[128,16,1024]{2,1,0:T(8,128)(2,1)}, u32[]{:S(2)}, u32[]{:S(2)}) async-start(bf16[128,16,1024]{2,1,0:T(8,128)(2,1)} %bitcast.406), calls=%async_computation.5 | async-start | bytes 8388608 | tf_op jit(solution)/shard_map/all_to_all | solution.py:213
  829.7 97.2 %all-to-all-start.7 = ((bf16[128,16,1024]{2,1,0:T(8,128)(2,1)}), bf16[128,16,1024]{2,1,0:T(8,128)(2,1)}, u32[]{:S(2)}, u32[]{:S(2)}) async-start(bf16[128,16,1024]{2,1,0:T(8,128)(2,1)} %bitcast.401), calls=%async_computation.7 | async-start | bytes 8388608 | tf_op jit(solution)/shard_map/all_to_all | solution.py:213
  834.4 269.7 %reduce-scatter.30.cloned.1.call-start = ((), (), s32[]{:S(2)}) async-start(), calls=%async_computation.30 | async-start | bytes 540672
  945.3 80.0 %copy-start.12 = (f32[64,1024]{1,0:T(8,128)}, f32[64,1024]{1,0:T(8,128)S(1)}, u32[]{:S(2)}) copy-start(f32[64,1024]{1,0:T(8,128)S(1)} %get-tuple-element.110) | copy-start | bytes 786436
  945.3 82.2 %copy-start.14 = (f32[64,1024]{1,0:T(8,128)}, f32[64,1024]{1,0:T(8,128)S(1)}, u32[]{:S(2)}) copy-start(f32[64,1024]{1,0:T(8,128)S(1)} %get-tuple-element.111) | copy-start | bytes 786436
  971.3 265.0 %reduce-scatter.32.cloned.1.call-start = ((), (), s32[]{:S(2)}) async-start(), calls=%async_computation.31 | async-start | bytes 540672
  974.2 305.5 %reduce-scatter.24.cloned.1.call-start = ((), (), s32[]{:S(2)}) async-start(), calls=%async_computation.27 | async-start | bytes 5242880 | tf_op jit(solution)/shard_map/reduce_scatter | solution.py:310
  982.7 344.0 %reduce-scatter.26.cloned.1.call-start = ((), (), s32[]{:S(2)}) async-start(), calls=%async_computation.28 | async-start | bytes 5242880 | tf_op jit(solution)/shard_map/reduce_scatter | solution.py:313
  992.6 471.0 %reduce-scatter.22.cloned.1.call-start = ((), (), s32[]{:S(2)}) async-start(), calls=%async_computation.26 | async-start | bytes 540672 | tf_op jit(solution)/shard_map/reduce_scatter | solution.py:307
  994.7 605.7 %reduce-scatter.16.cloned.1.call-start = ((), (), s32[]{:S(2)}) async-start(), calls=%async_computation.23 | async-start | bytes 2162688 | tf_op jit(solution)/shard_map/reduce_scatter | solution.py:300
  1000.1 737.3 %reduce-scatter.18.cloned.1.call-start = ((), (), s32[]{:S(2)}) async-start(), calls=%async_computation.24 | async-start | bytes 2162688 | tf_op jit(solution)/shard_map/reduce_scatter | solution.py:301
  1005.2 959.8 %reduce-scatter.28.cloned.1.call-start = ((), (), s32[]{:S(2)}) async-start(), calls=%async_computation.29 | async-start | bytes 10813440
  1025.0 1169.5 %reduce-scatter.20.cloned.1.call-start = ((), (), s32[]{:S(2)}) async-start(), calls=%async_computation.25 | async-start | bytes 10813440 | tf_op jit(solution)/shard_map/reduce_scatter | solution.py:303
  1035.3 49.8 %slice-start = ((s8[5242880]{0:T(1024)(128)(4,1)}), s8[1048576]{0:T(1024)(128)(4,1)S(1)}, s32[]{:S(2)}) async-start(s8[5242880]{0:T(1024)(128)(4,1)} %bitcast.396), calls=%async_computation.32 | async-start | bytes 2097152
  1038.5 46.6 %copy-start.13 = (f32[64,1024]{1,0:T(8,128)S(1)}, f32[64,1024]{1,0:T(8,128)}, u32[]{:S(2)}) copy-start(f32[64,1024]{1,0:T(8,128)} %copy-done.12) | copy-start | bytes 786436
  1038.5 46.6 %copy-start.21 = (bf16[64,2560]{1,0:T(8,128)(2,1)S(1)}, bf16[64,2560]{1,0:T(8,128)(2,1)}, u32[]{:S(2)}) copy-start(bf16[64,2560]{1,0:T(8,128)(2,1)} %copy-done.20) | copy-start | bytes 983044
  1038.5 46.6 %copy-start.122 = (f32[64]{0:T(128)S(1)}, f32[64]{0:T(128)}, u32[]{:S(2)}) copy-start(f32[64]{0:T(128)} %copy-done.120) | copy-start | bytes 772
  (107 other events, 655.0 us)
Sparse Core Ops, SparseCore 0:
  9.7 19.5 all-gather.12
  30.8 16.6 all-gather.10
  49.0 40.4 all-gather.8
  90.9 40.4 all-gather.14
  153.9 35.0 all-gather.16
  252.2 35.3 all-gather.18
  971.4 132.6 reduce-scatter.29
  1106.4 129.8 reduce-scatter.31
  1238.9 40.7 reduce-scatter.23
  1282.3 44.4 reduce-scatter.25
  1329.6 133.8 reduce-scatter.21
  1466.3 133.9 reduce-scatter.15
  1603.2 134.2 reduce-scatter.17
  1740.3 224.5 reduce-scatter.27
  1967.8 226.7 reduce-scatter.19
where the time goes:
time: 2210 us; the launch traced here: 2200 us
  waiting for transfers between devices  1760 us (80%)
  local copies, waits for them, and re-layouts  149 us (7%)
  matrix products  130 us (6%)
  blocking collectives  65.8 us (3%)
  other arithmetic  42 us (2%)
  starting transfers between devices  40.5 us (2%)
    unnamed x18, waiting for transfers between devices  378 us
    reduce_scatter x1, waiting for transfers between devices, per_device(): lax.psum_scatter(attn_totals[4], ('dp', 'expert'), scatter_dimension=0, t...  230 us
    all_to_all x2, waiting for transfers between devices, per_device(): lax.all_to_all(grad_rows, 'expert', split_axis=0, concat_axis=0, tiled=True)  150 us
    all_to_all x2, waiting for transfers between devices, per_device(): lax.all_to_all(send_grad, 'expert', split_axis=0, concat_axis=0, tiled=True)  148 us
    reduce_scatter x1, waiting for transfers between devices, per_device(): lax.psum_scatter(attn_totals[2], ('dp', 'expert'), scatter_dimension=0, t...  137 us
    reduce_scatter x1, waiting for transfers between devices, per_device(): lax.psum_scatter(attn_totals[1], ('dp', 'expert'), scatter_dimension=0, t...  137 us
    all_to_all x2, waiting for transfers between devices, per_device(): lax.all_to_all(expert_out, 'expert', split_axis=0, concat_axis=0, tiled=T...  134 us
    reduce_scatter x1, waiting for transfers between devices, per_device(): lax.psum_scatter(attn_totals[8], ('dp', 'expert'), scatter_dimension=0, t...  134 us
  transfers between devices with their start and end apart: 23, of which 21 were waited for; matrix products, arithmetic and copies ran while one was open for 12% of the time, Pallas kernels for 0%

commit v1 on v0

v1 whole, which is shorter than its diff:
```python
import functools

import jax
import jax.numpy as jnp
from jax import lax
from jax.experimental import pallas as pl
from jax.experimental.pallas import tpu as pltpu
from jax.sharding import PartitionSpec as P

H = 4
DH = 128
EA = 5
HE = H * EA
EXPERTS = 128
EPSILON = 1e-05
MASKED = -1e30
SCALE = DH ** (-0.5)
LANES = 128

BF = jnp.bfloat16
F32 = jnp.float32

COL_SEL = 2 * H * DH
COL_ROUTER = COL_SEL + LANES
COL_A = COL_ROUTER + LANES
LANE_GAIN_ONE = 2 * HE
LANE_GAIN_TWO = 2 * HE + 1
COL_VG = 2 * H * DH
COL_LG = COL_VG + H * DH
COL_RG = COL_LG + LANES
COL_LATE = COL_RG + LANES
G_V = 2 * H * DH
G_O = G_V + HE * DH
G_S = G_O + HE * DH
G_R = G_S + LANES
G_ALL = G_R + LANES

VMEM = pl.BlockSpec(memory_space=pltpu.VMEM)
SMEM = pl.BlockSpec(memory_space=pltpu.SMEM)
ANY = pl.BlockSpec(memory_space=pl.ANY)


def dot(a, b):
    return jnp.dot(a, b, preferred_element_type=F32)


def dot_nt(a, b):
    return lax.dot_general(a, b, (((1,), (1,)), ((), ())), preferred_element_type=F32)


def dot_tn(a, b):
    return lax.dot_general(a, b, (((0,), (0,)), ((), ())), preferred_element_type=F32)


def sigmoid(v):
    return 1.0 / (1.0 + jnp.exp(-v))


class Grid:
    def __init__(self, nd, ne):
        self.nd, self.ne = nd, ne
        self.C = 2 if nd % 2 == 0 else 1
        self.Y = nd // self.C
        x = 1
        while (2 * x) * (2 * x) <= ne and ne % (2 * x) == 0:
            x *= 2
        self.X, self.Z = x, ne // x

    def _dp(self, v, go):
        C = self.C
        pairs = []
        for i in range(self.nd):
            y, c = go(i // C, i % C)
            pairs.append((i, y * C + c))
        return lax.ppermute(v, "dp", pairs)

    def _ex(self, v, go):
        X = self.X
        pairs = []
        for i in range(self.ne):
            z, x = go(i // X, i % X)
            pairs.append((i, z * X + x))
        return lax.ppermute(v, "expert", pairs)

    def rot_y(self, v, k):
        return self._dp(v, lambda y, c: ((y + k) % self.Y, c))

    def swap(self, v):
        return self._dp(v, lambda y, c: (y, c ^ 1))

    def rot_yc(self, v, k, r):
        return self._dp(v, lambda y, c: ((y + k) % self.Y, c ^ r))

    def rot_x(self, v, j):
        return self._ex(v, lambda z, x: (z, (x + j) % self.X))

    def rot_z(self, v, k):
        return self._ex(v, lambda z, x: ((z + k) % self.Z, x))


def gather_split(grid, w, rows_axis, at_x):
    n = w.shape[rows_axis] // grid.X
    part = lax.dynamic_slice_in_dim(w, at_x * n, n, axis=rows_axis) if grid.X > 1 else w
    pieces = [(w, (0, 0, None))]
    if grid.C > 1:
        pieces.append((grid.swap(w), (0, 1, None)))
    for k in range(1, grid.Y):
        got = [(grid.rot_y(part, k), 0)]
        for j in range(1, grid.X):
            got.append((grid.rot_x(got[0][0], j), j))
        for v, j in got:
            pieces.append((v, (k, 0, j)))
            if grid.C > 1:
                pieces.append((grid.swap(v), (k, 1, j)))
    return [p[0] for p in pieces], [p[1] for p in pieces]


def gather_dp(grid, w):
    pieces, tags = [w], [(0, 0)]
    got = [(w, 0)]
    for k in range(1, grid.Y):
        v = grid.rot_y(w, k)
        got.append((v, k))
        pieces.append(v)
        tags.append((k, 0))
    if grid.C > 1:
        for v, k in got:
            pieces.append(grid.swap(v))
            tags.append((k, 1))
    return pieces, tags


def shard_at(grid, idx, k, r):
    return lax.rem(idx[0] + (grid.Y - k), grid.Y) * grid.C + lax.rem(idx[1] + r, grid.C)


def fetch_rows(grid, idx, refs, tags, dst, sems, columns=None):
    copies = []
    width = dst.shape[0] // grid.nd
    part = width // grid.X
    for i, (ref, (k, r, j)) in enumerate(zip(refs, tags)):
        at = shard_at(grid, idx, k, r) * width
        n = width
        if j is not None:
            at = at + lax.rem(idx[3] + (grid.X - j), grid.X) * part
            n = part
        at = pl.multiple_of(at, n)
        src = ref if columns is None else ref.at[:, pl.ds(columns[0], columns[1])]
        copy = pltpu.make_async_copy(src, dst.at[pl.ds(at, n), :], sems.at[i])
        copy.start()
        copies.append(copy)
    return copies


def wait_all(copies):
    for copy in copies:
        copy.wait()


def lanes_of(shape):
    return lax.broadcasted_iota(jnp.int32, shape, 1)


def norm_stats(v):
    centered = v - jnp.mean(v, axis=-1, keepdims=True)
    inverse = lax.rsqrt(jnp.mean(centered * centered, axis=-1, keepdims=True) + EPSILON)
    return centered * inverse, inverse


def gain_row(block, lane):
    return jnp.transpose(block.astype(F32))[lane : lane + 1, :]


def col(v, i):
    return v[:, i : i + 1]


def head(v, i):
    return v[:, i * DH : (i + 1) * DH]


def attend_kernel(grid, tags, n_a, idx, x_ref, segc, segr, vp, op, *rest):
    n = len(tags)
    a_refs, v_refs = rest[:n], rest[n : 2 * n]
    (n1_ref, qk_ref, val_ref, va_ref, sig_ref, mask_ref, pr_ref, att_ref, wa, wv, sem_a, sem_v) = rest[
        2 * n :
    ]
    get_a = fetch_rows(grid, idx, a_refs, tags, wa, sem_a)
    get_v = fetch_rows(grid, idx, v_refs, tags, wv, sem_v)
    x_bf = x_ref[...]
    unit, _ = norm_stats(x_bf.astype(F32))
    tokens = x_bf.shape[0]
    lane = lanes_of((tokens, LANES))
    mask = jnp.zeros((tokens, LANES), F32)
    for h in range(H):
        for k in range(2):
            mask = mask + (lane == col(vp, 2 * h + k) + EA * h).astype(F32)
            mask = mask + (lane == col(op, 2 * h + k) + (EA * h + HE)).astype(F32)
    mask_ref[...] = mask
    wait_all(get_a)
    gain = gain_row(wa[:, COL_SEL:COL_ROUTER], LANE_GAIN_ONE)
    n1 = (unit * gain).astype(BF)
    n1_ref[...] = n1
    qks = dot(n1, wa[:, :COL_ROUTER])
    qk = qks[:, :COL_SEL].astype(BF)
    qk_ref[...] = qk
    sig = sigmoid(qks[:, COL_SEL:])
    sig_ref[...] = sig
    gate = sig * mask
    allowed = (segc[...] == segr[...]) & (
        lanes_of((tokens, tokens)) <= lax.broadcasted_iota(jnp.int32, (tokens, tokens), 0)
    )
    probs = []
    for h in range(H):
        scores = dot_nt(head(qk, h), head(qk, H + h))
        scaled = jnp.where(allowed, scores * SCALE, MASKED)
        top = jnp.max(scaled, axis=-1, keepdims=True)
        expo = jnp.where(allowed, jnp.exp(scaled - top), 0.0)
        prob = expo / jnp.sum(expo, axis=-1, keepdims=True)
        pr_ref[:, h * tokens : (h + 1) * tokens] = prob
        probs.append(prob.astype(BF))
    wait_all(get_v)
    for h in range(H):
        va = dot(x_bf, wv[:, h * EA * DH : (h + 1) * EA * DH])
        va_ref[:, h * EA * DH : (h + 1) * EA * DH] = va
        total = col(gate, h * EA) * head(va, 0)
        for e in range(1, EA):
            total = total + col(gate, h * EA + e) * head(va, e)
        value = total.astype(BF)
        val_ref[:, h * DH : (h + 1) * DH] = value
        att_ref[:, h * DH : (h + 1) * DH] = dot(probs[h], value)


def mixed_of(gate, att, first):
    return jnp.concatenate(
        [
            (col(gate, first + h * EA + e) * head(att, h)).astype(BF)
            for h in range(H)
            for e in range(EA)
        ],
        axis=1,
    )


def route_kernel(grid, tags, idx, x_ref, att_ref, sig_ref, mask_ref, ep, *rest):
    n = len(tags)
    a_refs, o_refs = rest[:n], rest[n : 2 * n]
    (res_ref, xg_ref, n2_ref, router_ref, picked_ref, gate_ref, wa, wo, sem_a, sem_o) = rest[2 * n :]
    get_o = fetch_rows(grid, idx, o_refs, tags, wo, sem_o)
    get_a = fetch_rows(grid, idx, a_refs, tags, wa, sem_a, (COL_SEL, 2 * LANES))
    gate = sig_ref[...] * mask_ref[...]
    gate_ref[...] = gate
    mixed = mixed_of(gate, att_ref[...], HE)
    tokens = gate.shape[0]
    lane = lanes_of((tokens, EXPERTS))
    picked = jnp.zeros((tokens, EXPERTS), F32)
    for k in range(ep.shape[1]):
        picked = picked + (lane == col(ep, k)).astype(F32)
    picked_ref[...] = picked
    wait_all(get_o)
    res = x_ref[...].astype(F32) + dot_nt(mixed, wo[...])
    res_ref[...] = res
    width = res.shape[1]
    wait_all(get_a)
    unit, _ = norm_stats(res)
    n2 = (unit * gain_row(wa[:, :LANES], LANE_GAIN_TWO)).astype(BF)
    n2_ref[...] = n2
    router = sigmoid(dot(n2, wa[:, LANES:]))
    router_ref[...] = router
    xg_ref[:, :width] = res.astype(BF)
    xg_ref[:, width:] = (router * picked).astype(BF)


def expert_kernel(grid, tags, idx, xg_ref, g_ref, *rest):
    n, X = len(tags), grid.X
    u_refs, d_refs = rest[:n], rest[n : 2 * n]
    rest = rest[2 * n :]
    hg_ref, pg_ref = rest[:2]
    from_refs, out_refs = rest[2 : 2 + X], rest[2 + X : 2 + 2 * X]
    up, down, gg, sem_u, sem_d = rest[2 + 2 * X :]
    local, width = up.shape[0], up.shape[1]
    tokens = g_ref.shape[0]
    piece = width // grid.nd
    copies = []
    for i, (k, r) in enumerate(tags):
        at = pl.multiple_of(shard_at(grid, idx, k, r) * piece, piece)
        copies.append(pltpu.make_async_copy(d_refs[i], down.at[:, :, pl.ds(at, piece)], sem_d.at[i]))
        copies.append(pltpu.make_async_copy(u_refs[i], up.at[:, pl.ds(at, piece), :], sem_u.at[i]))
    for copy in copies:
        copy.start()
    first = (idx[2] * X + idx[3]) * local
    gg[...] = jnp.zeros_like(gg)
    lane = lanes_of((tokens, EXPERTS))
    wait_all(copies)

    def pair(p, carry):
        w2 = jnp.concatenate([up[2 * p], up[2 * p + 1]], axis=1)
        d2 = down[pl.ds(2 * p, 2)].reshape(2 * LANES, width)
        pre = dot(xg_ref[:, :width], w2)
        gh = dot_nt(g_ref[...], d2)
        at = first + 2 * p
        gates = pltpu.roll(xg_ref[:, width:].astype(F32), EXPERTS - at, 1)
        gate = jnp.concatenate(
            [jnp.broadcast_to(col(gates, i), (tokens, LANES)) for i in range(2)], axis=1
        )
        sig = sigmoid(pre)
        hidden = (pre * sig).astype(BF).astype(F32)
        part = hidden * gh
        total = gg[...]
        for i in range(2):
            each = jnp.sum(head(part, i), axis=1, keepdims=True)
            total = total + jnp.where(lane == at + i, each, 0.0)
        gg[...] = total
        columns = pl.ds(pl.multiple_of(p * 2 * LANES, 2 * LANES), 2 * LANES)
        hg_ref[:, columns] = (gate * hidden).astype(BF)
        pg_ref[:, columns] = (gate * gh * sig * (1.0 + pre * (1.0 - sig))).astype(BF)
        return carry

    lax.fori_loop(0, local // 2, pair, 0)
    rows = tokens // X

    def send(q, carry):
        columns = pl.ds(pl.multiple_of(q * piece, piece), piece)
        w = jnp.concatenate([up[e, columns, :] for e in range(local)], axis=1)
        back = dot_nt(pg_ref[...], w).astype(BF)
        out = dot(hg_ref[...], down[:, :, columns].reshape(local * LANES, piece)).astype(BF)
        for j in range(X):
            from_refs[j][:, columns] = back[j * rows : (j + 1) * rows]
            out_refs[j][:, columns] = out[j * rows : (j + 1) * rows]
        return carry

    lax.fori_loop(0, grid.nd, send, 0)
    for j in range(X):
        from_refs[j][:, width:] = gg[j * rows : (j + 1) * rows, :].astype(BF)


def expert_grad_kernel(local, idx, x0, x1, g0, g1, pg0, pg1, hg0, hg1, gu_ref, gd_ref):
    del idx
    up = dot_tn(x0[...], pg0[...]) + dot_tn(x1[...], pg1[...])
    down = dot_tn(g0[...], hg0[...]) + dot_tn(g1[...], hg1[...])
    for e in range(local):
        gu_ref[0, e] = head(up, e).astype(BF)
        gd_ref[0, e] = jnp.transpose(head(down, e)).astype(BF)


def backward_kernel(grid, tags, n_from, idx, x_ref, g_ref, res_ref, router_ref, picked_ref, gate_ref, sig_ref,
                    mask_ref, att_ref, qk_ref, val_ref, va_ref, pr_ref, *rest):
    n = len(tags)
    f_refs = rest[:n_from]
    rest = rest[n_from:]
    a_refs, o_refs, v_refs = rest[:n], rest[n : 2 * n], rest[2 * n : 3 * n]
    late_ref, bg_ref, gt_ref, wa, wo, wv, sem_a, sem_o, sem_v = rest[3 * n :]
    get_a = fetch_rows(grid, idx, a_refs, tags, wa, sem_a)
    get_o = fetch_rows(grid, idx, o_refs, tags, wo, sem_o)
    get_v = fetch_rows(grid, idx, v_refs, tags, wv, sem_v)
    width = x_ref.shape[1]
    tokens = x_ref.shape[0]
    back = f_refs[0][...].astype(F32)
    for ref in f_refs[1:]:
        back = back + ref[...].astype(F32)
    router = router_ref[...]
    rg = (back[:, width:] * picked_ref[...] * router * (1.0 - router)).astype(BF)
    unit, inverse = norm_stats(res_ref[...])
    wait_all(get_a)
    n2g = dot_nt(rg, wa[:, COL_ROUTER:])
    selections = wa[:, COL_SEL:COL_ROUTER]
    gains = jnp.transpose(selections.astype(F32))
    gain_two = jnp.sum(n2g * unit, axis=0, keepdims=True)
    a = n2g * gains[LANE_GAIN_TWO : LANE_GAIN_TWO + 1]
    from_norm = inverse * (
        a
        - jnp.mean(a, axis=-1, keepdims=True)
        - unit * jnp.mean(a * unit, axis=-1, keepdims=True)
    )
    res_grad = g_ref[...].astype(F32) + back[:, :width] + from_norm
    bg = res_grad.astype(BF)
    gate, sig, att = gate_ref[...], sig_ref[...], att_ref[...]
    lane = lanes_of((tokens, LANES))
    logits = jnp.zeros((tokens, LANES), F32)
    wait_all(get_o)
    qgs, kgs, vgs, vags = [], [], [], []
    for h in range(H):
        mg = dot(bg, wo[:, h * EA * DH : (h + 1) * EA * DH])
        ag = jnp.zeros((tokens, DH), F32)
        for e in range(EA):
            i = HE + h * EA + e
            ag = ag + col(gate, i) * head(mg, e)
            each = jnp.sum(head(mg, e) * head(att, h), axis=1, keepdims=True)
            logits = jnp.where(lane == i, each, logits)
        ag = ag.astype(BF)
        prob = pr_ref[:, h * tokens : (h + 1) * tokens]
        vg = dot_tn(prob.astype(BF), ag)
        pgrad = dot_nt(ag, val_ref[:, h * DH : (h + 1) * DH])
        delta = jnp.sum(prob * pgrad, axis=-1, keepdims=True)
        sg = (prob * (pgrad - delta) * SCALE).astype(BF)
        qgs.append(dot(sg, qk_ref[:, (H + h) * DH : (H + h + 1) * DH]).astype(BF))
        kgs.append(dot_tn(sg, qk_ref[:, h * DH : (h + 1) * DH]).astype(BF))
        vgs.append(vg.astype(BF))
        for e in range(EA):
            i = h * EA + e
            va = va_ref[:, i * DH : (i + 1) * DH]
            each = jnp.sum(va * vg, axis=1, keepdims=True)
            logits = jnp.where(lane == i, each, logits)
            vags.append((col(gate, i) * vg).astype(BF))
    lg = (logits * mask_ref[...] * sig * (1.0 - sig)).astype(BF)
    qkg = jnp.concatenate(qgs + kgs, axis=1)
    late_ref[:, :COL_VG] = qkg
    late_ref[:, COL_VG:COL_LG] = jnp.concatenate(vgs, axis=1)
    late_ref[:, COL_LG:COL_RG] = lg
    late_ref[:, COL_RG:] = rg
    n1g = dot_nt(qkg, wa[:, :COL_SEL]) + dot_nt(lg, selections)
    unit, inverse = norm_stats(x_ref[...].astype(F32))
    gain_one = jnp.sum(n1g * unit, axis=0, keepdims=True)
    b = n1g * gains[LANE_GAIN_ONE : LANE_GAIN_ONE + 1]
    from_norm = inverse * (
        b
        - jnp.mean(b, axis=-1, keepdims=True)
        - unit * jnp.mean(b * unit, axis=-1, keepdims=True)
    )
    bg_ref[:tokens] = bg
    row = lax.broadcasted_iota(jnp.int32, (16, width), 0)
    high_one, high_two = gain_one.astype(BF).astype(F32), gain_two.astype(BF).astype(F32)
    extra = jnp.where(row == 0, high_one, 0.0)
    extra = jnp.where(row == 1, gain_one - high_one, extra)
    extra = jnp.where(row == 2, high_two, extra)
    extra = jnp.where(row == 3, gain_two - high_two, extra)
    bg_ref[tokens:] = extra.astype(BF)
    wait_all(get_v)
    gt_ref[...] = res_grad + dot_nt(jnp.concatenate(vags, axis=1), wv[...]) + from_norm


def weight_grad_kernel(nd, *refs):
    early, columns, late, bgs = refs[:nd], refs[nd : 2 * nd], refs[2 * nd : 3 * nd], refs[3 * nd : 4 * nd]
    out = refs[4 * nd]
    tokens = early[0].shape[0]
    width = bgs[0].shape[1]
    stack = functools.partial(jnp.concatenate, axis=0)
    xc = stack([r[:, :width] for r in columns])
    n1 = stack([r[:, width : 2 * width] for r in columns])
    n2 = stack([r[:, 2 * width :] for r in columns])
    bg = stack([r[:tokens] for r in bgs])
    acts = stack([r[...] for r in late])
    att = stack([r[:, : H * DH] for r in early])
    gate = stack([r[:, H * DH :] for r in early])
    out[:, :G_V] = dot_tn(n1, acts[:, :COL_VG]).astype(BF)
    values = acts[:, COL_VG:COL_LG].astype(F32)
    out[:, G_V:G_O] = dot_tn(xc, mixed_of(gate, values, 0)).astype(BF)
    out[:, G_O:G_S] = dot_tn(bg, mixed_of(gate, att, HE)).astype(BF)
    sums = bgs[0][tokens:].astype(F32)
    for r in bgs[1:]:
        sums = sums + r[tokens:].astype(F32)
    row = lax.broadcasted_iota(jnp.int32, (LANES, width), 0)
    extra = jnp.where(row == LANE_GAIN_ONE, sums[0:1] + sums[1:2], 0.0)
    extra = jnp.where(row == LANE_GAIN_TWO, sums[2:3] + sums[3:4], extra)
    out[:, G_S:G_R] = (dot_tn(n1, acts[:, COL_LG:COL_RG]) + jnp.transpose(extra)).astype(BF)
    out[:, G_R:] = dot_tn(n2, acts[:, COL_RG:]).astype(BF)


def params(mib):
    return pltpu.CompilerParams(vmem_limit_bytes=mib * 1024 * 1024)


def shape(dims, dtype):
    return jax.ShapeDtypeStruct(dims, dtype)


def per_device(
    nd,
    ne,
    tokens,
    cotangent,
    segments,
    value_picks,
    output_picks,
    expert_picks,
    attn_gain,
    query_weight,
    key_weight,
    value_weight,
    output_expert_weight,
    value_select,
    output_select,
    moe_gain,
    router_weight,
    up_weight,
    down_weight,
):
    grid = Grid(nd, ne)
    X, Y, Z, C = grid.X, grid.Y, grid.Z, grid.C
    micros, length, width = tokens.shape
    rows = micros * length
    local = up_weight.shape[0]
    piece = width // nd
    dp, ex = lax.axis_index("dp"), lax.axis_index("expert")
    at_y, at_c, at_z, at_x = dp // C, dp % C, ex // X, ex % X
    idx = jnp.stack([at_y, at_c, at_z, at_x]).astype(jnp.int32)

    block_a = jnp.concatenate(
        [
            query_weight,
            key_weight,
            value_select,
            output_select,
            attn_gain[:, None],
            moe_gain[:, None],
            jnp.zeros((piece, LANES - 2 * HE - 2), BF),
            router_weight,
        ],
        axis=1,
    )
    a_pieces, tags = gather_split(grid, block_a, 0, at_x)
    v_pieces, _ = gather_split(grid, value_weight, 0, at_x)
    o_pieces, _ = gather_split(grid, output_expert_weight, 0, at_x)
    u_pieces, dp_tags = gather_dp(grid, up_weight)
    d_pieces, _ = gather_dp(grid, down_weight)
    n_tags = len(tags)

    x_all = tokens.reshape(rows, width)
    g_all = cotangent.reshape(rows, width)
    seg = (segments[:, 0, :] + 8 * jnp.arange(micros, dtype=jnp.int32)[:, None]).reshape(rows)
    sem = pltpu.SemaphoreType.DMA((n_tags,))
    wide = H * DH
    n1, qk, vals, va, sig, mask, probs, att = pl.pallas_call(
        functools.partial(attend_kernel, grid, tags, n_tags),
        out_shape=(
            shape((rows, width), BF),
            shape((rows, 2 * wide), BF),
            shape((rows, wide), BF),
            shape((rows, HE * DH), F32),
            shape((rows, LANES), F32),
            shape((rows, LANES), F32),
            shape((rows, H * rows), F32),
            shape((rows, wide), F32),
        ),
        in_specs=[SMEM] + [VMEM] * 5 + [ANY] * (2 * n_tags),
        out_specs=(VMEM,) * 8,
        scratch_shapes=[
            pltpu.VMEM((width, COL_A), BF),
            pltpu.VMEM((width, HE * DH), BF),
            sem,
            sem,
        ],
        compiler_params=params(40),
        name="attend",
    )(
        idx,
        x_all,
        seg[:, None],
        seg[None, :],
        value_picks.reshape(rows, 2 * H),
        output_picks.reshape(rows, 2 * H),
        *a_pieces,
        *v_pieces,
    )
    res, xg, n2, router, picked, gate = pl.pallas_call(
        functools.partial(route_kernel, grid, tags),
        out_shape=(
            shape((rows, width), F32),
            shape((rows, width + EXPERTS), BF),
            shape((rows, width), BF),
            shape((rows, EXPERTS), F32),
            shape((rows, EXPERTS), F32),
            shape((rows, LANES), F32),
        ),
        in_specs=[SMEM] + [VMEM] * 5 + [ANY] * (2 * n_tags),
        out_specs=(VMEM,) * 6,
        scratch_shapes=[
            pltpu.VMEM((width, 2 * LANES), BF),
            pltpu.VMEM((width, HE * DH), BF),
            sem,
            sem,
        ],
        compiler_params=params(40),
        name="route",
    )(idx, x_all, att, sig, mask, expert_picks.reshape(rows, -1), *a_pieces, *o_pieces)

    def gather_rows(v):
        column = jnp.concatenate([v] + [grid.rot_z(v, k) for k in range(1, Z)], axis=0)
        return jnp.concatenate([column] + [grid.rot_x(column, j) for j in range(1, X)], axis=0)

    def return_rows(parts):
        total = parts[0].astype(F32)
        for j in range(1, X):
            total = total + grid.rot_x(parts[j], -j).astype(F32)
        total = total.astype(BF)
        return [total[:length]] + [
            grid.rot_z(total[k * length : (k + 1) * length], -k) for k in range(1, Z)
        ]

    group = ne * length
    g_group = [gather_rows(g_all[m * length : (m + 1) * length]) for m in range(micros)]
    xg_group = [gather_rows(xg[m * length : (m + 1) * length]) for m in range(micros)]
    hgs, pgs, froms, outs = [], [], [], []
    ff = local * LANES
    for m in range(micros):
        got = pl.pallas_call(
            functools.partial(expert_kernel, grid, dp_tags),
            out_shape=(
                shape((group, ff), BF),
                shape((group, ff), BF),
                *[shape((group // X, width + EXPERTS), BF)] * X,
                *[shape((group // X, width), BF)] * X,
            ),
            in_specs=[SMEM, VMEM, VMEM] + [ANY] * (2 * nd),
            out_specs=(VMEM,) * (2 + 2 * X),
            scratch_shapes=[
                pltpu.VMEM((local, width, LANES), BF),
                pltpu.VMEM((local, LANES, width), BF),
                pltpu.VMEM((group, EXPERTS), F32),
                pltpu.SemaphoreType.DMA((nd,)),
                pltpu.SemaphoreType.DMA((nd,)),
            ],
            compiler_params=params(56),
            name="experts",
        )(idx, xg_group[m], g_group[m], *u_pieces, *d_pieces)
        hgs.append(got[0])
        pgs.append(got[1])
        froms.append(return_rows(got[2 : 2 + X]))
        outs.append(return_rows(got[2 + X :]))
    output = jnp.stack(
        [
            sum((p.astype(F32) for p in outs[m]), res[m * length : (m + 1) * length])
            for m in range(micros)
        ]
    )

    def expert_grads(r):
        def shard(s, idx):
            return lax.rem(idx[0] + s, Y) * C + lax.rem(idx[1] + r, C)

        full = pl.BlockSpec((group, ff), lambda s, idx: (0, 0))
        part = pl.BlockSpec((group, piece), lambda s, idx: (0, shard(s, idx)))
        return pl.pallas_call(
            functools.partial(expert_grad_kernel, local),
            out_shape=(shape((Y, local, piece, LANES), BF), shape((Y, local, LANES, piece), BF)),
            grid_spec=pltpu.PrefetchScalarGridSpec(
                num_scalar_prefetch=1,
                grid=(Y,),
                in_specs=[part] * 4 + [full] * 4,
                out_specs=(
                    pl.BlockSpec((1, local, piece, LANES), lambda s, idx: (s, 0, 0, 0)),
                    pl.BlockSpec((1, local, LANES, piece), lambda s, idx: (s, 0, 0, 0)),
                ),
            ),
            compiler_params=params(56),
            name="expert_grads",
        )(idx, *xg_group, *g_group, *pgs, *hgs)

    far = expert_grads(1) if C > 1 else None
    near = expert_grads(0)

    def reduce_dp(own, other):
        total = own.astype(F32)
        if C > 1:
            total = total + grid.swap(other).astype(F32)
        sent = total[1:].astype(BF)
        result = total[0]
        for k in range(1, Y):
            result = result + grid.rot_y(sent[k - 1], k).astype(F32)
        return result

    grad_up = reduce_dp(near[0], far[0] if C > 1 else None)
    grad_down = reduce_dp(near[1], far[1] if C > 1 else None)

    back = [jnp.concatenate([froms[m][k] for m in range(micros)], axis=0) for k in range(Z)]
    late, bg, grad_tokens = pl.pallas_call(
        functools.partial(backward_kernel, grid, tags, Z),
        out_shape=(
            shape((rows, COL_LATE), BF),
            shape((rows + 16, width), BF),
            shape((rows, width), F32),
        ),
        in_specs=[SMEM] + [VMEM] * (13 + Z) + [ANY] * (3 * n_tags),
        out_specs=(VMEM,) * 3,
        scratch_shapes=[
            pltpu.VMEM((width, COL_A), BF),
            pltpu.VMEM((width, HE * DH), BF),
            pltpu.VMEM((width, HE * DH), BF),
            sem,
            sem,
            sem,
        ],
        compiler_params=params(48),
        name="backward",
    )(
        idx, x_all, g_all, res, router, picked, gate, sig, mask, att, qk, vals, va, probs,
        *back, *a_pieces, *o_pieces, *v_pieces,
    )

    def columns_to(parts):
        def cut(k, r):
            at = (((at_y + k) % Y) * C + (at_c + r) % C) * piece
            return jnp.concatenate(
                [lax.dynamic_slice_in_dim(v, at, piece, axis=1) for v in parts], axis=1
            )

        return [
            cut(0, 0) if (k, r) == (0, 0) else grid.rot_yc(cut(k, r), k, r) for k, r in dp_tags
        ]

    early, _ = gather_dp(grid, jnp.concatenate([att, gate], axis=1))
    cols = columns_to([x_all, n1, n2])
    lates, _ = gather_dp(grid, late)
    bgs = columns_to([bg])
    grads = pl.pallas_call(
        functools.partial(weight_grad_kernel, nd),
        out_shape=shape((piece, G_ALL), BF),
        in_specs=[VMEM] * (4 * nd),
        out_specs=VMEM,
        compiler_params=params(48),
        name="weight_grads",
    )(*early, *cols, *lates, *bgs)
    mine = piece // ne
    blocks = grads.reshape(Z, X, mine, G_ALL)

    def at_block(v, axis, i, n):
        return lax.dynamic_index_in_dim(v, i % n, axis=axis, keepdims=False)

    total = at_block(blocks, 1, at_x, X).astype(F32)
    for j in range(1, X):
        total = total + grid.rot_x(at_block(blocks, 1, at_x + j, X), j).astype(F32)
    sent = total.astype(BF)
    final = at_block(total, 0, at_z, Z)
    for k in range(1, Z):
        final = final + grid.rot_z(at_block(sent, 0, at_z + k, Z), k).astype(F32)
    return (
        output,
        grad_tokens.reshape(micros, length, width),
        final[:, G_S + LANE_GAIN_ONE],
        final[:, :wide],
        final[:, wide : 2 * wide],
        final[:, G_V:G_O],
        final[:, G_O:G_S],
        final[:, G_S : G_S + HE],
        final[:, G_S + HE : G_S + 2 * HE],
        final[:, G_S + LANE_GAIN_TWO],
        final[:, G_R:],
        grad_up,
        grad_down,
    )


def solution(mesh):
    rows = ("dp", "expert")
    placed = (
        P(None, rows, None),
        P(None, rows, None),
        P(None, rows, None),
        P(None, rows, None, None),
        P(None, rows, None, None),
        P(None, rows, None),
        P("dp"),
        P("dp", None),
        P("dp", None),
        P("dp", None),
        P("dp", None),
        P("dp", None),
        P("dp", None),
        P("dp"),
        P("dp", None),
        P("expert", "dp", None),
        P("expert", None, "dp"),
    )
    return jax.shard_map(
        functools.partial(per_device, mesh.shape["dp"], mesh.shape["expert"]),
        mesh=mesh,
        in_specs=placed,
        out_specs=(
            P(None, rows, None),
            P(None, rows, None),
            P(rows),
            P(rows, None),
            P(rows, None),
            P(rows, None),
            P(rows, None),
            P(rows, None),
            P(rows, None),
            P(rows),
            P(rows, None),
            P("expert", "dp", None),
            P("expert", None, "dp"),
        ),
        check_vma=False,
    )
```

time: 2210 us -> 416 us (0.19)
  waiting for transfers between devices: 1760 us -> 194 us
  matrix products: 130 us -> 0 us
  local copies, waits for them, and re-layouts: 149 us -> 36.2 us
  Pallas kernels: 0 us -> 87.5 us
  blocking collectives: 65.8 us -> 0 us
  starting transfers between devices: 40.5 us -> 80.6 us
  other arithmetic: 42 us -> 15.3 us
    reduce_scatter x6 -> x0, waiting for transfers between devices: 724 us -> none  [the longest x1 230 us: per_device(): lax.psum_scatter(attn_totals[4], ('dp', 'expert'), scatter_dimension=0, t...]
    all_to_all x8 -> x0, waiting for transfers between devices: 549 us -> none  [the longest x2 150 us: per_device(): lax.all_to_all(grad_rows, 'expert', split_axis=0, concat_axis=0, tiled=True)]
    unnamed x18 -> x0, waiting for transfers between devices: 378 us -> none
    ppermute x0 -> x73, waiting for transfers between devices: none -> 194 us  [the longest x39 162 us: _ex(): return lax.ppermute(v, 'expert', pairs)]
    dot_general x66 -> x0, matrix products: 130 us -> none  [the longest x14 26.8 us: matmul(): return jnp.dot(matrix_a, matrix_b, preferred_element_type=jnp.float32)]
    all_gather x6 -> x0, waiting for transfers between devices: 107 us -> none  [the longest x1 40.2 us: per_device(): lax.all_gather(value_weight, 'dp', axis=0, tiled=True)]
    pallas_call x0 -> x8, Pallas kernels: none -> 87.5 us  [the longest x2 39.1 us: per_device(): pl.pallas_call(functools.partial(expert_kernel, grid, dp_tags), out_shape...]
    ppermute x0 -> x73, starting transfers between devices: none -> 80.6 us  [the longest x39 63.2 us: _ex(): return lax.ppermute(v, 'expert', pairs)]
  transfers between devices with their start and end apart: 23 -> 73, of which waited for: 21 -> 26; matrix products, arithmetic and copies ran while one was open for 12% -> 10% of each run, Pallas kernels for 0% -> 21%
where the time goes in v1:
time: 416 us; the launch traced here: 415 us
  waiting for transfers between devices  194 us (47%)
  Pallas kernels  87.5 us (21%)
  starting transfers between devices  80.6 us (19%)
  local copies, waits for them, and re-layouts  36.2 us (9%)
  other arithmetic  15.3 us (4%)
    ppermute x39, waiting for transfers between devices, _ex(): return lax.ppermute(v, 'expert', pairs)  162 us
    ppermute x39, starting transfers between devices, _ex(): return lax.ppermute(v, 'expert', pairs)  63.2 us
    pallas_call x2, Pallas kernels, per_device(): pl.pallas_call(functools.partial(expert_kernel, grid, dp_tags), out_shape...  39.1 us
    ppermute x34, waiting for transfers between devices, _dp(): return lax.ppermute(v, 'dp', pairs)  32.4 us
    pallas_call x2, Pallas kernels, expert_grads(): pl.pallas_call(functools.partial(expert_grad_kernel, local), out_shape=(s...  21.2 us
    ppermute x34, starting transfers between devices, _dp(): return lax.ppermute(v, 'dp', pairs)  17.4 us
    unnamed x134, local copies, waits for them, and re-layouts  14.7 us
    pallas_call x1, Pallas kernels, per_device(): pl.pallas_call(functools.partial(backward_kernel, grid, tags, Z), out_sha...  12.1 us
  transfers between devices with their start and end apart: 73, of which 26 were waited for; matrix products, arithmetic and copies ran while one was open for 10% of the time, Pallas kernels for 21%

profile of v1, /device:TPU:0, one launch (start us, length us, event | category | flops | bytes accessed | tf_op | source)
XLA Modules:
  0.0 415.3 jit_solution(17698965973803507335)
XLA Ops:
  0.6 1.7 slice_bitcast_fusion.3
  2.3 3.0 collective-permute-start.19
  5.4 2.6 collective-permute-start.20
  18.7 3.2 collective-permute-start.39
  21.8 2.2 collective-permute-done.1.rest_2_.rest_6_
  26.6 3.0 collective-permute-done.38
  30.1 2.0 pad_maximum_fusion.2
  35.0 18.7 %collective-permute-done.3.rest_4_.rest_8_ = bf16[128,1280]{1,0:T(8,128)(2,1)S(1)} collective-permute-done((bf16[128,1280]{1,0:T(8,128)(2,1)S(1)}, bf16[128,1280]{1,0:T(8,128)(2,1)S(1)}, u32[]{:S(2)}, u32[]{:S(2)}) %collective-permute-start.3) | collective-permute-done | bytes 327712 | tf_op jit(solution)/shard_map/ppermute | solution.py:83
  73.1 10.4 %collective-permute-done.8.rest_10_.rest_20_ = bf16[128,2560]{1,0:T(8,128)(2,1)} collective-permute-done((bf16[128,2560]{1,0:T(8,128)(2,1)}, bf16[128,2560]{1,0:T(8,128)(2,1)}, u32[]{:S(2)}, u32[]{:S(2)}) %collective-permute-start.8) | collective-permute-done | bytes 655392 | tf_op jit(solution)/shard_map/ppermute | solution.py:83
  83.5 12.8 %collective-permute-done.13.rest_10_.rest_14_ = bf16[128,2560]{1,0:T(8,128)(2,1)} collective-permute-done((bf16[128,2560]{1,0:T(8,128)(2,1)}, bf16[128,2560]{1,0:T(8,128)(2,1)}, u32[]{:S(2)}, u32[]{:S(2)}) %collective-permute-start.13) | collective-permute-done | bytes 655392 | tf_op jit(solution)/shard_map/ppermute | solution.py:83
  102.7 5.0 %attend.1 = (bf16[128,1024]{1,0:T(8,128)(2,1)S(1)}, bf16[128,1024]{1,0:T(8,128)(2,1)S(1)}, bf16[128,512]{1,0:T(8,128)(2,1)S(1)}, f32[128,2560]{1,0:T(8,128)S(1)}...) custom-call(s32[4]{0:T(128)S(1)} %pad_add_fusion.idx, ...), custom_call_target="tpu_custom_call" | custom-call | tf_op jit(solution)/shard_map/attend/pallas_call | solution.py:523
  108.8 4.8 %route.1 = (f32[128,1024]{1,0:T(8,128)S(1)}, bf16[128,1152]{1,0:T(8,128)(2,1)S(1)}, bf16[128,1024]{1,0:T(8,128)(2,1)S(1)}, f32[128,128]{1,0:T(8,128)S(1)}, f32[1...) custom-call(s32[4]{0:T(128)S(1)} %pad_add_fusion.idx, bf16[128,1024]{1,0:T(8,128)(2,1)S(1)} %bitcast.58, ...), custom_call_target="tpu_custom_call" | custom-call | tf_op jit(solution)/shard_map/route/pallas_call | solution.py:555
  113.8 2.1 collective-permute-start.33
  115.8 2.0 collective-permute-start.34
  118.7 3.7 collective-permute-done.33
  122.4 5.6 %collective-permute-done.34 = bf16[64,1152]{1,0:T(8,128)(2,1)S(1)} collective-permute-done((bf16[64,1152]{1,0:T(8,128)(2,1)S(1)}, bf16[64,1152]{1,0:T(8,128)(2,1)S(1)}, u32[]{:S(2)}, u32[]{:S(2)}) %collective-permute-start.34) | collective-permute-done | bytes 147488 | tf_op jit(solution)/shard_map/ppermute | solution.py:83
  129.2 3.4 collective-permute-start.16
  132.7 15.6 %collective-permute-done.26.rest_5_ = bf16[16,128,256]{2,1,0:T(8,128)(2,1)S(1)} collective-permute-done((bf16[16,128,256]{2,1,0:T(8,128)(2,1)S(1)}, bf16[16,128,256]{2,1,0:T(8,128)(2,1)S(1)}, u32[]{:S(2)}, u32[]{:S(2)}) %collective-permute-start.26) | collective-permute-done | bytes 1048608 | tf_op jit(solution)/shard_map/ppermute | solution.py:75
  148.8 3.7 collective-permute-start.17
  152.6 3.5 collective-permute-done.17
  158.5 12.3 %collective-permute-done.36 = bf16[256,1152]{1,0:T(8,128)(2,1)S(1)} collective-permute-done((bf16[256,1152]{1,0:T(8,128)(2,1)S(1)}, bf16[256,1152]{1,0:T(8,128)(2,1)S(1)}, u32[]{:S(2)}, u32[]{:S(2)}) %collective-permute-start.36) | collective-permute-done | bytes 589856 | tf_op jit(solution)/shard_map/ppermute | solution.py:83
  175.4 19.6 %experts.3 = (bf16[512,2048]{1,0:T(8,128)(2,1)}, bf16[512,2048]{1,0:T(8,128)(2,1)}, bf16[256,1152]{1,0:T(8,128)(2,1)}, bf16[256,1152]{1,0:T(8,128)(2,1)}, bf16[2...) custom-call(s32[4]{0:T(128)} %copy-done.19, bf16[512,1152]{1,0:T(8,128)(2,1)} %copy-done.23, bf16[512,1024]{1,0:T(8,128)(2,1)} %copy-done.24, ...), custom_call_target="tpu_custom_call" | custom-call | tf_op jit(solution)/shard_map/experts/pallas_call | solution.py:596
  197.8 19.6 %experts.2 = (bf16[512,2048]{1,0:T(8,128)(2,1)}, bf16[512,2048]{1,0:T(8,128)(2,1)}, bf16[256,1152]{1,0:T(8,128)(2,1)}, bf16[256,1152]{1,0:T(8,128)(2,1)}, bf16[2...) custom-call(s32[4]{0:T(128)} %copy-done.19, bf16[512,1152]{1,0:T(8,128)(2,1)} %copy-done.22, bf16[512,1024]{1,0:T(8,128)(2,1)} %copy-done.25, ...), custom_call_target="tpu_custom_call" | custom-call | tf_op jit(solution)/shard_map/experts/pallas_call | solution.py:596
  219.7 23.7 %collective-permute-done.45 = bf16[256,1152]{1,0:T(8,128)(2,1)S(1)} collective-permute-done((bf16[256,1152]{1,0:T(8,128)(2,1)}, bf16[256,1152]{1,0:T(8,128)(2,1)S(1)}, u32[]{:S(2)}, u32[]{:S(2)}) %collective-permute-start.45) | collective-permute-done | bytes 589856 | tf_op jit(solution)/shard_map/ppermute | solution.py:83
  243.6 4.3 %collective-permute-start.48 = (bf16[64,1152]{1,0:T(8,128)(2,1)S(1)}, bf16[64,1152]{1,0:T(8,128)(2,1)S(1)}, u32[]{:S(2)}, u32[]{:S(2)}) collective-permute-start(bf16[64,1152]{1,0:T(8,128)(2,1)S(1)} %get-tuple-element.137), channel_id=1, source_target_pairs={{0,6},{1,7},{2,0},{3,1},{4,2},{5,3},{6,4},{7,5},{8,14},{9,15},{10,... | collective-permute-start | bytes 442376 | tf_op jit(solution)/shard_map/ppermute | solution.py:83
  248.1 4.2 %collective-permute-done.48 = bf16[64,1152]{1,0:T(8,128)(2,1)S(1)} collective-permute-done((bf16[64,1152]{1,0:T(8,128)(2,1)S(1)}, bf16[64,1152]{1,0:T(8,128)(2,1)S(1)}, u32[]{:S(2)}, u32[]{:S(2)}) %collective-permute-start.48) | collective-permute-done | bytes 147488 | tf_op jit(solution)/shard_map/ppermute | solution.py:83
  252.4 3.0 collective-permute-done.47
  255.5 5.8 %collective-permute-done.50 = bf16[64,1152]{1,0:T(8,128)(2,1)S(1)} collective-permute-done((bf16[64,1152]{1,0:T(8,128)(2,1)S(1)}, bf16[64,1152]{1,0:T(8,128)(2,1)S(1)}, u32[]{:S(2)}, u32[]{:S(2)}) %collective-permute-start.50) | collective-permute-done | bytes 147488 | tf_op jit(solution)/shard_map/ppermute | solution.py:83
  261.3 2.5 collective-permute-start.52
  264.4 2.5 collective-permute-start.51
  266.9 3.6 collective-permute-done.52
  270.5 3.2 collective-permute-done.51
  275.2 12.1 %backward.1 = (bf16[128,1792]{1,0:T(8,128)(2,1)S(1)}, bf16[144,1024]{1,0:T(8,128)(2,1)S(1)}, f32[128,1024]{1,0:T(8,128)}) custom-call(s32[4]{0:T(128)S(1)} %copy-done.20, bf16[128,1024]{1,0:T(8,128)(2,1)S(1)} %bitcast.59, bf16[128,1024]{1,0:T(8,128)(2,1)S(1)} %bitcast.60, f32[128,1024]{1,0:T(8,128)S(1)} %get-tuple-element.49.res_ref, ...), custom_call_target="tpu_custom_call" | custom-call | tf_op jit(solution)/shard_map/backward/pallas_call | solution.py:666
  289.4 10.5 %expert_grads.3 = (bf16[2,16,256,128]{3,2,1,0:T(8,128)(2,1)}, bf16[2,16,128,256]{3,2,1,0:T(8,128)(2,1)}) custom-call(s32[4]{0:T(128)} %copy-done.19, bf16[512,1152]{1,0:T(8,128)(2,1)} %copy-done.22, bf16[512,1152]{1,0:T(8,128)(2,1)} %copy-done.23, bf16[512,1024]{1,0:T(8,128)(2,1)} %copy-done.25, bf16[512,1024]{1,0:T(8,128)(2,1)} %copy-done.24, ...), custom_call_target="tpu_custom_call" | custom-call | tf_op jit(solution)/shard_map/expert_grads/pallas_call | solution.py:633
  299.9 10.6 %expert_grads.2 = (bf16[2,16,256,128]{3,2,1,0:T(8,128)(2,1)}, bf16[2,16,128,256]{3,2,1,0:T(8,128)(2,1)}) custom-call(s32[4]{0:T(128)} %copy-done.19, bf16[512,1152]{1,0:T(8,128)(2,1)} %copy-done.22, bf16[512,1152]{1,0:T(8,128)(2,1)} %copy-done.23, bf16[512,1024]{1,0:T(8,128)(2,1)} %copy-done.25, bf16[512,1024]{1,0:T(8,128)(2,1)} %copy-done.24, ...), custom_call_target="tpu_custom_call" | custom-call | tf_op jit(solution)/shard_map/expert_grads/pallas_call | solution.py:633
  318.7 2.9 collective-permute-done.64.refs_15_
  321.6 2.8 collective-permute-start.31
  326.0 5.3 %weight_grads.1 = bf16[256,6400]{1,0:T(8,128)(2,1)} custom-call(f32[128,640]{1,0:T(8,128)S(1)} %constant_dynamic-update-slice_fusion.20.refs_0_, f32[128,640]{1,0:T(8,128)S(1)} %collective-permute-done.53.refs_1_, f32[128,640]{1,0:T(8,128)S(1)} %collective-permute-done.54.refs_2_, f32[128,640]{1,0:T(8,128)S(1)} %collective-permute-done.55.refs_3_, ...), custom_call_target="tpu_custom_call" | custom-call | tf_op jit(solution)/shard_map/weight_grads/pallas_call | solution.py:705
  332.4 1.9 collective-permute-done.31
  334.4 5.1 %collective-permute-start.42 = (bf16[64,1024]{1,0:T(8,128)(2,1)S(1)}, bf16[64,1024]{1,0:T(8,128)(2,1)S(1)}, u32[]{:S(2)}, u32[]{:S(2)}) collective-permute-start(bf16[64,1024]{1,0:T(8,128)(2,1)S(1)} %get-tuple-element.144), channel_id=1, source_target_pairs={{0,6},{1,7},{2,0},{3,1},{4,2},{5,3},{6,4},{7,5},{8,14},{9,15},{10,... | collective-permute-start | bytes 393224 | tf_op jit(solution)/shard_map/ppermute | solution.py:83
  341.7 3.8 collective-permute-done.43
  347.9 1.8 collective-permute-start.70
  351.9 25.2 %collective-permute-done.65 = bf16[4,32,6400]{2,1,0:T(8,128)(2,1)S(1)} collective-permute-done((bf16[4,32,6400]{2,1,0:T(8,128)(2,1)S(1)}, bf16[4,32,6400]{2,1,0:T(8,128)(2,1)S(1)}, u32[]{:S(2)}, u32[]{:S(2)}) %collective-permute-start.65) | collective-permute-done | bytes 1638432 | tf_op jit(solution)/shard_map/ppermute | solution.py:83
  377.9 2.0 collective-permute-start.67
  379.9 1.9 collective-permute-start.66
  383.4 9.7 %collective-permute-done.72 = bf16[16,128,256]{2,1,0:T(8,128)(2,1)S(1)} collective-permute-done((bf16[16,128,256]{2,1,0:T(8,128)(2,1)S(1)}, bf16[16,128,256]{2,1,0:T(8,128)(2,1)S(1)}, u32[]{:S(2)}, u32[]{:S(2)}) %collective-permute-start.72) | collective-permute-done | bytes 1048608 | tf_op jit(solution)/shard_map/ppermute | solution.py:75
  393.1 1.6 fusion
  394.7 16.2 %collective-permute-done.67 = bf16[32,6400]{1,0:T(8,128)(2,1)S(1)} collective-permute-done((bf16[32,6400]{1,0:T(8,128)(2,1)S(1)}, bf16[32,6400]{1,0:T(8,128)(2,1)S(1)}, u32[]{:S(2)}, u32[]{:S(2)}) %collective-permute-start.67) | collective-permute-done | bytes 409632 | tf_op jit(solution)/shard_map/ppermute | solution.py:83
  (310 shorter events, 87.0 us)
Async XLA Ops:
  2.3 14.1 %collective-permute-start.19 = (bf16[64,1024]{1,0:T(8,128)(2,1)}, bf16[64,1024]{1,0:T(8,128)(2,1)S(1)}, u32[]{:S(2)}, u32[]{:S(2)}) collective-permute-start(bf16[64,1024]{1,0:T(8,128)(2,1)} %get-tuple-element.167), channel_id=1, source_target_pairs={{0,2},{1,3},{2,4},{3,5},{4,6},{5,7},{6,0},{7,1},{8,10},{9,11},{10,... | collective-permute-start | bytes 393224 | tf_op jit(solution)/shard_map/ppermute | solution.py:83
  5.4 11.8 %collective-permute-start.20 = (bf16[64,1024]{1,0:T(8,128)(2,1)}, bf16[64,1024]{1,0:T(8,128)(2,1)}, u32[]{:S(2)}, u32[]{:S(2)}) collective-permute-start(bf16[64,1024]{1,0:T(8,128)(2,1)} %get-tuple-element.167), channel_id=1, source_target_pairs={{0,4},{1,5},{2,6},{3,7},{4,0},{5,1},{6,2},{7,3},{8,12},{9,13},{10,... | collective-permute-start | bytes 393224 | tf_op jit(solution)/shard_map/ppermute | solution.py:83
  13.8 18.3 %collective-permute-start = (bf16[256,1280]{1,0:T(8,128)(2,1)S(1)}, bf16[256,1280]{1,0:T(8,128)(2,1)}, u32[]{:S(2)}, u32[]{:S(2)}) collective-permute-start(bf16[256,1280]{1,0:T(8,128)(2,1)S(1)} %concatenate.58.rest_0_.rest_4_), channel_id=1, source_target_pairs={{0,8},{8,0},{16,24},{24,16},{1,9},{9,1},{17,25},{25,17},{2,10},{10... | collective-permute-start | bytes 1966088 | tf_op jit(solution)/shard_map/ppermute | solution.py:75
  17.2 12.5 %collective-permute-start.38 = (bf16[64,1024]{1,0:T(8,128)(2,1)S(1)}, bf16[64,1024]{1,0:T(8,128)(2,1)S(1)}, u32[]{:S(2)}, u32[]{:S(2)}) collective-permute-start(bf16[64,1024]{1,0:T(8,128)(2,1)S(1)} %copy-done.47), channel_id=1, source_target_pairs={{0,4},{1,5},{2,6},{3,7},{4,0},{5,1},{6,2},{7,3},{8,12},{9,13},{10,... | collective-permute-start | bytes 393224 | tf_op jit(solution)/shard_map/ppermute | solution.py:83
  18.7 11.4 %collective-permute-start.39 = (bf16[64,1024]{1,0:T(8,128)(2,1)S(1)}, bf16[64,1024]{1,0:T(8,128)(2,1)S(1)}, u32[]{:S(2)}, u32[]{:S(2)}) collective-permute-start(bf16[64,1024]{1,0:T(8,128)(2,1)S(1)} %copy-done.47), channel_id=1, source_target_pairs={{0,6},{1,7},{2,0},{3,1},{4,2},{5,3},{6,4},{7,5},{8,14},{9,15},{10,... | collective-permute-start | bytes 393224 | tf_op jit(solution)/shard_map/ppermute | solution.py:83
  25.1 31.5 %collective-permute-start.6 = (bf16[128,2560]{1,0:T(8,128)(2,1)}, bf16[128,2560]{1,0:T(8,128)(2,1)}, u32[]{:S(2)}, u32[]{:S(2)}) collective-permute-start(bf16[128,2560]{1,0:T(8,128)(2,1)} %constant_dynamic-slice_fusion.17), channel_id=1, source_target_pairs={{0,16},{8,24},{16,0},{24,8},{1,17},{9,25},{17,1},{25,9},{2,18},{10... | collective-permute-start | bytes 1966088 | tf_op jit(solution)/shard_map/ppermute | solution.py:75
  29.6 27.0 %collective-permute-start.11 = (bf16[128,2560]{1,0:T(8,128)(2,1)}, bf16[128,2560]{1,0:T(8,128)(2,1)}, u32[]{:S(2)}, u32[]{:S(2)}) collective-permute-start(bf16[128,2560]{1,0:T(8,128)(2,1)} %constant_dynamic-slice_fusion.16), channel_id=1, source_target_pairs={{0,16},{8,24},{16,0},{24,8},{1,17},{9,25},{17,1},{25,9},{2,18},{10... | collective-permute-start | bytes 1966088 | tf_op jit(solution)/shard_map/ppermute | solution.py:75
  30.1 42.9 %collective-permute-start.5 = (bf16[256,2560]{1,0:T(8,128)(2,1)S(1)}, bf16[256,2560]{1,0:T(8,128)(2,1)}, u32[]{:S(2)}, u32[]{:S(2)}) collective-permute-start(bf16[256,2560]{1,0:T(8,128)(2,1)S(1)} %copy-done), channel_id=1, source_target_pairs={{0,8},{8,0},{16,24},{24,16},{1,9},{9,1},{17,25},{25,17},{2,10},{10... | collective-permute-start | bytes 3932168 | tf_op jit(solution)/shard_map/ppermute | solution.py:75
  32.1 26.0 %collective-permute-start.22 = (bf16[256,1024]{1,0:T(8,128)(2,1)}, bf16[256,1024]{1,0:T(8,128)(2,1)}, u32[]{:S(2)}, u32[]{:S(2)}) collective-permute-start(bf16[256,1024]{1,0:T(8,128)(2,1)} %pad_maximum_fusion.2), channel_id=1, source_target_pairs={{0,1},{1,0},{2,3},{3,2},{4,5},{5,4},{6,7},{7,6},{8,9},{9,8},{10,11... | collective-permute-start | bytes 1572872 | tf_op jit(solution)/shard_map/ppermute | solution.py:83
  33.6 20.0 %collective-permute-start.3 = (bf16[128,1280]{1,0:T(8,128)(2,1)S(1)}, bf16[128,1280]{1,0:T(8,128)(2,1)S(1)}, u32[]{:S(2)}, u32[]{:S(2)}) collective-permute-start(bf16[128,1280]{1,0:T(8,128)(2,1)S(1)} %collective-permute-done.1.rest_2_.rest_6_), channel_id=1, source_target_pairs={{0,1},{1,0},{2,3},{3,2},{4,5},{5,4},{6,7},{7,6},{8,9},{9,8},{10,11... | collective-permute-start | bytes 983048 | tf_op jit(solution)/shard_map/ppermute | solution.py:83
  54.4 16.0 %collective-permute-start.40 = (bf16[256,1024]{1,0:T(8,128)(2,1)}, bf16[256,1024]{1,0:T(8,128)(2,1)}, u32[]{:S(2)}, u32[]{:S(2)}) collective-permute-start(bf16[256,1024]{1,0:T(8,128)(2,1)} %pad_maximum_fusion.3), channel_id=1, source_target_pairs={{0,1},{1,0},{2,3},{3,2},{4,5},{5,4},{6,7},{7,6},{8,9},{9,8},{10,11... | collective-permute-start | bytes 1572872 | tf_op jit(solution)/shard_map/ppermute | solution.py:83
  56.6 52.2 %collective-permute-start.10 = (bf16[256,2560]{1,0:T(8,128)(2,1)S(1)}, bf16[256,2560]{1,0:T(8,128)(2,1)}, u32[]{:S(2)}, u32[]{:S(2)}) collective-permute-start(bf16[256,2560]{1,0:T(8,128)(2,1)S(1)} %copy-done.1), channel_id=1, source_target_pairs={{0,8},{8,0},{16,24},{24,16},{1,9},{9,1},{17,25},{25,17},{2,10},{10... | collective-permute-start | bytes 3932168 | tf_op jit(solution)/shard_map/ppermute | solution.py:75
  56.6 27.0 %collective-permute-start.8 = (bf16[128,2560]{1,0:T(8,128)(2,1)}, bf16[128,2560]{1,0:T(8,128)(2,1)}, u32[]{:S(2)}, u32[]{:S(2)}) collective-permute-start(bf16[128,2560]{1,0:T(8,128)(2,1)} %collective-permute-done.6.rest_8_.rest_18_), channel_id=1, source_target_pairs={{0,1},{1,0},{2,3},{3,2},{4,5},{5,4},{6,7},{7,6},{8,9},{9,8},{10,11... | collective-permute-start | bytes 1966088 | tf_op jit(solution)/shard_map/ppermute | solution.py:83
  58.1 38.3 %collective-permute-start.13 = (bf16[128,2560]{1,0:T(8,128)(2,1)}, bf16[128,2560]{1,0:T(8,128)(2,1)}, u32[]{:S(2)}, u32[]{:S(2)}) collective-permute-start(bf16[128,2560]{1,0:T(8,128)(2,1)} %collective-permute-done.11.rest_8_.rest_12_), channel_id=1, source_target_pairs={{0,1},{1,0},{2,3},{3,2},{4,5},{5,4},{6,7},{7,6},{8,9},{9,8},{10,11... | collective-permute-start | bytes 1966088 | tf_op jit(solution)/shard_map/ppermute | solution.py:83
  72.5 27.7 %collective-permute-start.7 = (bf16[128,2560]{1,0:T(8,128)(2,1)}, bf16[128,2560]{1,0:T(8,128)(2,1)S(1)}, u32[]{:S(2)}, u32[]{:S(2)}) collective-permute-start(bf16[128,2560]{1,0:T(8,128)(2,1)} %collective-permute-done.6.rest_8_.rest_18_), channel_id=1, source_target_pairs={{0,8},{8,0},{16,24},{24,16},{1,9},{9,1},{17,25},{25,17},{2,10},{10... | collective-permute-start | bytes 1966088 | tf_op jit(solution)/shard_map/ppermute | solution.py:75
  73.0 35.7 %collective-permute-start.12 = (bf16[128,2560]{1,0:T(8,128)(2,1)}, bf16[128,2560]{1,0:T(8,128)(2,1)S(1)}, u32[]{:S(2)}, u32[]{:S(2)}) collective-permute-start(bf16[128,2560]{1,0:T(8,128)(2,1)} %collective-permute-done.11.rest_8_.rest_12_), channel_id=1, source_target_pairs={{0,8},{8,0},{16,24},{24,16},{1,9},{9,1},{17,25},{25,17},{2,10},{10... | collective-permute-start | bytes 1966088 | tf_op jit(solution)/shard_map/ppermute | solution.py:75
  83.5 18.2 %collective-permute-start.9 = (bf16[128,2560]{1,0:T(8,128)(2,1)}, bf16[128,2560]{1,0:T(8,128)(2,1)S(1)}, u32[]{:S(2)}, u32[]{:S(2)}) collective-permute-start(bf16[128,2560]{1,0:T(8,128)(2,1)} %collective-permute-done.8.rest_10_.rest_20_), channel_id=1, source_target_pairs={{0,8},{8,0},{16,24},{24,16},{1,9},{9,1},{17,25},{25,17},{2,10},{10... | collective-permute-start | bytes 1966088 | tf_op jit(solution)/shard_map/ppermute | solution.py:75
  96.4 12.4 %collective-permute-start.14 = (bf16[128,2560]{1,0:T(8,128)(2,1)}, bf16[128,2560]{1,0:T(8,128)(2,1)S(1)}, u32[]{:S(2)}, u32[]{:S(2)}) collective-permute-start(bf16[128,2560]{1,0:T(8,128)(2,1)} %collective-permute-done.13.rest_10_.rest_14_), channel_id=1, source_target_pairs={{0,8},{8,0},{16,24},{24,16},{1,9},{9,1},{17,25},{25,17},{2,10},{10... | collective-permute-start | bytes 1966088 | tf_op jit(solution)/shard_map/ppermute | solution.py:75
  100.2 32.4 %collective-permute-start.23 = (bf16[16,256,128]{2,1,0:T(8,128)(2,1)S(1)}, bf16[16,256,128]{2,1,0:T(8,128)(2,1)S(1)}, u32[]{:S(2)}, u32[]{:S(2)}) collective-permute-start(bf16[16,256,128]{2,1,0:T(8,128)(2,1)S(1)} %copy-done.26), channel_id=1, source_target_pairs={{0,16},{8,24},{16,0},{24,8},{1,17},{9,25},{17,1},{25,9},{2,18},{10... | collective-permute-start | bytes 3145736 | tf_op jit(solution)/shard_map/ppermute | solution.py:75
  101.8 46.5 %collective-permute-start.26 = (bf16[16,128,256]{2,1,0:T(8,128)(2,1)S(1)}, bf16[16,128,256]{2,1,0:T(8,128)(2,1)S(1)}, u32[]{:S(2)}, u32[]{:S(2)}) collective-permute-start(bf16[16,128,256]{2,1,0:T(8,128)(2,1)S(1)} %copy-done.27), channel_id=1, source_target_pairs={{0,16},{8,24},{16,0},{24,8},{1,17},{9,25},{17,1},{25,9},{2,18},{10... | collective-permute-start | bytes 3145736 | tf_op jit(solution)/shard_map/ppermute | solution.py:75
  115.8 12.2 %collective-permute-start.34 = (bf16[64,1152]{1,0:T(8,128)(2,1)S(1)}, bf16[64,1152]{1,0:T(8,128)(2,1)S(1)}, u32[]{:S(2)}, u32[]{:S(2)}) collective-permute-start(bf16[64,1152]{1,0:T(8,128)(2,1)S(1)} %get-tuple-element.154), channel_id=1, source_target_pairs={{0,4},{1,5},{2,6},{3,7},{4,0},{5,1},{6,2},{7,3},{8,12},{9,13},{10,... | collective-permute-start | bytes 442376 | tf_op jit(solution)/shard_map/ppermute | solution.py:83
  122.4 49.9 %collective-permute-start.24 = (bf16[16,256,128]{2,1,0:T(8,128)(2,1)S(1)}, bf16[16,256,128]{2,1,0:T(8,128)(2,1)S(1)}, u32[]{:S(2)}, u32[]{:S(2)}) collective-permute-start(bf16[16,256,128]{2,1,0:T(8,128)(2,1)S(1)} %copy-done.26), channel_id=1, source_target_pairs={{0,8},{8,0},{16,24},{24,16},{1,9},{9,1},{17,25},{25,17},{2,10},{10... | collective-permute-start | bytes 3145736 | tf_op jit(solution)/shard_map/ppermute | solution.py:75
  128.0 20.3 %collective-permute-start.15 = (bf16[64,1152]{1,0:T(8,128)(2,1)S(1)}, bf16[64,1152]{1,0:T(8,128)(2,1)S(1)}, u32[]{:S(2)}, u32[]{:S(2)}) collective-permute-start(bf16[64,1152]{1,0:T(8,128)(2,1)S(1)} %get-tuple-element.151), channel_id=1, source_target_pairs={{0,2},{1,3},{2,4},{3,5},{4,6},{5,7},{6,0},{7,1},{8,10},{9,11},{10,... | collective-permute-start | bytes 442376 | tf_op jit(solution)/shard_map/ppermute | solution.py:83
  129.2 19.7 %collective-permute-start.16 = (bf16[64,1152]{1,0:T(8,128)(2,1)S(1)}, bf16[64,1152]{1,0:T(8,128)(2,1)S(1)}, u32[]{:S(2)}, u32[]{:S(2)}) collective-permute-start(bf16[64,1152]{1,0:T(8,128)(2,1)S(1)} %get-tuple-element.151), channel_id=1, source_target_pairs={{0,4},{1,5},{2,6},{3,7},{4,0},{5,1},{6,2},{7,3},{8,12},{9,13},{10,... | collective-permute-start | bytes 442376 | tf_op jit(solution)/shard_map/ppermute | solution.py:83
  132.6 40.8 %collective-permute-start.27 = (bf16[16,128,256]{2,1,0:T(8,128)(2,1)S(1)}, bf16[16,128,256]{2,1,0:T(8,128)(2,1)S(1)}, u32[]{:S(2)}, u32[]{:S(2)}) collective-permute-start(bf16[16,128,256]{2,1,0:T(8,128)(2,1)S(1)} %copy-done.27), channel_id=1, source_target_pairs={{0,8},{8,0},{16,24},{24,16},{1,9},{9,1},{17,25},{25,17},{2,10},{10... | collective-permute-start | bytes 3145736 | tf_op jit(solution)/shard_map/ppermute | solution.py:75
  148.3 25.2 %collective-permute-start.25 = (bf16[16,256,128]{2,1,0:T(8,128)(2,1)S(1)}, bf16[16,256,128]{2,1,0:T(8,128)(2,1)S(1)}, u32[]{:S(2)}, u32[]{:S(2)}) collective-permute-start(bf16[16,256,128]{2,1,0:T(8,128)(2,1)S(1)} %collective-permute-done.23.rest_1_), channel_id=1, source_target_pairs={{0,8},{8,0},{16,24},{24,16},{1,9},{9,1},{17,25},{25,17},{2,10},{10... | collective-permute-start | bytes 3145736 | tf_op jit(solution)/shard_map/ppermute | solution.py:75
  148.3 27.1 %collective-permute-start.28 = (bf16[16,128,256]{2,1,0:T(8,128)(2,1)S(1)}, bf16[16,128,256]{2,1,0:T(8,128)(2,1)}, u32[]{:S(2)}, u32[]{:S(2)}) collective-permute-start(bf16[16,128,256]{2,1,0:T(8,128)(2,1)S(1)} %collective-permute-done.26.rest_5_), channel_id=1, source_target_pairs={{0,8},{8,0},{16,24},{24,16},{1,9},{9,1},{17,25},{25,17},{2,10},{10... | collective-permute-start | bytes 3145736 | tf_op jit(solution)/shard_map/ppermute | solution.py:75
  156.1 14.7 %collective-permute-start.36 = (bf16[256,1152]{1,0:T(8,128)(2,1)S(1)}, bf16[256,1152]{1,0:T(8,128)(2,1)S(1)}, u32[]{:S(2)}, u32[]{:S(2)}) collective-permute-start(bf16[256,1152]{1,0:T(8,128)(2,1)S(1)} %pad_maximum_fusion.1), channel_id=1, source_target_pairs={{0,1},{1,0},{2,3},{3,2},{4,5},{5,4},{6,7},{7,6},{8,9},{9,8},{10,11... | collective-permute-start | bytes 1769480 | tf_op jit(solution)/shard_map/ppermute | solution.py:83
  170.7 24.9 %collective-permute-start.18 = (bf16[256,1152]{1,0:T(8,128)(2,1)}, bf16[256,1152]{1,0:T(8,128)(2,1)}, u32[]{:S(2)}, u32[]{:S(2)}) collective-permute-start(bf16[256,1152]{1,0:T(8,128)(2,1)} %pad_maximum_fusion), channel_id=1, source_target_pairs={{0,1},{1,0},{2,3},{3,2},{4,5},{5,4},{6,7},{7,6},{8,9},{9,8},{10,11... | collective-permute-start | bytes 1769480 | tf_op jit(solution)/shard_map/ppermute | solution.py:83
  172.3 114.9 %collective-permute-start.56 = (bf16[128,768]{1,0:T(8,128)(2,1)S(1)}, bf16[128,768]{1,0:T(8,128)(2,1)S(1)}, u32[]{:S(2)}, u32[]{:S(2)}) collective-permute-start(bf16[128,768]{1,0:T(8,128)(2,1)S(1)} %pad_maximum_fusion.10), channel_id=1, source_target_pairs={{0,16},{8,24},{16,0},{24,8},{1,17},{9,25},{17,1},{25,9},{2,18},{10... | collective-permute-start | bytes 589832 | tf_op jit(solution)/shard_map/ppermute | solution.py:75
  173.5 114.9 %collective-permute-start.57 = (bf16[128,768]{1,0:T(8,128)(2,1)S(1)}, bf16[128,768]{1,0:T(8,128)(2,1)S(1)}, u32[]{:S(2)}, u32[]{:S(2)}) collective-permute-start(bf16[128,768]{1,0:T(8,128)(2,1)S(1)} %pad_maximum_fusion.11), channel_id=1, source_target_pairs={{0,8},{8,0},{16,24},{24,16},{1,9},{9,1},{17,25},{25,17},{2,10},{10... | collective-permute-start | bytes 589832 | tf_op jit(solution)/shard_map/ppermute | solution.py:75
  195.0 24.5 %collective-permute-start.46 = (bf16[256,1152]{1,0:T(8,128)(2,1)}, bf16[256,1152]{1,0:T(8,128)(2,1)S(1)}, u32[]{:S(2)}, u32[]{:S(2)}) collective-permute-start(bf16[256,1152]{1,0:T(8,128)(2,1)} %get-tuple-element.65), channel_id=1, source_target_pairs={{0,1},{1,0},{2,3},{3,2},{4,5},{5,4},{6,7},{7,6},{8,9},{9,8},{10,11... | collective-permute-start | bytes 1769480 | tf_op jit(solution)/shard_map/ppermute | solution.py:83
  217.4 93.3 %collective-permute-start.29 = (bf16[256,1024]{1,0:T(8,128)(2,1)}, bf16[256,1024]{1,0:T(8,128)(2,1)}, u32[]{:S(2)}, u32[]{:S(2)}) collective-permute-start(bf16[256,1024]{1,0:T(8,128)(2,1)} %get-tuple-element.52), channel_id=1, source_target_pairs={{0,1},{1,0},{2,3},{3,2},{4,5},{5,4},{6,7},{7,6},{8,9},{9,8},{10,11... | collective-permute-start | bytes 1572872 | tf_op jit(solution)/shard_map/ppermute | solution.py:83
  219.0 24.4 %collective-permute-start.45 = (bf16[256,1152]{1,0:T(8,128)(2,1)}, bf16[256,1152]{1,0:T(8,128)(2,1)S(1)}, u32[]{:S(2)}, u32[]{:S(2)}) collective-permute-start(bf16[256,1152]{1,0:T(8,128)(2,1)} %get-tuple-element.63), channel_id=1, source_target_pairs={{0,1},{1,0},{2,3},{3,2},{4,5},{5,4},{6,7},{7,6},{8,9},{9,8},{10,11... | collective-permute-start | bytes 1769480 | tf_op jit(solution)/shard_map/ppermute | solution.py:83
  270.5 40.1 %collective-permute-start.58 = (bf16[128,768]{1,0:T(8,128)(2,1)S(1)}, bf16[128,768]{1,0:T(8,128)(2,1)S(1)}, u32[]{:S(2)}, u32[]{:S(2)}) collective-permute-start(bf16[128,768]{1,0:T(8,128)(2,1)S(1)} %pad_maximum_fusion.12), channel_id=1, source_target_pairs={{0,24},{8,16},{16,8},{24,0},{1,25},{9,17},{17,9},{25,1},{2,26},{10... | collective-permute-start | bytes 589832 | tf_op jit(solution)/shard_map/ppermute | solution.py:75
  273.7 39.5 %collective-permute-start.41 = (bf16[256,1024]{1,0:T(8,128)(2,1)S(1)}, bf16[256,1024]{1,0:T(8,128)(2,1)}, u32[]{:S(2)}, u32[]{:S(2)}) collective-permute-start(bf16[256,1024]{1,0:T(8,128)(2,1)S(1)} %copy-done.55), channel_id=1, source_target_pairs={{0,1},{1,0},{2,3},{3,2},{4,5},{5,4},{6,7},{7,6},{8,9},{9,8},{10,11... | collective-permute-start | bytes 1572872 | tf_op jit(solution)/shard_map/ppermute | solution.py:83
  287.3 25.1 %collective-permute-start.53 = (f32[128,640]{1,0:T(8,128)S(1)}, f32[128,640]{1,0:T(8,128)S(1)}, u32[]{:S(2)}, u32[]{:S(2)}) collective-permute-start(f32[128,640]{1,0:T(8,128)S(1)} %constant_dynamic-update-slice_fusion.20.refs_0_), channel_id=1, source_target_pairs={{0,16},{8,24},{16,0},{24,8},{1,17},{9,25},{17,1},{25,9},{2,18},{10... | collective-permute-start | bytes 983048 | tf_op jit(solution)/shard_map/ppermute | solution.py:75
  288.3 25.8 %collective-permute-start.59 = (bf16[128,1792]{1,0:T(8,128)(2,1)S(1)}, bf16[128,1792]{1,0:T(8,128)(2,1)S(1)}, u32[]{:S(2)}, u32[]{:S(2)}) collective-permute-start(bf16[128,1792]{1,0:T(8,128)(2,1)S(1)} %get-tuple-element.69.refs_8_), channel_id=1, source_target_pairs={{0,16},{8,24},{16,0},{24,8},{1,17},{9,25},{17,1},{25,9},{2,18},{10... | collective-permute-start | bytes 1376264 | tf_op jit(solution)/shard_map/ppermute | solution.py:75
  310.7 36.3 %collective-permute-start.69 = (bf16[2,16,256,128]{3,2,1,0:T(8,128)(2,1)}, bf16[2,16,256,128]{3,2,1,0:T(8,128)(2,1)S(1)}, u32[]{:S(2)}, u32[]{:S(2)}) collective-permute-start(bf16[2,16,256,128]{3,2,1,0:T(8,128)(2,1)} %get-tuple-element.76), channel_id=1, source_target_pairs={{0,8},{8,0},{16,24},{24,16},{1,9},{9,1},{17,25},{25,17},{2,10},{10... | collective-permute-start | bytes 6291464 | tf_op jit(solution)/shard_map/ppermute | solution.py:75
  317.5 32.1 %collective-permute-start.71 = (bf16[2,16,128,256]{3,2,1,0:T(8,128)(2,1)S(1)}, bf16[2,16,128,256]{3,2,1,0:T(8,128)(2,1)S(1)}, u32[]{:S(2)}, u32[]{:S(2)}) collective-permute-start(bf16[2,16,128,256]{3,2,1,0:T(8,128)(2,1)S(1)} %copy-done.54), channel_id=1, source_target_pairs={{0,8},{8,0},{16,24},{24,16},{1,9},{9,1},{17,25},{25,17},{2,10},{10... | collective-permute-start | bytes 6291464 | tf_op jit(solution)/shard_map/ppermute | solution.py:75
  321.6 12.7 %collective-permute-start.31 = (bf16[64,1024]{1,0:T(8,128)(2,1)S(1)}, bf16[64,1024]{1,0:T(8,128)(2,1)S(1)}, u32[]{:S(2)}, u32[]{:S(2)}) collective-permute-start(bf16[64,1024]{1,0:T(8,128)(2,1)S(1)} %get-tuple-element.143), channel_id=1, source_target_pairs={{0,4},{1,5},{2,6},{3,7},{4,0},{5,1},{6,2},{7,3},{8,12},{9,13},{10,... | collective-permute-start | bytes 393224 | tf_op jit(solution)/shard_map/ppermute | solution.py:83
  334.4 11.5 %collective-permute-start.42 = (bf16[64,1024]{1,0:T(8,128)(2,1)S(1)}, bf16[64,1024]{1,0:T(8,128)(2,1)S(1)}, u32[]{:S(2)}, u32[]{:S(2)}) collective-permute-start(bf16[64,1024]{1,0:T(8,128)(2,1)S(1)} %get-tuple-element.144), channel_id=1, source_target_pairs={{0,6},{1,7},{2,0},{3,1},{4,2},{5,3},{6,4},{7,5},{8,14},{9,15},{10,... | collective-permute-start | bytes 393224 | tf_op jit(solution)/shard_map/ppermute | solution.py:83
  341.1 35.9 %collective-permute-start.65 = (bf16[4,32,6400]{2,1,0:T(8,128)(2,1)S(1)}, bf16[4,32,6400]{2,1,0:T(8,128)(2,1)S(1)}, u32[]{:S(2)}, u32[]{:S(2)}) collective-permute-start(bf16[4,32,6400]{2,1,0:T(8,128)(2,1)S(1)} %dynamic-slice_bitcast_fusion), channel_id=1, source_target_pairs={{0,1},{1,0},{2,3},{3,2},{4,5},{5,4},{6,7},{7,6},{8,9},{9,8},{10,11... | collective-permute-start | bytes 4915208 | tf_op jit(solution)/shard_map/ppermute | solution.py:83
  347.9 34.0 %collective-permute-start.70 = (bf16[16,256,128]{2,1,0:T(8,128)(2,1)S(1)}, bf16[16,256,128]{2,1,0:T(8,128)(2,1)S(1)}, u32[]{:S(2)}, u32[]{:S(2)}) collective-permute-start(bf16[16,256,128]{2,1,0:T(8,128)(2,1)S(1)} %fusion.2), channel_id=1, source_target_pairs={{0,16},{8,24},{16,0},{24,8},{1,17},{9,25},{17,1},{25,9},{2,18},{10... | collective-permute-start | bytes 3145736 | tf_op jit(solution)/shard_map/ppermute | solution.py:75
  350.5 42.6 %collective-permute-start.72 = (bf16[16,128,256]{2,1,0:T(8,128)(2,1)S(1)}, bf16[16,128,256]{2,1,0:T(8,128)(2,1)S(1)}, u32[]{:S(2)}, u32[]{:S(2)}) collective-permute-start(bf16[16,128,256]{2,1,0:T(8,128)(2,1)S(1)} %fusion.3), channel_id=1, source_target_pairs={{0,16},{8,24},{16,0},{24,8},{1,17},{9,25},{17,1},{25,9},{2,18},{10... | collective-permute-start | bytes 3145736 | tf_op jit(solution)/shard_map/ppermute | solution.py:75
  377.5 17.2 %collective-permute-start.68 = (bf16[32,6400]{1,0:T(8,128)(2,1)S(1)}, bf16[32,6400]{1,0:T(8,128)(2,1)S(1)}, u32[]{:S(2)}, u32[]{:S(2)}) collective-permute-start(bf16[32,6400]{1,0:T(8,128)(2,1)S(1)} %get-tuple-element.123), channel_id=1, source_target_pairs={{0,6},{1,7},{2,0},{3,1},{4,2},{5,3},{6,4},{7,5},{8,14},{9,15},{10,... | collective-permute-start | bytes 1228808 | tf_op jit(solution)/shard_map/ppermute | solution.py:83
  377.9 33.0 %collective-permute-start.67 = (bf16[32,6400]{1,0:T(8,128)(2,1)S(1)}, bf16[32,6400]{1,0:T(8,128)(2,1)S(1)}, u32[]{:S(2)}, u32[]{:S(2)}) collective-permute-start(bf16[32,6400]{1,0:T(8,128)(2,1)S(1)} %get-tuple-element.124), channel_id=1, source_target_pairs={{0,4},{1,5},{2,6},{3,7},{4,0},{5,1},{6,2},{7,3},{8,12},{9,13},{10,... | collective-permute-start | bytes 1228808 | tf_op jit(solution)/shard_map/ppermute | solution.py:83
  379.9 30.9 %collective-permute-start.66 = (bf16[32,6400]{1,0:T(8,128)(2,1)S(1)}, bf16[32,6400]{1,0:T(8,128)(2,1)S(1)}, u32[]{:S(2)}, u32[]{:S(2)}) collective-permute-start(bf16[32,6400]{1,0:T(8,128)(2,1)S(1)} %get-tuple-element.122), channel_id=1, source_target_pairs={{0,2},{1,3},{2,4},{3,5},{4,6},{5,7},{6,0},{7,1},{8,10},{9,11},{10,... | collective-permute-start | bytes 1228808 | tf_op jit(solution)/shard_map/ppermute | solution.py:83
  (81 other events, 968.9 us)

commit v2 on v1

v2 whole, which is shorter than its diff:
```python
import functools

import jax
import jax.numpy as jnp
from jax import lax
from jax.experimental import pallas as pl
from jax.experimental.pallas import tpu as pltpu
from jax.sharding import PartitionSpec as P

H = 4
DH = 128
EA = 5
HE = H * EA
EXPERTS = 128
EPSILON = 1e-05
MASKED = -1e30
SCALE = DH ** (-0.5)
LANES = 128

BF = jnp.bfloat16
F32 = jnp.float32

COL_SEL = 2 * H * DH
COL_ROUTER = COL_SEL + LANES
COL_VALUES = COL_ROUTER + LANES
COL_OUT = COL_VALUES + HE * DH
COL_A = COL_OUT + HE * DH
STARTS = (0, 17 * LANES, 34 * LANES)
LANE_GAIN_ONE = 2 * HE
LANE_GAIN_TWO = 2 * HE + 1
LANE_MEAN = 2 * HE
LANE_INVERSE = 2 * HE + 1
COL_LG = 2 * H * DH
COL_VG = COL_LG + LANES
COL_RG = COL_VG + H * DH
COL_LATE = COL_RG + LANES

VMEM = pl.BlockSpec()
SMEM = pl.BlockSpec(memory_space=pltpu.SMEM)
ANY = pl.BlockSpec(memory_space=pltpu.HBM)


def dot(a, b):
    return jnp.dot(a, b, preferred_element_type=F32)


def dot_nt(a, b):
    return lax.dot_general(a, b, (((1,), (1,)), ((), ())), preferred_element_type=F32)


def dot_tn(a, b):
    return lax.dot_general(a, b, (((0,), (0,)), ((), ())), preferred_element_type=F32)


def sigmoid(v):
    return 1.0 / (1.0 + jnp.exp(-v))


class Grid:
    def __init__(self, nd, ne):
        self.nd, self.ne = nd, ne
        self.C = 2 if nd % 2 == 0 else 1
        self.Y = nd // self.C
        x = 1
        while (2 * x) * (2 * x) <= ne and ne % (2 * x) == 0:
            x *= 2
        self.X, self.Z = x, ne // x

    def _dp(self, v, go):
        C = self.C
        pairs = []
        for i in range(self.nd):
            y, c = go(i // C, i % C)
            pairs.append((i, y * C + c))
        return lax.ppermute(v, "dp", pairs)

    def _ex(self, v, go):
        X = self.X
        pairs = []
        for i in range(self.ne):
            z, x = go(i // X, i % X)
            pairs.append((i, z * X + x))
        return lax.ppermute(v, "expert", pairs)

    def rot_y(self, v, k):
        return self._dp(v, lambda y, c: ((y + k) % self.Y, c))

    def swap(self, v):
        return self._dp(v, lambda y, c: (y, c ^ 1))

    def rot_yc(self, v, k, r):
        return self._dp(v, lambda y, c: ((y + k) % self.Y, c ^ r))

    def rot_x(self, v, j):
        return self._ex(v, lambda z, x: (z, (x + j) % self.X))

    def rot_z(self, v, k):
        return self._ex(v, lambda z, x: ((z + k) % self.Z, x))

    def lines_z(self):
        return [[z * self.X + x for z in range(self.Z)] for x in range(self.X)]

    def gather_z(self, v):
        return lax.all_gather(v, "expert", axis=0, tiled=True, axis_index_groups=self.lines_z())

    def swap_z(self, v):
        return lax.all_to_all(v, "expert", 0, 0, tiled=True, axis_index_groups=self.lines_z())

    def send_z(self, parts):
        return [parts[0]] + [self.rot_z(parts[k], k) for k in range(1, self.Z)]

    def swap_dp(self, v):
        return lax.all_to_all(v, "dp", 0, 0, tiled=True)


def after(v, *deps):
    flat = [d for dep in deps for d in (dep if isinstance(dep, (list, tuple)) else [dep])]
    if not flat:
        return v
    return lax.optimization_barrier((v, *flat))[0]


def gather_dp(grid, w, over_y, swapped=None):
    got = [w] + list(over_y)
    if grid.C > 1:
        got = got + [grid.swap(w) if swapped is None else swapped] + [grid.swap(v) for v in over_y]
    return got


def dp_tags(grid):
    return [(k, r) for r in range(grid.C) for k in range(grid.Y)]


def shard_at(grid, idx, k, r):
    return lax.rem(idx[0] + (grid.Y - k), grid.Y) * grid.C + lax.rem(idx[1] + r, grid.C)


def fetch_rows(grid, idx, refs, tags, dst, sems, first=0):
    copies = []
    width, last = dst.shape[0] // grid.nd, first + dst.shape[1]
    for i, (ref, (k, r, split, j, column)) in enumerate(zip(refs, tags)):
        low, high = max(first, column), min(last, column + ref.shape[1])
        if low >= high:
            continue
        at = shard_at(grid, idx, k, r) * width
        n = width
        if split is not None:
            size, mine = (grid.X, idx[3]) if split == "x" else (grid.Z, idx[2])
            n = width // size
            at = at + lax.rem(mine + (size - j), size) * n
        at = pl.multiple_of(at, n)
        copy = pltpu.make_async_copy(
            ref.at[:, pl.ds(low - column, high - low)],
            dst.at[pl.ds(at, n), pl.ds(low - first, high - low)],
            sems.at[i],
        )
        copy.start()
        copies.append(copy)
    return copies


def fetch_experts(grid, idx, refs, tags, dst, axis, sems):
    copies = []
    n = dst.shape[axis] // grid.nd
    for i, (ref, (k, r, first)) in enumerate(zip(refs, tags)):
        at = pl.ds(pl.multiple_of(shard_at(grid, idx, k, r) * n, n), n)
        held = pl.ds(first, ref.shape[0])
        place = dst.at[held, at, :] if axis == 1 else dst.at[held, :, at]
        copy = pltpu.make_async_copy(ref, place, sems.at[i])
        copy.start()
        copies.append(copy)
    return copies


def wait_all(copies):
    for copy in copies:
        copy.wait()


def lanes_of(dims):
    return lax.broadcasted_iota(jnp.int32, dims, 1)


def rows_of(dims):
    return lax.broadcasted_iota(jnp.int32, dims, 0)


def norm_stats(v):
    centered = v - jnp.mean(v, axis=-1, keepdims=True)
    inverse = lax.rsqrt(jnp.mean(centered * centered, axis=-1, keepdims=True) + EPSILON)
    return centered * inverse, inverse


def window(pieces, tags, low, high):
    held = [(p, t) for p, t in zip(pieces, tags) if t[4] < high and t[4] + p.shape[1] > low]
    return [p for p, _ in held], [t for _, t in held]


def norm_back(grad, unit, inverse):
    return inverse * (
        grad
        - jnp.mean(grad, axis=-1, keepdims=True)
        - unit * jnp.mean(grad * unit, axis=-1, keepdims=True)
    )


def gain_row(block, lane):
    return jnp.transpose(block.astype(F32))[lane : lane + 1, :]


def col(v, i):
    return v[:, i : i + 1]


def head(v, i):
    return v[:, i * DH : (i + 1) * DH]


def mixed_of(gate, vectors, first):
    return jnp.concatenate(
        [
            (col(gate, first + h * EA + e) * head(vectors, h)).astype(BF)
            for h in range(H)
            for e in range(EA)
        ],
        axis=1,
    )


def pack_kernel(grid, idx, q, k, vs, os, gain_one, gain_two, router, v_ref, o_ref, w_ref, a_ref, *rest):
    parts, misc = rest[:-1], rest[-1]
    piece = q.shape[0]
    nx = piece // grid.X
    at_x = pl.ds(pl.multiple_of(idx[3] * nx, nx), nx)
    misc[...] = jnp.zeros_like(misc)
    misc[:HE, :] = vs[...].astype(F32)
    misc[HE : 2 * HE, :] = os[...].astype(F32)
    misc[LANE_GAIN_ONE : LANE_GAIN_ONE + 1, :] = gain_one[...].astype(F32).reshape(1, piece)
    misc[LANE_GAIN_TWO : LANE_GAIN_TWO + 1, :] = gain_two[...].astype(F32).reshape(1, piece)
    wide = H * DH
    a_ref[:, :wide] = q[...]
    a_ref[:, wide:COL_SEL] = k[...]
    a_ref[:, COL_SEL:COL_ROUTER] = jnp.transpose(misc[...]).astype(BF)
    a_ref[:, COL_ROUTER:] = router[...]
    w_ref[:, :COL_VALUES] = a_ref[...]
    w_ref[:, COL_VALUES:COL_OUT] = v_ref[...]
    w_ref[:, COL_OUT:] = o_ref[...]
    for part, low in zip(parts, STARTS):
        part[...] = w_ref[at_x, low : low + part.shape[1]]


def attend_kernel(grid, tags, length, idx, x_ref, seg_ref, vp, op, *rest):
    n = len(tags)
    a_refs = rest[:n]
    n1_ref, qk_ref, sig_ref, mask_ref, pr_ref, wmr_ref, wa, sem_a = rest[n:]
    get_a = fetch_rows(grid, idx, a_refs, tags, wa, sem_a)
    unit, _ = norm_stats(x_ref[...].astype(F32))
    tokens = unit.shape[0]
    lane = lanes_of((tokens, LANES))
    mask = jnp.zeros((tokens, LANES), F32)
    for h in range(H):
        for k in range(2):
            mask = mask + (lane == col(vp, 2 * h + k) + EA * h).astype(F32)
            mask = mask + (lane == col(op, 2 * h + k) + (EA * h + HE)).astype(F32)
    mask_ref[...] = mask
    square = (tokens, tokens)
    row, lane = rows_of(square), lanes_of(square)
    seg = jnp.broadcast_to(seg_ref[...].astype(F32), square)
    allowed = (seg == jnp.transpose(seg)) & (lane <= row) & (lane // length == row // length)
    wait_all(get_a)
    n1 = (unit * gain_row(wa[:, COL_SEL:COL_ROUTER], LANE_GAIN_ONE)).astype(BF)
    n1_ref[...] = n1
    qks = dot(n1, wa[:, :COL_ROUTER])
    qk = qks[:, :COL_SEL].astype(BF)
    qk_ref[...] = qk
    sig_ref[...] = sigmoid(qks[:, COL_SEL:])
    wmr_ref[...] = wa[:, COL_SEL:]
    for h in range(H):
        scores = dot_nt(head(qk, h), head(qk, H + h))
        scaled = jnp.where(allowed, scores * SCALE, MASKED)
        top = jnp.max(scaled, axis=-1, keepdims=True)
        expo = jnp.where(allowed, jnp.exp(scaled - top), 0.0)
        pr_ref[:, h * tokens : (h + 1) * tokens] = expo / jnp.sum(expo, axis=-1, keepdims=True)


def route_kernel(grid, v_tags, o_tags, idx, x_ref, n1_ref, sig_ref, mask_ref, pr_ref, wmr_ref, ep, *rest):
    nv, no = len(v_tags), len(o_tags)
    v_refs, o_refs = rest[:nv], rest[nv : nv + no]
    rest = rest[nv + no :]
    val_ref, va_ref, early_ref, res_ref, router_ref, picked_ref = rest[:6]
    xg_ref, col_ref, wv, wo, sem_v, sem_o = rest[6:]
    get_v = fetch_rows(grid, idx, v_refs, v_tags, wv, sem_v, COL_VALUES)
    get_o = fetch_rows(grid, idx, o_refs, o_tags, wo, sem_o, COL_OUT)
    gate = sig_ref[...] * mask_ref[...]
    tokens, width = x_ref.shape
    lane = lanes_of((tokens, EXPERTS))
    picked = jnp.zeros((tokens, EXPERTS), F32)
    for k in range(ep.shape[1]):
        picked = picked + (lane == col(ep, k)).astype(F32)
    picked_ref[...] = picked
    x_bf = x_ref[...]
    wait_all(get_v)
    atts = []
    for h in range(H):
        va = dot(x_bf, wv[:, h * EA * DH : (h + 1) * EA * DH])
        va_ref[:, h * EA * DH : (h + 1) * EA * DH] = va
        total = col(gate, h * EA) * head(va, 0)
        for e in range(1, EA):
            total = total + col(gate, h * EA + e) * head(va, e)
        value = total.astype(BF)
        val_ref[:, h * DH : (h + 1) * DH] = value
        atts.append(dot(pr_ref[:, h * tokens : (h + 1) * tokens].astype(BF), value))
    att = jnp.concatenate(atts, axis=1)
    early_ref[:, : H * DH] = att
    mean = jnp.mean(x_bf.astype(F32), axis=-1, keepdims=True)
    centered = x_bf.astype(F32) - mean
    inverse = lax.rsqrt(jnp.mean(centered * centered, axis=-1, keepdims=True) + EPSILON)
    lane = lanes_of((tokens, LANES))
    early_ref[:, H * DH :] = jnp.where(
        lane == LANE_MEAN, mean, jnp.where(lane == LANE_INVERSE, inverse, gate)
    )
    mixed = mixed_of(gate, att, HE)
    wait_all(get_o)
    res = x_bf.astype(F32) + dot_nt(mixed, wo[...])
    res_ref[...] = res
    unit, _ = norm_stats(res)
    n2 = (unit * gain_row(wmr_ref[:, :LANES], LANE_GAIN_TWO)).astype(BF)
    router = sigmoid(dot(n2, wmr_ref[:, LANES:]))
    router_ref[...] = router
    xg_ref[:, :width] = res.astype(BF)
    xg_ref[:, width:] = (router * picked).astype(BF)
    col_ref[:, :width] = x_bf
    col_ref[:, width : 2 * width] = n1_ref[...]
    col_ref[:, 2 * width :] = n2


def ahead_kernel(grid, tags, idx, g_ref, *rest):
    d_refs, (gh_ref, g, down, gh, sem_g, sem_d, sem_o) = rest[: len(tags)], rest[len(tags) :]
    local, width = down.shape[0], down.shape[2]
    micros = g.shape[1]
    get_g = pltpu.make_async_copy(g_ref, g, sem_g.at[0])
    get_g.start()
    get_d = fetch_experts(grid, idx, d_refs, tags, down, 2, sem_d)
    get_g.wait()
    wait_all(get_d)
    group = g.shape[0] * g.shape[2]
    copies = []
    for p in range(local // 2):
        d2 = down[2 * p : 2 * p + 2].reshape(2 * LANES, width)
        columns = pl.ds(p * 2 * LANES, 2 * LANES)
        for m in range(micros):
            gh[m * group : (m + 1) * group, columns] = dot_nt(g[:, m].reshape(group, width), d2).astype(BF)
        copies.append(pltpu.make_async_copy(gh.at[:, columns], gh_ref.at[:, columns], sem_o.at[p]))
        copies[-1].start()
    wait_all(copies)


def place_of(grid, idx, j, k):
    return lax.rem(idx[2] + (grid.Z - k), grid.Z) * grid.X + lax.rem(idx[3] + (grid.X - j), grid.X)


def expert_kernel(grid, tags, micro, micros, idx, gh_ref, *rest):
    n, X, Z, nd, nt = grid.ne, grid.X, grid.Z, grid.nd, len(tags)
    x_refs, u_refs = rest[:n], rest[n : n + nt]
    rest = rest[n + nt + (3 if micro else 0) :]
    hg_ref, pg_ref, xg_ref = rest[:3]
    from_refs = rest[3 : 3 + X]
    hg, pg, xg, gh, up, gg, back, sem_x, sem_u, sem_g, sem_o = rest[3 + X :]
    local, width = up.shape[0], up.shape[1]
    tokens = xg.shape[0]
    rows = tokens // n
    mine = pl.ds(micro * tokens, tokens)
    get_x = []
    for j in range(X):
        for k in range(Z):
            at = pl.multiple_of(place_of(grid, idx, j, k) * rows, rows)
            i = j * Z + k
            get_x.append(
                pltpu.make_async_copy(
                    x_refs[i].at[pl.ds(micro * rows, rows), :], xg.at[pl.ds(at, rows), :], sem_x.at[i]
                )
            )
            get_x[-1].start()
    get_u = fetch_experts(grid, idx, u_refs, tags, up, 1, sem_u)
    get_g = pltpu.make_async_copy(gh_ref.at[mine, :], gh, sem_g.at[0])
    get_g.start()
    first = (idx[2] * X + idx[3]) * local
    gg[...] = jnp.zeros_like(gg)
    lane = lanes_of((tokens, EXPERTS))
    wait_all(get_x)
    copies = [pltpu.make_async_copy(xg, xg_ref.at[mine, :], sem_o.at[0])]
    copies[0].start()
    wait_all(get_u)
    get_g.wait()

    def pair(p, carry):
        w2 = jnp.concatenate([up[2 * p], up[2 * p + 1]], axis=1)
        pre = dot(xg[:, :width], w2)
        columns = pl.ds(pl.multiple_of(p * 2 * LANES, 2 * LANES), 2 * LANES)
        grad = gh[:, columns].astype(F32)
        at = first + 2 * p
        gates = pltpu.roll(xg[:, width:].astype(F32), EXPERTS - at, 1)
        gate = jnp.concatenate(
            [jnp.broadcast_to(col(gates, i), (tokens, LANES)) for i in range(2)], axis=1
        )
        sig = sigmoid(pre)
        hidden = (pre * sig).astype(BF).astype(F32)
        part = hidden * grad
        total = gg[...]
        for i in range(2):
            each = jnp.sum(head(part, i), axis=1, keepdims=True)
            total = total + jnp.where(lane == at + i, each, 0.0)
        gg[...] = total
        hg[:, columns] = (gate * hidden).astype(BF)
        pg[:, columns] = (gate * grad * sig * (1.0 + pre * (1.0 - sig))).astype(BF)
        return carry

    lax.fori_loop(0, local // 2, pair, 0, unroll=2)
    for i, (src, dst) in enumerate(((hg, hg_ref), (pg, pg_ref)), 1):
        copies.append(pltpu.make_async_copy(src, dst.at[mine, :], sem_o.at[i]))
        copies[-1].start()
    piece = width // nd

    def blocks(columns):
        for j in range(X):
            for k in range(Z):
                at = pl.multiple_of(place_of(grid, idx, j, k) * rows, rows)
                from_refs[j][k, :, columns] = back[pl.ds(at, rows), : columns.size].astype(BF)

    for q in range(nd):
        columns = pl.ds(q * piece, piece)
        w = jnp.concatenate([up[e, columns, :] for e in range(local)], axis=1)
        back[:, :piece] = dot_nt(pg[...], w)
        blocks(columns)
    back[:, :EXPERTS] = gg[...]
    blocks(pl.ds(width, EXPERTS))
    wait_all(copies)


def out_kernel(grid, tags, micros, idx, hg_ref, *rest):
    nd, nt = grid.nd, len(tags)
    d_refs, (out_ref, hg, down, sem_g, sem_d) = rest[:nt], rest[nt:]
    local, width = down.shape[0], down.shape[2]
    group = hg.shape[0] // micros
    rows = group // grid.ne
    piece = width // nd
    get_d = fetch_experts(grid, idx, d_refs, tags, down, 2, sem_d)
    get_g = pltpu.make_async_copy(hg_ref, hg, sem_g.at[0])
    get_g.start()
    wait_all(get_d)
    get_g.wait()
    for q in range(nd):
        columns = pl.ds(q * piece, piece)
        back = dot(hg[...], down[:, :, columns].reshape(local * LANES, piece)).astype(BF)
        for e in range(grid.ne):
            for m in range(micros):
                at = m * group + e * rows
                out_ref[e, m * rows : (m + 1) * rows, columns] = back[at : at + rows]


def to_dp_place(grid, idx, k, r, piece):
    at = lax.rem(idx[0] + k, grid.Y) * grid.C + lax.rem(idx[1] + r, grid.C)
    return pl.ds(pl.multiple_of(at * piece, piece), piece)


def up_grad_kernel(grid, idx, x_ref, pg_ref, *rest):
    outs, acc = rest[:-1], rest[-1]
    acc[...] = dot_tn(x_ref[...], pg_ref[...])
    piece = outs[0].shape[2]
    for k, r in dp_tags(grid):
        rows = to_dp_place(grid, idx, k, r, piece)
        for e in range(outs[r].shape[1]):
            outs[r][k, e] = acc[rows, e * LANES : (e + 1) * LANES].astype(BF)


def down_grad_kernel(grid, idx, g_ref, hg_ref, *rest):
    outs, acc = rest[:-1], rest[-1]
    places, micros, rows, width = g_ref.shape
    g = jnp.concatenate([g_ref[:, m].reshape(places * rows, width) for m in range(micros)], axis=0)
    acc[...] = dot_tn(hg_ref[...], g)
    piece = outs[0].shape[3]
    for k, r in dp_tags(grid):
        columns = to_dp_place(grid, idx, k, r, piece)
        for e in range(outs[r].shape[1]):
            outs[r][k, e] = acc[e * LANES : (e + 1) * LANES, columns].astype(BF)


def fold_kernel(idx, own, *refs):
    Z = own.shape[0]
    others, out = refs[:-Z], refs[-Z:]
    del idx
    for k in range(Z):
        at = (Z - k) % Z
        total = own[at].astype(F32)
        for ref in others:
            total = total + ref[at].astype(F32)
        out[k][...] = total.astype(BF)


def fold_at_kernel(idx, own, *refs):
    Z = own.shape[0]
    others, out = refs[:-Z], refs[-Z:]
    for k in range(Z):
        at = lax.rem(idx[2] + k, Z)
        total = own[at].astype(F32)
        for ref in others:
            total = total + ref[at].astype(F32)
        out[k][...] = total.astype(BF)


def sum_kernel(*refs):
    total = refs[0][...].astype(F32)
    for ref in refs[1:-1]:
        total = total + ref[...].astype(F32)
    refs[-1][...] = total


def sum_places_kernel(parts, own, out):
    total = own[...]
    for z in range(parts.shape[0]):
        total = total + parts[z].astype(F32)
    out[...] = total


def back_norm_kernel(grid, micros, idx, wmr_ref, res_ref, g_ref, router_ref, picked_ref, *rest):
    nd, Z = grid.nd, grid.Z
    n = micros * Z
    rg_ref, bg_ref, late_ref = rest[n : n + 3]
    cols = rest[n + 3 :]
    width = res_ref.shape[1]
    parts = []
    for m in range(micros):
        total = rest[m * Z][...].astype(F32)
        for ref in rest[m * Z + 1 : (m + 1) * Z]:
            total = total + ref[...].astype(F32)
        parts.append(total)
    back = jnp.concatenate(parts, axis=0)
    router = router_ref[...]
    late = (back[:, width:] * picked_ref[...] * router * (1.0 - router)).astype(BF)
    late_ref[...] = late
    unit, inverse = norm_stats(res_ref[...])
    n2g = dot_nt(late, wmr_ref[:, LANES:])
    a = n2g * gain_row(wmr_ref[:, :LANES], LANE_GAIN_TWO)
    res_grad = g_ref[...].astype(F32) + back[:, :width] + norm_back(a, unit, inverse)
    rg_ref[...] = res_grad
    bg_ref[...] = res_grad.astype(BF)
    piece = width // nd
    for ref, (k, r) in zip(cols, dp_tags(grid)):
        at = lax.rem(idx[0] + k, grid.Y) * grid.C + lax.rem(idx[1] + r, grid.C)
        ref[...] = bg_ref[:, pl.ds(pl.multiple_of(at * piece, piece), piece)]


def back_attend_kernel(grid, tags, idx, bg_ref, rg_ref, sig_ref, mask_ref, early_ref, qk_ref, val_ref, va_ref,
                       pr_ref, *rest):
    n = len(tags)
    o_refs = rest[:n]
    late_ref, vag_ref, wo, sem_o = rest[n:]
    get_o = fetch_rows(grid, idx, o_refs, tags, wo, sem_o, COL_OUT)
    bg = bg_ref[...]
    tokens = bg.shape[0]
    sig, gate = sig_ref[...], early_ref[:, H * DH :]
    lane = lanes_of((tokens, LANES))
    logits = jnp.zeros((tokens, LANES), F32)
    wait_all(get_o)
    for h in range(H):
        att = early_ref[:, h * DH : (h + 1) * DH]
        mg = dot(bg, wo[:, h * EA * DH : (h + 1) * EA * DH])
        ag = jnp.zeros((tokens, DH), F32)
        for e in range(EA):
            i = HE + h * EA + e
            ag = ag + col(gate, i) * head(mg, e)
            each = jnp.sum(head(mg, e) * att, axis=1, keepdims=True)
            logits = jnp.where(lane == i, each, logits)
        ag = ag.astype(BF)
        prob = pr_ref[:, h * tokens : (h + 1) * tokens]
        vg = dot_tn(prob.astype(BF), ag)
        pgrad = dot_nt(ag, val_ref[:, h * DH : (h + 1) * DH])
        delta = jnp.sum(prob * pgrad, axis=-1, keepdims=True)
        sg = (prob * (pgrad - delta) * SCALE).astype(BF)
        late_ref[:, h * DH : (h + 1) * DH] = dot(
            sg, qk_ref[:, (H + h) * DH : (H + h + 1) * DH]
        ).astype(BF)
        late_ref[:, (H + h) * DH : (H + h + 1) * DH] = dot_tn(
            sg, qk_ref[:, h * DH : (h + 1) * DH]
        ).astype(BF)
        late_ref[:, COL_VG + h * DH : COL_VG + (h + 1) * DH] = vg.astype(BF)
        for e in range(EA):
            i = h * EA + e
            each = jnp.sum(va_ref[:, i * DH : (i + 1) * DH] * vg, axis=1, keepdims=True)
            logits = jnp.where(lane == i, each, logits)
            vag_ref[:, i * DH : (i + 1) * DH] = (col(gate, i) * vg).astype(BF)
    late_ref[:, COL_LG:COL_VG] = (logits * mask_ref[...] * sig * (1.0 - sig)).astype(BF)
    late_ref[:, COL_RG:] = rg_ref[...]


def back_token_kernel(grid, a_tags, idx, x_ref, rg_ref, late_ref, vag_ref, *rest):
    na = len(a_tags)
    a_refs = rest[:na]
    gt_ref, wa, wv, sem_a, sem_v = rest[na:]
    get_a = fetch_rows(grid, idx, a_refs, a_tags, wa, sem_a)
    get_v = fetch_rows(grid, idx, a_refs, a_tags, wv, sem_v, COL_VALUES)
    unit, inverse = norm_stats(x_ref[...].astype(F32))
    wait_all(get_a)
    n1g = dot_nt(late_ref[:, :COL_VG], wa[:, :COL_ROUTER])
    b = n1g * gain_row(wa[:, COL_SEL:COL_ROUTER], LANE_GAIN_ONE)
    wait_all(get_v)
    gt_ref[...] = rg_ref[...] + dot_nt(vag_ref[...], wv[...]) + norm_back(b, unit, inverse)


def stacked(refs, first=0, last=None):
    return jnp.concatenate([r[:, first:last] for r in refs], axis=0)


def in_order(grid, idx, ref, first=0, size=None):
    size = ref.shape[2] - first if size is None else size
    return jnp.concatenate(
        [ref[shard_at(grid, idx, k, r), :, pl.ds(first, size)] for k, r in dp_tags(grid)], axis=0
    )


def by_owner(grid, idx, out_refs, value, first=0):
    X, Z = grid.X, grid.Z
    mine = value.shape[0] // (X * Z)
    columns = pl.ds(first, value.shape[1])
    for z in range(Z):
        blocks = [value[(z * X + x) * mine : (z * X + x + 1) * mine] for x in range(X)]
        for j in range(X):
            chosen = blocks[0]
            for x in range(1, X):
                chosen = jnp.where(lax.rem(idx[3] + j, X) == x, blocks[x], chosen)
            out_refs[j][z, :, columns] = chosen.astype(BF)


def grad_out_kernel(grid, idx, early, *refs):
    nd = grid.nd
    bgs, out = refs[:nd], refs[nd:]
    wide = H * DH
    gate = in_order(grid, idx, early, wide)
    att = in_order(grid, idx, early, 0, wide)
    by_owner(grid, idx, out, dot_tn(stacked(bgs), mixed_of(gate, att, HE)))


def own_columns(grid, idx, cols, which):
    piece = cols.shape[2] // (3 * grid.nd)
    at = which * piece * grid.nd + shard_at(grid, idx, 0, 0) * piece
    return in_order(grid, idx, cols, pl.multiple_of(at, piece), piece)


def grad_rest_kernel(grid, idx, cols, early, a_ref, *refs):
    nd = grid.nd
    late, out = refs[:nd], refs[nd:]
    x, n1, n2 = [own_columns(grid, idx, cols, i) for i in range(3)]
    acts = stacked(late)
    both = dot_tn(n1, acts[:, :COL_VG])
    by_owner(grid, idx, out, both[:, :COL_SEL])
    misc = a_ref[:, COL_SEL:COL_ROUTER].astype(F32)
    stats = in_order(grid, idx, early, H * DH)
    unit = (x.astype(F32) - col(stats, LANE_MEAN)) * col(stats, LANE_INVERSE)
    n1_grad = dot_nt(acts[:, :COL_VG], a_ref[:, :COL_ROUTER])
    n2_grad = dot_nt(acts[:, COL_RG:], a_ref[:, COL_ROUTER:])
    one = jnp.sum(n1_grad * unit, axis=0, keepdims=True)
    gains = jnp.transpose(misc)[LANE_GAIN_TWO : LANE_GAIN_TWO + 1]
    two = jnp.sum(n2_grad * n2.astype(F32), axis=0, keepdims=True) / gains
    row = rows_of((LANES, one.shape[1]))
    extra = jnp.where(row == LANE_GAIN_ONE, one, 0.0)
    extra = jnp.where(row == LANE_GAIN_TWO, two, extra)
    by_owner(grid, idx, out, both[:, COL_SEL:] + jnp.transpose(extra), COL_SEL)
    by_owner(grid, idx, out, dot_tn(n2, acts[:, COL_RG:]), COL_ROUTER)
    mixed = mixed_of(stats, acts[:, COL_VG:COL_RG].astype(F32), 0)
    by_owner(grid, idx, out, dot_tn(x, mixed), COL_VALUES)


def finish_kernel(*refs):
    parts, (q, k, v, vs, os, router, one, two) = refs[:-8], refs[-8:]
    total = parts[0][...].astype(F32)
    for ref in parts[1:]:
        total = total + ref[...].astype(F32)
    wide = H * DH
    q[...] = total[:, :wide]
    k[...] = total[:, wide:COL_SEL]
    misc = total[:, COL_SEL:COL_ROUTER]
    turned = jnp.transpose(misc)
    vs[...] = turned[:HE]
    os[...] = turned[HE : 2 * HE]
    one[...] = turned[LANE_GAIN_ONE : LANE_GAIN_ONE + 1]
    two[...] = turned[LANE_GAIN_TWO : LANE_GAIN_TWO + 1]
    router[...] = total[:, COL_ROUTER:COL_VALUES]
    v[...] = total[:, COL_VALUES:]


def shape(dims, dtype):
    return jax.ShapeDtypeStruct(dims, dtype)


def call(name, kernel, operands, specs, outs, scratch=(), mib=58, us=5, aliases=None):
    outs = [o if isinstance(o, tuple) else (o, VMEM) for o in outs]
    operands = [
        o if s is SMEM else pltpu.with_memory_space_constraint(o, pltpu.HBM)
        for o, s in zip(operands, specs, strict=True)
    ]
    return pl.pallas_call(
        kernel,
        out_shape=tuple(pltpu.HBM(o[0].shape, o[0].dtype) for o in outs),
        in_specs=list(specs),
        out_specs=tuple(o[1] for o in outs),
        scratch_shapes=list(scratch),
        input_output_aliases=aliases or {},
        compiler_params=pltpu.CompilerParams(vmem_limit_bytes=mib * 1024 * 1024),
        cost_estimate=pl.CostEstimate(
            flops=us, bytes_accessed=us, transcendentals=0
        ),
        name=name,
    )(*operands)


def dma(n):
    return pltpu.SemaphoreType.DMA((n,))


def per_device(
    nd,
    ne,
    tokens,
    cotangent,
    segments,
    value_picks,
    output_picks,
    expert_picks,
    attn_gain,
    query_weight,
    key_weight,
    value_weight,
    output_expert_weight,
    value_select,
    output_select,
    moe_gain,
    router_weight,
    up_weight,
    down_weight,
):
    grid = Grid(nd, ne)
    X, Y, Z, C = grid.X, grid.Y, grid.Z, grid.C
    micros, length, width = tokens.shape
    rows = micros * length
    local = up_weight.shape[0]
    piece = width // nd
    wide = H * DH
    values_wide = HE * DH
    dp, ex = lax.axis_index("dp"), lax.axis_index("expert")
    idx = jnp.stack([dp // C, dp % C, ex // X, ex % X]).astype(jnp.int32)


    x_all = tokens.reshape(rows, width)
    g_all = cotangent.reshape(rows, width)

    ends = (*STARTS[1:], COL_A)
    block_w, block_a, *parts_a = call(
        "pack",
        functools.partial(pack_kernel, grid),
        (
            idx,
            query_weight,
            key_weight,
            value_select.T,
            output_select.T,
            attn_gain,
            moe_gain,
            router_weight,
            value_weight,
            output_expert_weight,
        ),
        [SMEM] + [VMEM] * 9,
        [shape((piece, COL_A), BF), shape((piece, COL_VALUES), BF)]
        + [shape((piece // X, high - low), BF) for low, high in zip(STARTS, ends)],
        [pltpu.VMEM((LANES, piece), F32)],
        us=3,
    )

    def to_y(v, *deps):
        v = after(v, *deps)
        return [grid.rot_y(v, k) for k in range(1, Y)]

    def over_x(got_y, *deps):
        return [[v] + [grid.rot_x(after(v, *deps), j) for j in range(1, X)] for v in got_y]

    def add_pieces(arrays, tags, v, tag, swapped=None):
        k, split, j, column = tag
        arrays.append(v)
        tags.append((k, 0, split, j, column))
        if C > 1:
            arrays.append(grid.swap(v) if swapped is None else swapped)
            tags.append((k, 1, split, j, column))

    def swap(v, *deps):
        return grid.swap(after(v, *deps)) if C > 1 else None

    def spread_x(got_y, *deps):
        return [[v] + [grid.rot_x(after(v, *deps), j) for j in range(1, X)] for v in got_y]

    def swap_all(values, *deps):
        return [swap(v, *deps) for v in values]

    def flat(by_k):
        return [v for by_j in by_k for v in by_j]

    g_gathered = lax.all_gather(g_all, "expert", axis=0, tiled=True)
    swap_w = swap(block_w)
    seg = segments.reshape(1, rows)
    v_picks, o_picks = value_picks.reshape(rows, 2 * H), output_picks.reshape(rows, 2 * H)
    e_picks = expert_picks.reshape(rows, -1)
    done = [swap_w, seg, v_picks, o_picks, e_picks]
    over_y, over_x_too, swap_y, swap_x = [to_y(parts_a[0])], [], [], []
    done.append(over_y[0])
    swap_d = swap_u = d_y = None
    for i in range(len(STARTS)):
        last_round = i == len(STARTS) - 1
        new = []
        if not last_round:
            over_y.append(to_y(parts_a[i + 1], *done))
            new += over_y[-1]
        else:
            d_y = to_y(down_weight, *done)
            swap_u = swap(up_weight, *done)
            new.append(swap_u)
        if i == len(STARTS) - 2:
            new.append(g_gathered)
            swap_d = swap(down_weight, *done)
            new.append(swap_d)
        over_x_too.append(spread_x(over_y[i], *done))
        swap_y.append(swap_all(over_y[i], *done))
        new += flat(over_x_too[-1]) + swap_y[-1]
        if i:
            swap_x.append([swap_all(by_j[1:], *done) for by_j in over_x_too[i - 1]])
            new += flat(swap_x[-1])
        done = new
    swap_x.append([swap_all(by_j[1:], *done) for by_j in over_x_too[-1]])
    done = flat(swap_x[-1])

    def weight_pieces(own, swapped, chunks):
        arrays, tags = [own, swapped], [(0, 0, None, 0, 0), (0, 1, None, 0, 0)]
        for column, got, others in chunks:
            for k, (by_j, swaps) in enumerate(zip(got, others), 1):
                for j, (v, o) in enumerate(zip(by_j, swaps)):
                    split = "x" if len(by_j) > 1 else None
                    arrays += [v, o]
                    tags += [(k, 0, split, j, column), (k, 1, split, j, column)]
        return arrays, tags

    chunks = [
        (low, got, [[v] + more for v, more in zip(ys, xs)])
        for low, got, ys, xs in zip(STARTS, over_x_too, swap_y, swap_x)
    ]
    first_pieces, first_tags = weight_pieces(block_w, swap_w, chunks[:1])
    a_pieces, a_tags = weight_pieces(block_w, swap_w, chunks)

    n1, qk, sig, mask, probs, wmr = call(
        "attend",
        functools.partial(attend_kernel, grid, first_tags, length),
        (
            idx,
            x_all,
            seg,
            v_picks,
            o_picks,
            *first_pieces,
        ),
        [SMEM] + [VMEM] * 4 + [ANY] * len(first_pieces),
        [
            shape((rows, width), BF),
            shape((rows, 2 * wide), BF),
            shape((rows, LANES), F32),
            shape((rows, LANES), F32),
            shape((rows, H * rows), F32),
            shape((width, 2 * LANES), BF),
        ],
        [pltpu.VMEM((width, COL_VALUES), BF), dma(len(first_pieces))],
        us=4,
    )
    v_pieces, v_tags = window(a_pieces, a_tags, COL_VALUES, COL_OUT)
    o_pieces, o_tags = window(a_pieces, a_tags, COL_OUT, COL_A)
    vals, va, early, res, router, picked, xg, cols = call(
        "route",
        functools.partial(route_kernel, grid, v_tags, o_tags),
        (idx, x_all, n1, sig, mask, probs, wmr, e_picks, *v_pieces, *o_pieces),
        [SMEM] + [VMEM] * 7 + [ANY] * (len(v_pieces) + len(o_pieces)),
        [
            shape((rows, wide), BF),
            shape((rows, values_wide), F32),
            shape((rows, wide + LANES), F32),
            shape((rows, width), F32),
            shape((rows, EXPERTS), F32),
            shape((rows, EXPERTS), F32),
            shape((rows, width + EXPERTS), BF),
            shape((rows, 3 * width), BF),
        ],
        [
            pltpu.VMEM((width, values_wide), BF),
            pltpu.VMEM((width, values_wide), BF),
            dma(len(v_pieces)),
            dma(len(o_pieces)),
        ],
        us=8,
    )

    group = ne * length
    ff = local * LANES
    swap_dy = swap_all(d_y, xg)
    u_y = to_y(up_weight, xg, *d_y)
    column, x_over, done = [xg], [], []
    for k in range(1, Z):
        held = after(column[-1], *done)
        column.append(grid.rot_z(held, 1))
        x_over.append([grid.rot_x(held, j) for j in range(1, X)])
        last_done, done = done, [column[-1], x_over[-1], *([u_y] if k == Z - 2 else [])]
    ring_done = done
    swap_uy = swap_all(u_y, *last_done)

    def expert_pieces(own, swapped, got, others):
        arrays, tags = [own, swapped], [(0, 0, 0), (0, 1, 0)]
        for k, (v, o) in enumerate(zip(got, others), 1):
            arrays += [v, o]
            tags += [(k, 0, 0), (k, 1, 0)]
        return arrays, tags

    d_pieces, d_tags = expert_pieces(down_weight, swap_d, d_y, swap_dy)
    u_pieces, u_tags = expert_pieces(up_weight, swap_u, u_y, swap_uy)
    g_rows = g_gathered.reshape(ne, micros, length, width)
    total = micros * group
    (ahead,) = call(
        "ahead",
        functools.partial(ahead_kernel, grid, d_tags),
        (idx, after(g_rows, *last_done), *d_pieces),
        [SMEM] + [ANY] * (1 + len(d_tags)),
        [(shape((total, ff), BF), ANY)],
        [
            pltpu.VMEM((ne, micros, length, width), BF),
            pltpu.VMEM((local, LANES, width), BF),
            pltpu.VMEM((total, ff), BF),
            dma(1),
            dma(len(d_tags)),
            dma(local // 2),
        ],
        us=9,
    )
    x_over.append([grid.rot_x(after(column[-1], ahead, *ring_done), j) for j in range(1, X)])
    x_pieces = column + [by_j[j] for j in range(X - 1) for by_j in x_over]
    froms = []

    def over_x(parts):
        return [grid.rot_x(parts[j], -j) for j in range(1, X)]

    def fold(parts, others, *deps):
        return call(
            "fold",
            fold_kernel,
            (idx, after(parts[0], *deps), *others),
            [SMEM] + [VMEM] * X,
            [shape(parts[0].shape[1:], BF)] * Z,
            us=2,
        )

    sent, shared = [], []
    for m in range(micros):
        hg, pg, x_group, *back = call(
            "experts",
            functools.partial(expert_kernel, grid, u_tags, m, micros),
            (idx, ahead, *x_pieces, *u_pieces, *shared),
            [SMEM, ANY] + [ANY] * (ne + len(u_tags) + len(shared)),
            [
                (shape((total, ff), BF), ANY),
                (shape((total, ff), BF), ANY),
                (shape((total, width + EXPERTS), BF), ANY),
                *[shape((Z, length, width + EXPERTS), BF)] * X,
            ],
            [
                pltpu.VMEM((group, ff), BF),
                pltpu.VMEM((group, ff), BF),
                pltpu.VMEM((group, width + EXPERTS), BF),
                pltpu.VMEM((group, ff), BF),
                pltpu.VMEM((local, width, LANES), BF),
                pltpu.VMEM((group, EXPERTS), F32),
                pltpu.VMEM((group, max(piece, EXPERTS)), F32),
                dma(ne),
                dma(len(u_tags)),
                dma(1),
                dma(3),
            ],
            us=12,
            aliases={2 + ne + len(u_tags) + i: i for i in range(len(shared))},
        )
        shared = [hg, pg, x_group]
        sent.append(back)

    def out_rows(*deps):
        return call(
            "out",
            functools.partial(out_kernel, grid, d_tags, micros),
            (idx, after(hg, *deps), *d_pieces),
            [SMEM] + [ANY] * (1 + len(d_tags)),
            [shape((ne, rows, width), BF)],
            [
                pltpu.VMEM((total, ff), BF),
                pltpu.VMEM((local, LANES, width), BF),
                dma(1),
                dma(len(d_tags)),
            ],
            us=10,
        )

    def expert_grad(name, kernel, lhs, rhs, dims, *deps):
        halves = 2
        block = pl.BlockSpec((Y, local // halves, *dims), lambda h, idx: (0, h, 0, 0))
        if lhs.ndim == 4:
            whole = pl.BlockSpec((ne, micros, length, width), lambda h, idx: (0, 0, 0, 0))
        else:
            whole = pl.BlockSpec((total, width), lambda h, idx: (0, 0))
        part = (width, ff // halves) if lhs.ndim == 2 else (ff // halves, width)
        return pl.pallas_call(
            functools.partial(kernel, grid),
            out_shape=[pltpu.HBM((Y, local, *dims), BF)] * C,
            grid_spec=pltpu.PrefetchScalarGridSpec(
                num_scalar_prefetch=1,
                grid=(halves,),
                in_specs=[whole, pl.BlockSpec((total, ff // halves), lambda h, idx: (0, h))],
                out_specs=[block] * C,
                scratch_shapes=[pltpu.VMEM(part, F32)],
            ),
            compiler_params=pltpu.CompilerParams(vmem_limit_bytes=58 * 1024 * 1024),
            cost_estimate=pl.CostEstimate(flops=4, bytes_accessed=12, transcendentals=0),
            name=name,
        )(idx, *[pltpu.with_memory_space_constraint(v, pltpu.HBM) for v in (after(lhs, *deps), rhs)])

    def added_blocks(name, arrays, dtype, split):
        steps = 2
        dims = arrays[0].shape[1:] if split else arrays[0].shape
        some = (dims[0] // steps, *dims[1:])
        one = pl.BlockSpec(some, lambda i: (i, 0, 0))
        spec = pl.BlockSpec((Y, *some), lambda i: (0, i, 0, 0)) if split else one
        results = Y if split else 1

        def kernel(*refs):
            for k, out in enumerate(refs[len(arrays) :]):
                total = 0.0
                for ref in refs[: len(arrays)]:
                    total = total + (ref[k] if split else ref[...]).astype(F32)
                out[...] = total.astype(dtype)

        return pl.pallas_call(
            kernel,
            out_shape=[pltpu.HBM(dims, dtype)] * results,
            grid=(steps,),
            in_specs=[spec] * len(arrays),
            out_specs=[one] * results,
            compiler_params=pltpu.CompilerParams(vmem_limit_bytes=58 * 1024 * 1024),
            cost_estimate=pl.CostEstimate(flops=1, bytes_accessed=3, transcendentals=0),
            name=name,
        )(*[pltpu.with_memory_space_constraint(v, pltpu.HBM) for v in arrays])

    down_args = ("down_grad", down_grad_kernel, g_rows, hg, (LANES, piece))
    up_args = ("up_grad", up_grad_kernel, x_group, pg, (piece, LANES))

    def reduce_y(total, *deps):
        got = [grid.rot_y(after(total[k], *deps), k) for k in range(1, Y)]
        return lambda *more: added_blocks("last_sum", [after(total[0], *more), *got], F32, False)[0], got

    from_x = [over_x(v) for v in sent]
    sums = fold(sent[0], from_x[0], hg)
    froms.append(grid.send_z(sums))
    outs_sent = out_rows(sums[0])
    before, down_came, up_came = outs_sent[0], [], []
    for m in range(1, micros):
        sums = fold(sent[m], from_x[m], before, froms[-1])
        froms.append(grid.send_z(sums))
        before = sums[0]
    down_near, *down_far = expert_grad(*down_args, before)
    up_near, *up_far = expert_grad(*up_args, down_near)
    before = up_near

    early_all = lax.all_gather(after(early, u_pieces), "dp", axis=0)
    cols_all = lax.all_gather(after(cols, u_pieces), "dp", axis=0)
    res_grad, bg, rg, *bg_cols = call(
        "back_norm",
        functools.partial(back_norm_kernel, grid, micros),
        (
            idx,
            wmr,
            res,
            g_all,
            after(router, before, early_all, cols_all),
            picked,
            *[p for f in froms for p in f],
        ),
        [SMEM] + [VMEM] * (5 + micros * Z),
        [
            shape((rows, width), F32),
            shape((rows, width), BF),
            shape((rows, EXPERTS), BF),
            *[shape((rows, piece), BF)] * nd,
        ],
        us=3,
    )
    bgs = [v if t == (0, 0) else grid.rot_yc(v, *t) for v, t in zip(bg_cols, dp_tags(grid))]
    late, vag = call(
        "back_attend",
        functools.partial(back_attend_kernel, grid, o_tags),
        (idx, bg, rg, sig, mask, early, qk, vals, va, probs, *o_pieces),
        [SMEM] + [VMEM] * 9 + [ANY] * len(o_pieces),
        [shape((rows, COL_LATE), BF), shape((rows, values_wide), BF)],
        [pltpu.VMEM((width, values_wide), BF), dma(len(o_pieces))],
        us=8,
    )
    outs = lax.all_to_all(after(outs_sent[0], bg), "expert", 0, 0, tiled=True)
    down_came, up_came = swap_all(down_far, bg), swap_all(up_far, bg)
    late_swap = swap(late, bgs[1:], *down_came, *up_came)
    late_y = to_y(late, bgs[1:])

    mine = piece // ne

    def weight_grad(name, kernel, operands, columns):
        parts = call(
            name,
            functools.partial(kernel, grid),
            (idx, *operands),
            [SMEM] + [VMEM] * len(operands),
            [shape((Z, mine, columns), BF)] * X,
            us=3,
        )
        return parts, [grid.rot_x(parts[j], j) for j in range(1, X)]

    def fold_at(parts, others, *deps):
        sums = call(
            "fold_at",
            fold_at_kernel,
            (idx, after(parts[0], *deps), *others),
            [SMEM] + [VMEM] * X,
            [shape(parts[0].shape[1:], BF)] * Z,
            us=1,
        )
        return sums[0], grid.send_z(sums)

    def added(parts, *deps):
        return call(
            "sum",
            sum_kernel,
            (after(parts[0], *deps), *parts[1:]),
            [VMEM] * len(parts),
            [shape(parts[0].shape, F32)],
            us=1,
        )[0]

    down_sum = added_blocks("core_sum", [after(down_near, late), *down_came], BF, True)
    up_sum = added_blocks("core_sum", [after(up_near, down_sum), *up_came], BF, True)
    o_parts, o_others = weight_grad(
        "grad_out", grad_out_kernel, [after(early_all, up_sum), *bgs], values_wide
    )
    down_last, down_got = reduce_y(down_sum, late_y)
    up_last, up_got = reduce_y(up_sum, late_y)
    late_all = [late, *late_y, late_swap, *swap_all(late_y, o_parts[0])]
    r_parts, r_others = weight_grad(
        "grad_rest",
        grad_rest_kernel,
        [after(cols_all, o_parts[0]), early_all, block_a, *late_all],
        COL_OUT,
    )
    o_fold, o_sums = fold_at(o_parts, o_others, r_parts[0])
    r_fold, r_sums = fold_at(r_parts, r_others, o_sums, outs)
    grad_down = down_last(r_fold)
    grad_up = up_last(grad_down)
    (grad_tokens,) = call(
        "back_token",
        functools.partial(back_token_kernel, grid, a_tags),
        (idx, x_all, res_grad, after(late, r_fold), vag, *a_pieces),
        [SMEM] + [VMEM] * 4 + [ANY] * len(a_pieces),
        [shape((rows, width), F32)],
        [
            pltpu.VMEM((width, COL_VALUES), BF),
            pltpu.VMEM((width, values_wide), BF),
            dma(len(a_pieces)),
            dma(len(a_pieces)),
        ],
        us=8,
    )
    (output,) = call(
        "add_out",
        sum_places_kernel,
        (outs, after(res, grad_tokens)),
        [VMEM] * 2,
        [shape((rows, width), F32)],
        us=2,
    )
    grad_output = added(o_sums, output)
    q, k, grad_value, vs, os, r, one, two = call(
        "finish",
        finish_kernel,
        (after(r_sums[0], grad_tokens, output, grad_output, grad_up), *r_sums[1:]),
        [VMEM] * Z,
        [
            shape((mine, wide), F32),
            shape((mine, wide), F32),
            shape((mine, values_wide), F32),
            shape((HE, mine), F32),
            shape((HE, mine), F32),
            shape((mine, EXPERTS), F32),
            shape((1, mine), F32),
            shape((1, mine), F32),
        ],
        us=1,
    )
    return (
        output.reshape(micros, length, width),
        grad_tokens.reshape(micros, length, width),
        one.reshape(mine),
        q,
        k,
        grad_value,
        grad_output,
        vs.T,
        os.T,
        two.reshape(mine),
        r,
        grad_up,
        grad_down,
    )


def solution(mesh):
    rows = ("dp", "expert")
    placed = (
        P(None, rows, None),
        P(None, rows, None),
        P(None, rows, None),
        P(None, rows, None, None),
        P(None, rows, None, None),
        P(None, rows, None),
        P("dp"),
        P("dp", None),
        P("dp", None),
        P("dp", None),
        P("dp", None),
        P("dp", None),
        P("dp", None),
        P("dp"),
        P("dp", None),
        P("expert", "dp", None),
        P("expert", None, "dp"),
    )
    return jax.shard_map(
        functools.partial(per_device, mesh.shape["dp"], mesh.shape["expert"]),
        mesh=mesh,
        in_specs=placed,
        out_specs=(
            P(None, rows, None),
            P(None, rows, None),
            P(rows),
            P(rows, None),
            P(rows, None),
            P(rows, None),
            P(rows, None),
            P(rows, None),
            P(rows, None),
            P(rows),
            P(rows, None),
            P("expert", "dp", None),
            P("expert", None, "dp"),
        ),
        check_vma=False,
    )
```

time: 416 us -> 360 us (0.87); the launches traced: 415 us -> 353 us
  waiting for transfers between devices: 194 us -> 110 us
  Pallas kernels: 87.5 us -> 150 us
  local copies, waits for them, and re-layouts: 36.2 us -> 13.3 us
  starting transfers between devices: 80.6 us -> 63.4 us
  other arithmetic: 15.3 us -> 1.25 us
  between operations: 1.75 us -> 14.7 us
    ppermute x39 -> x26, waiting for transfers between devices: 162 us -> 70.4 us  [_ex(): return lax.ppermute(v, 'expert', pairs)]
    pallas_call x8 -> x25, Pallas kernels: 87.5 us -> 150 us  [the longest x19 119 us: call(): pl.pallas_call(kernel, out_shape=tuple((pltpu.HBM(o[0].shape, o[0].dtype)...]
    all_gather x0 -> x3, waiting for transfers between devices: none -> 21 us  [the longest x1 21 us: per_device(): g_gathered = lax.all_gather(g_all, 'expert', axis=0, tiled=True)]
    ppermute x39 -> x26, starting transfers between devices: 63.2 us -> 42.3 us  [_ex(): return lax.ppermute(v, 'expert', pairs)]
    ppermute x34 -> x26, waiting for transfers between devices: 32.4 us -> 18 us  [_dp(): return lax.ppermute(v, 'dp', pairs)]
    add x7 -> x0, other arithmetic: 6.05 us -> none  [the longest x2 3.12 us: reduce_dp(): result = result + grid.rot_y(sent[k - 1], k).astype(F32)]
    concatenate x6 -> x0, local copies, waits for them, and re-layouts: 5.14 us -> none  [the longest x4 3.87 us: gather_rows(): jnp.concatenate([column] + [grid.rot_x(column, j) for j in range(1, X)],...]
    slice x11 -> x0, local copies, waits for them, and re-layouts: 4.8 us -> none  [the longest x1 1.68 us: per_device(): g_all[m * length:(m + 1) * length]]
  transfers between devices with their start and end apart: 73 -> 56, of which waited for: 26 -> 15; matrix products, arithmetic and copies ran while one was open for 10% -> 1% of each run, Pallas kernels for 21% -> 40%
where the time goes in v2:
time: 360 us; the launch traced here: 353 us
  Pallas kernels  150 us (42%)
  waiting for transfers between devices  110 us (31%)
  starting transfers between devices  63.4 us (18%)
  between operations  14.7 us (4%)
  local copies, waits for them, and re-layouts  13.3 us (4%)
    pallas_call x19, Pallas kernels, call(): pl.pallas_call(kernel, out_shape=tuple((pltpu.HBM(o[0].shape, o[0].dtype)...  119 us
    ppermute x26, waiting for transfers between devices, _ex(): return lax.ppermute(v, 'expert', pairs)  70.4 us
    ppermute x26, starting transfers between devices, _ex(): return lax.ppermute(v, 'expert', pairs)  42.3 us
    all_gather x1, waiting for transfers between devices, per_device(): g_gathered = lax.all_gather(g_all, 'expert', axis=0, tiled=True)  21 us
    pallas_call x2, Pallas kernels, expert_grad(): pl.pallas_call(functools.partial(kernel, grid), out_shape=[pltpu.HBM((Y,...  19.6 us
    ppermute x26, waiting for transfers between devices, _dp(): return lax.ppermute(v, 'dp', pairs)  18 us
    ppermute x26, starting transfers between devices, _dp(): return lax.ppermute(v, 'dp', pairs)  17.1 us
    pallas_call x4, Pallas kernels, added_blocks(): pl.pallas_call(kernel, out_shape=[pltpu.HBM(dims, dtype)] * results, grid...  11.9 us
  transfers between devices with their start and end apart: 56, of which 15 were waited for; matrix products, arithmetic and copies ran while one was open for 1% of the time, Pallas kernels for 40%

profile of v2, /device:TPU:0, one launch (start us, length us, event | category | flops | bytes accessed | tf_op | source)
XLA Modules:
  0.0 353.4 jit_solution(11766147236491808849)
XLA Ops:
  7.9 4.6 %pack.1 = (bf16[256,6400]{1,0:T(8,128)(2,1)}, bf16[256,1280]{1,0:T(8,128)(2,1)}, bf16[128,2176]{1,0:T(8,128)(2,1)}, bf16[128,2176]{1,0:T(8,128)(2,1)}, bf16[128,2048]{1,0:T(8,128)(2,1)}) custom-call(s32[4]{0:T(128)} %pad_add_fusion.idx, bf16[256,512]{1,0:T(8,128)(2,1)} %q.1, bf16[256,512]{1,0:T(8,128)(2,1)} %k.1, bf16[20,256]{1,0:T(8,128)(2,1)} %bitcast.35, ...), custom_call_target="tpu_custom_call" | custom-call | flops 3 | bytes 3 | tf_op jit(solution)/shard_map/pack/pallas_call | solution.py:701
  13.0 2.6 collective-permute-start.1
  18.2 11.0 %collective-permute-done.1.rest_2_ = bf16[128,2176]{1,0:T(8,128)(2,1)} collective-permute-done((bf16[128,2176]{1,0:T(8,128)(2,1)}, bf16[128,2176]{1,0:T(8,128)(2,1)}, u32[]{:S(2)}, u32[]{:S(2)}) %collective-permute-start.1) | collective-permute-done | bytes 557088 | tf_op jit(solution)/shard_map/ppermute | solution.py:75
  32.5 13.2 %collective-permute-done.3.rest_4_ = bf16[128,2176]{1,0:T(8,128)(2,1)} collective-permute-done((bf16[128,2176]{1,0:T(8,128)(2,1)}, bf16[128,2176]{1,0:T(8,128)(2,1)}, u32[]{:S(2)}, u32[]{:S(2)}) %collective-permute-start.3) | collective-permute-done | bytes 557088 | tf_op jit(solution)/shard_map/ppermute | solution.py:83
  46.5 2.2 collective-permute-start.7
  50.1 21.0 %all-gather.6.cloned.1.call-done = bf16[1024,1024]{1,0:T(8,128)(2,1)} async-done(((bf16[128,1024]{1,0:T(8,128)(2,1)}), bf16[1024,1024]{1,0:T(8,128)(2,1)}) %all-gather.6.cloned.1.call-update) | async-done | bytes 2097168 | tf_op jit(solution)/shard_map/all_gather | solution.py:806
  75.7 10.6 %collective-permute-done.12.rest_18_.rest_8_.rest_12_ = bf16[128,2048]{1,0:T(8,128)(2,1)} collective-permute-done((bf16[128,2048]{1,0:T(8,128)(2,1)}, bf16[128,2048]{1,0:T(8,128)(2,1)}, u32[]{:S(2)}, u32[]{:S(2)}) %collective-permute-start.12) | collective-permute-done | bytes 524320 | tf_op jit(solution)/shard_map/ppermute | solution.py:83
  87.8 4.5 %attend.1 = (bf16[128,1024]{1,0:T(8,128)(2,1)}, bf16[128,1024]{1,0:T(8,128)(2,1)}, f32[128,128]{1,0:T(8,128)}, f32[128,128]{1,0:T(8,128)}, f32[128,512]{1,0:T(8,128)}, /*index=5*/bf16[1024,256]{1,0:T(8,128)(2,1)}) custom-call(s32[4]{0:T(128)} %pad_add_fusion.idx, bf16[128,1024]{1,0:T(8,128)(2,1)} %bitcast.27, s32[1,128]{1,0:T(1,128)} %reshape.62.seg_ref, ...), custom_call_target="tpu_custom_call" | custom-call | flops 4 | bytes 4 | tf_op jit(solution)/shard_map/attend/pallas_call | solution.py:701
  92.3 10.3 %route.1 = (bf16[128,512]{1,0:T(8,128)(2,1)}, f32[128,2560]{1,0:T(8,128)}, f32[128,640]{1,0:T(8,128)}, f32[128,1024]{1,0:T(8,128)}, f32[128,128]{1,0:T(8,128)}, ...) custom-call(s32[4]{0:T(128)} %pad_add_fusion.idx, bf16[128,1024]{1,0:T(8,128)(2,1)} %bitcast.28, ...), custom_call_target="tpu_custom_call" | custom-call | flops 8 | bytes 8 | tf_op jit(solution)/shard_map/route/pallas_call | solution.py:701
  107.0 8.3 %collective-permute-done.15.rest_1_ = bf16[128,1152]{1,0:T(8,128)(2,1)S(1)} collective-permute-done((bf16[128,1152]{1,0:T(8,128)(2,1)}, bf16[128,1152]{1,0:T(8,128)(2,1)S(1)}, u32[]{:S(2)}, u32[]{:S(2)}) %collective-permute-start.15) | collective-permute-done | bytes 294944 | tf_op jit(solution)/shard_map/ppermute | solution.py:83
  117.0 8.5 %collective-permute-done.17.rest_2_ = bf16[128,1152]{1,0:T(8,128)(2,1)S(1)} collective-permute-done((bf16[128,1152]{1,0:T(8,128)(2,1)S(1)}, bf16[128,1152]{1,0:T(8,128)(2,1)S(1)}, u32[]{:S(2)}, u32[]{:S(2)}) %collective-permute-start.17) | collective-permute-done | bytes 294944 | tf_op jit(solution)/shard_map/ppermute | solution.py:83
  125.5 2.8 collective-permute-done.20.rest_10_
  128.3 2.7 collective-permute-done.25.rest_11_
  131.9 2.2 collective-permute-start.22
  136.2 9.2 %ahead.1.gh_ref = bf16[1024,2048]{1,0:T(8,128)(2,1)} custom-call(s32[4]{0:T(128)} %pad_add_fusion.idx, bf16[8,2,64,1024]{3,2,1,0:T(8,128)(2,1)} %bitcast.22, bf16[16,128,256]{2,1,0:T(8,128)(2,1)} %rest_0_.3, bf16[16,128,256]{2,1,0:T(8,128)(2,1)} %collective-permute-done.9.rest_1_, bf16[16,128,256]{2,1,0:T(8,128)(2,1)} %collective-permute-done.19.rest_2_, ...), custom_call_target="tpu_custom_call" | custom-call | flops 9 | bytes 9 | tf_op jit(solution)/shard_map/ahead/pallas_call | solution.py:701
  146.5 7.8 %collective-permute-done.24.rest_7_ = bf16[128,1152]{1,0:T(8,128)(2,1)S(1)} collective-permute-done((bf16[128,1152]{1,0:T(8,128)(2,1)S(1)}, bf16[128,1152]{1,0:T(8,128)(2,1)S(1)}, u32[]{:S(2)}, u32[]{:S(2)}) %collective-permute-start.24) | collective-permute-done | bytes 294944 | tf_op jit(solution)/shard_map/ppermute | solution.py:83
  155.1 16.6 %experts.2 = (bf16[1024,2048]{1,0:T(8,128)(2,1)}, bf16[1024,2048]{1,0:T(8,128)(2,1)}, bf16[1024,1152]{1,0:T(8,128)(2,1)}, bf16[4,64,1152]{2,1,0:T(8,128)(2,1)}, bf16[4,64,1152]{2,1,0:T(8,128)(2,1)}) custom-call(s32[4]{0:T(128)} %pad_add_fusion.idx, bf16[1024,2048]{1,0:T(8,128)(2,1)} %ahead.1.gh_ref, bf16[128,1152]{1,0:T(8,128)(2,1)} %get-tuple-element.152.rest_0_, ...), custom_call_target="tpu_custom_call" | custom-call | flops 12 | bytes 12 | tf_op jit(solution)/shard_map/experts/pallas_call | solution.py:701
  172.5 15.8 %experts.3 = (bf16[1024,2048]{1,0:T(8,128)(2,1)}, bf16[1024,2048]{1,0:T(8,128)(2,1)}, bf16[1024,1152]{1,0:T(8,128)(2,1)}, bf16[4,64,1152]{2,1,0:T(8,128)(2,1)}, bf16[4,64,1152]{2,1,0:T(8,128)(2,1)}) custom-call(s32[4]{0:T(128)} %pad_add_fusion.idx, bf16[1024,2048]{1,0:T(8,128)(2,1)} %ahead.1.gh_ref, ...), custom_call_target="tpu_custom_call", output_to_operand_aliasing={{0}: (14, {}), {1}: (15, {}), {2}: (16, {})} | custom-call | flops 12 | bytes 12 | tf_op jit(solution)/shard_map/experts/pallas_call | solution.py:701
  190.5 2.1 fold.2
  194.8 2.5 collective-permute-start.29
  197.2 9.9 %out.1 = bf16[8,128,1024]{2,1,0:T(8,128)(2,1)} custom-call(s32[4]{0:T(128)} %pad_add_fusion.idx, bf16[1024,2048]{1,0:T(8,128)(2,1)} %get-tuple-element.169.hg_ref, bf16[16,128,256]{2,1,0:T(8,128)(2,1)} %rest_0_.3, bf16[16,128,256]{2,1,0:T(8,128)(2,1)} %collective-permute-done.9.rest_1_, bf16[16,128,256]{2,1,0:T(8,128)(2,1)} %collective-permute-done.19.rest_2_, ...), custom_call_target="tpu_custom_call" | custom-call | flops 10 | bytes 10 | tf_op jit(solution)/shard_map/out/pallas_call | solution.py:701
  208.1 2.1 fold.3
  212.5 1.9 collective-permute-start.33
  214.5 9.9 %down_grad.1 = (bf16[2,16,128,256]{3,2,1,0:T(8,128)(2,1)}, bf16[2,16,128,256]{3,2,1,0:T(8,128)(2,1)}) custom-call(s32[4]{0:T(128)} %pad_add_fusion.idx, bf16[8,2,64,1024]{3,2,1,0:T(8,128)(2,1)} %bitcast.23, bf16[1024,2048]{1,0:T(8,128)(2,1)} %get-tuple-element.169.hg_ref), custom_call_target="tpu_custom_call" | custom-call | flops 4 | bytes 12 | tf_op jit(solution)/shard_map/down_grad/pallas_call | solution.py:1018
  224.4 9.7 %up_grad.1 = (bf16[2,16,256,128]{3,2,1,0:T(8,128)(2,1)}, bf16[2,16,256,128]{3,2,1,0:T(8,128)(2,1)}) custom-call(s32[4]{0:T(128)} %pad_add_fusion.idx, bf16[1024,1152]{1,0:T(8,128)(2,1)} %get-tuple-element.182.x_ref, bf16[1024,2048]{1,0:T(8,128)(2,1)} %get-tuple-element.183.pg_ref), custom_call_target="tpu_custom_call" | custom-call | flops 4 | bytes 12 | tf_op jit(solution)/shard_map/up_grad/pallas_call | solution.py:1018
  235.0 3.3 back_norm.1
  238.3 4.0 %all-to-all-start = ((bf16[8,128,1024]{2,1,0:T(8,128)(2,1)}), bf16[8,128,1024]{2,1,0:T(8,128)(2,1)S(1)}, u32[]{:S(2)}, u32[]{:S(2)}) async-start(bf16[8,128,1024]{2,1,0:T(8,128)(2,1)} %out.1), calls=%async_computation | async-start | bytes 4194304 | tf_op jit(solution)/shard_map/all_to_all | solution.py:1112
  245.0 8.9 %back_attend.1 = (bf16[128,1792]{1,0:T(8,128)(2,1)}, bf16[128,2560]{1,0:T(8,128)(2,1)}) custom-call(s32[4]{0:T(128)} %pad_add_fusion.idx, bf16[128,1024]{1,0:T(8,128)(2,1)} %get-tuple-element.194.bg_ref, bf16[128,128]{1,0:T(8,128)(2,1)} %get-tuple-element.197.rg_ref, f32[128,128]{1,0:T(8,128)} %get-tuple-element.140.sig_ref, ...), custom_call_target="tpu_custom_call" | custom-call | flops 8 | bytes 8 | tf_op jit(solution)/shard_map/back_attend/pallas_call | solution.py:701
  255.5 3.3 core_sum.2
  260.2 3.4 core_sum.3
  263.5 4.3 %grad_out.1 = (bf16[4,32,2560]{2,1,0:T(8,128)(2,1)}, bf16[4,32,2560]{2,1,0:T(8,128)(2,1)}) custom-call(s32[4]{0:T(128)} %pad_add_fusion.idx, f32[4,128,640]{2,1,0:T(8,128)} %bitcast.24, bf16[128,256]{1,0:T(8,128)(2,1)} %get-tuple-element.213.refs_0_, bf16[128,256]{1,0:T(8,128)(2,1)} %copy-done.33, bf16[128,256]{1,0:T(8,128)(2,1)} %copy-done.34, ...), custom_call_target="tpu_custom_call" | custom-call | flops 3 | bytes 3 | tf_op jit(solution)/shard_map/grad_out/pallas_call | solution.py:701
  268.4 1.9 collective-permute-start.42
  271.4 6.5 %grad_rest.1 = (bf16[4,32,3840]{2,1,0:T(8,128)(2,1)}, bf16[4,32,3840]{2,1,0:T(8,128)(2,1)}) custom-call(s32[4]{0:T(128)} %pad_add_fusion.idx, bf16[4,128,3072]{2,1,0:T(8,128)(2,1)} %bitcast.26, f32[4,128,640]{2,1,0:T(8,128)} %bitcast.25, bf16[256,1280]{1,0:T(8,128)(2,1)} %get-tuple-element.219.a_ref, bf16[128,1792]{1,0:T(8,128)(2,1)} %get-tuple-element.233.refs_0_.late_ref, ...), custom_call_target="tpu_custom_call" | custom-call | flops 3 | bytes 3 | tf_op jit(solution)/shard_map/grad_rest/pallas_call | solution.py:701
  281.2 8.6 %collective-permute-done.42.refs_0_ = bf16[4,32,2560]{2,1,0:T(8,128)(2,1)S(1)} collective-permute-done((bf16[4,32,2560]{2,1,0:T(8,128)(2,1)}, bf16[4,32,2560]{2,1,0:T(8,128)(2,1)S(1)}, u32[]{:S(2)}, u32[]{:S(2)}) %collective-permute-start.42) | collective-permute-done | bytes 655392 | tf_op jit(solution)/shard_map/ppermute | solution.py:83
  290.7 2.2 fold_at.2
  292.9 3.7 %collective-permute-start.43 = (bf16[32,2560]{1,0:T(8,128)(2,1)}, bf16[32,2560]{1,0:T(8,128)(2,1)S(1)}, u32[]{:S(2)}, u32[]{:S(2)}) collective-permute-start(bf16[32,2560]{1,0:T(8,128)(2,1)} %get-tuple-element.227), channel_id=1, source_target_pairs={{0,2},{1,3},{2,4},{3,5},{4,6},{5,7},{6,0},{7,1},{8,10},{9,11},{10,... | collective-permute-start | bytes 491528 | tf_op jit(solution)/shard_map/ppermute | solution.py:83
  298.4 4.7 %collective-permute-done.43.refs_1_ = bf16[32,2560]{1,0:T(8,128)(2,1)S(1)} collective-permute-done((bf16[32,2560]{1,0:T(8,128)(2,1)}, bf16[32,2560]{1,0:T(8,128)(2,1)S(1)}, u32[]{:S(2)}, u32[]{:S(2)}) %collective-permute-start.43) | collective-permute-done | bytes 163872 | tf_op jit(solution)/shard_map/ppermute | solution.py:83
  304.6 3.8 %collective-permute-done.44.refs_2_ = bf16[32,2560]{1,0:T(8,128)(2,1)S(1)} collective-permute-done((bf16[32,2560]{1,0:T(8,128)(2,1)}, bf16[32,2560]{1,0:T(8,128)(2,1)S(1)}, u32[]{:S(2)}, u32[]{:S(2)}) %collective-permute-start.44) | collective-permute-done | bytes 163872 | tf_op jit(solution)/shard_map/ppermute | solution.py:83
  308.4 4.8 %collective-permute-done.45.refs_3_ = bf16[32,2560]{1,0:T(8,128)(2,1)} collective-permute-done((bf16[32,2560]{1,0:T(8,128)(2,1)}, bf16[32,2560]{1,0:T(8,128)(2,1)}, u32[]{:S(2)}, u32[]{:S(2)}) %collective-permute-start.45) | collective-permute-done | bytes 163872 | tf_op jit(solution)/shard_map/ppermute | solution.py:83
  313.2 3.4 fold_at.3
  316.6 2.3 collective-permute-start.49
  320.4 3.2 collective-permute-start.51
  323.5 8.3 %back_token.1 = f32[128,1024]{1,0:T(8,128)} custom-call(s32[4]{0:T(128)} %pad_add_fusion.idx, bf16[128,1024]{1,0:T(8,128)(2,1)} %bitcast.29, f32[128,1024]{1,0:T(8,128)} %get-tuple-element.196.rg_ref, bf16[128,1792]{1,0:T(8,128)(2,1)} %get-tuple-element.233.refs_0_.late_ref, bf16[128,2560]{1,0:T(8,128)(2,1)} %get-tuple-element.234.vag_ref, ...), custom_call_target="tpu_custom_call" | custom-call | flops 8 | bytes 8 | tf_op jit(solution)/shard_map/back_token/pallas_call | solution.py:701
  331.9 2.7 add_out.1
  334.7 2.0 sum.1
  336.6 2.6 last_sum.2
  340.2 2.6 last_sum.3
  344.4 2.2 finish.1
  (189 shorter events, 54.0 us)
Async XLA Ops:
  7.2 63.9 %all-gather.6.cloned.1.call-start = ((), (), s32[]{:S(2)}) async-start(), calls=%async_computation.1 | async-start | bytes 2359296 | tf_op jit(solution)/shard_map/all_gather | solution.py:806
  12.5 16.7 %collective-permute-start = (bf16[256,6400]{1,0:T(8,128)(2,1)}, bf16[256,6400]{1,0:T(8,128)(2,1)S(1)}, u32[]{:S(2)}, u32[]{:S(2)}) collective-permute-start(bf16[256,6400]{1,0:T(8,128)(2,1)} %get-tuple-element.133.rest_0_.rest_10_), channel_id=1, source_target_pairs={{0,8},{8,0},{16,24},{24,16},{1,9},{9,1},{17,25},{25,17},{2,10},{10... | collective-permute-start | bytes 9830408 | tf_op jit(solution)/shard_map/ppermute | solution.py:75
  12.9 221.2 %all-gather.8.cloned.1.call-start = ((), (), s32[]{:S(2)}) async-start(), calls=%async_computation.2 | async-start | bytes 1638400 | tf_op jit(solution)/shard_map/all_gather | solution.py:1079
  13.0 16.2 %collective-permute-start.1 = (bf16[128,2176]{1,0:T(8,128)(2,1)}, bf16[128,2176]{1,0:T(8,128)(2,1)}, u32[]{:S(2)}, u32[]{:S(2)}) collective-permute-start(bf16[128,2176]{1,0:T(8,128)(2,1)} %get-tuple-element.134), channel_id=1, source_target_pairs={{0,16},{8,24},{16,0},{24,8},{1,17},{9,25},{17,1},{25,9},{2,18},{10... | collective-permute-start | bytes 1671176 | tf_op jit(solution)/shard_map/ppermute | solution.py:75
  29.2 16.5 %collective-permute-start.3 = (bf16[128,2176]{1,0:T(8,128)(2,1)}, bf16[128,2176]{1,0:T(8,128)(2,1)}, u32[]{:S(2)}, u32[]{:S(2)}) collective-permute-start(bf16[128,2176]{1,0:T(8,128)(2,1)} %collective-permute-done.1.rest_2_), channel_id=1, source_target_pairs={{0,1},{1,0},{2,3},{3,2},{4,5},{5,4},{6,7},{7,6},{8,9},{9,8},{10,11... | collective-permute-start | bytes 1671176 | tf_op jit(solution)/shard_map/ppermute | solution.py:83
  31.0 15.0 %collective-permute-start.4 = (bf16[128,2176]{1,0:T(8,128)(2,1)}, bf16[128,2176]{1,0:T(8,128)(2,1)}, u32[]{:S(2)}, u32[]{:S(2)}) collective-permute-start(bf16[128,2176]{1,0:T(8,128)(2,1)} %get-tuple-element.137), channel_id=1, source_target_pairs={{0,16},{8,24},{16,0},{24,8},{1,17},{9,25},{17,1},{25,9},{2,18},{10... | collective-permute-start | bytes 1671176 | tf_op jit(solution)/shard_map/ppermute | solution.py:75
  46.0 25.1 %collective-permute-start.9 = (bf16[16,128,256]{2,1,0:T(8,128)(2,1)}, bf16[16,128,256]{2,1,0:T(8,128)(2,1)}, u32[]{:S(2)}, u32[]{:S(2)}) collective-permute-start(bf16[16,128,256]{2,1,0:T(8,128)(2,1)} %rest_0_.3), channel_id=1, source_target_pairs={{0,8},{8,0},{16,24},{24,16},{1,9},{9,1},{17,25},{25,17},{2,10},{10... | collective-permute-start | bytes 3145736 | tf_op jit(solution)/shard_map/ppermute | solution.py:75
  46.0 25.1 %collective-permute-start.5 = (bf16[128,2176]{1,0:T(8,128)(2,1)}, bf16[128,2176]{1,0:T(8,128)(2,1)}, u32[]{:S(2)}, u32[]{:S(2)}) collective-permute-start(bf16[128,2176]{1,0:T(8,128)(2,1)} %collective-permute-done.3.rest_4_), channel_id=1, source_target_pairs={{0,8},{8,0},{16,24},{24,16},{1,9},{9,1},{17,25},{25,17},{2,10},{10... | collective-permute-start | bytes 1671176 | tf_op jit(solution)/shard_map/ppermute | solution.py:75
  46.5 24.6 %collective-permute-start.6 = (bf16[128,2176]{1,0:T(8,128)(2,1)}, bf16[128,2176]{1,0:T(8,128)(2,1)}, u32[]{:S(2)}, u32[]{:S(2)}) collective-permute-start(bf16[128,2176]{1,0:T(8,128)(2,1)} %collective-permute-done.4.rest_6_.rest_12_.rest_2_), channel_id=1, source_target_pairs={{0,8},{8,0},{16,24},{24,16},{1,9},{9,1},{17,25},{25,17},{2,10},{10... | collective-permute-start | bytes 1671176 | tf_op jit(solution)/shard_map/ppermute | solution.py:75
  46.5 24.6 %collective-permute-start.7 = (bf16[128,2176]{1,0:T(8,128)(2,1)}, bf16[128,2176]{1,0:T(8,128)(2,1)}, u32[]{:S(2)}, u32[]{:S(2)}) collective-permute-start(bf16[128,2176]{1,0:T(8,128)(2,1)} %collective-permute-done.4.rest_6_.rest_12_.rest_2_), channel_id=1, source_target_pairs={{0,1},{1,0},{2,3},{3,2},{4,5},{5,4},{6,7},{7,6},{8,9},{9,8},{10,11... | collective-permute-start | bytes 1671176 | tf_op jit(solution)/shard_map/ppermute | solution.py:83
  48.7 22.3 %collective-permute-start.8 = (bf16[128,2048]{1,0:T(8,128)(2,1)}, bf16[128,2048]{1,0:T(8,128)(2,1)}, u32[]{:S(2)}, u32[]{:S(2)}) collective-permute-start(bf16[128,2048]{1,0:T(8,128)(2,1)} %get-tuple-element.146), channel_id=1, source_target_pairs={{0,16},{8,24},{16,0},{24,8},{1,17},{9,25},{17,1},{25,9},{2,18},{10... | collective-permute-start | bytes 1572872 | tf_op jit(solution)/shard_map/ppermute | solution.py:75
  71.1 15.3 %collective-permute-start.13 = (bf16[16,256,128]{2,1,0:T(8,128)(2,1)}, bf16[16,256,128]{2,1,0:T(8,128)(2,1)}, u32[]{:S(2)}, u32[]{:S(2)}) collective-permute-start(bf16[16,256,128]{2,1,0:T(8,128)(2,1)} %rest_8_.3), channel_id=1, source_target_pairs={{0,8},{8,0},{16,24},{24,16},{1,9},{9,1},{17,25},{25,17},{2,10},{10... | collective-permute-start | bytes 3145736 | tf_op jit(solution)/shard_map/ppermute | solution.py:75
  71.2 15.2 %collective-permute-start.10 = (bf16[128,2176]{1,0:T(8,128)(2,1)}, bf16[128,2176]{1,0:T(8,128)(2,1)}, u32[]{:S(2)}, u32[]{:S(2)}) collective-permute-start(bf16[128,2176]{1,0:T(8,128)(2,1)} %collective-permute-done.7.rest_8_.rest_14_.rest_4_), channel_id=1, source_target_pairs={{0,8},{8,0},{16,24},{24,16},{1,9},{9,1},{17,25},{25,17},{2,10},{10... | collective-permute-start | bytes 1671176 | tf_op jit(solution)/shard_map/ppermute | solution.py:75
  71.8 14.6 %collective-permute-start.12 = (bf16[128,2048]{1,0:T(8,128)(2,1)}, bf16[128,2048]{1,0:T(8,128)(2,1)}, u32[]{:S(2)}, u32[]{:S(2)}) collective-permute-start(bf16[128,2048]{1,0:T(8,128)(2,1)} %collective-permute-done.8.rest_16_.rest_6_.rest_10_), channel_id=1, source_target_pairs={{0,1},{1,0},{2,3},{3,2},{4,5},{5,4},{6,7},{7,6},{8,9},{9,8},{10,11... | collective-permute-start | bytes 1572872 | tf_op jit(solution)/shard_map/ppermute | solution.py:83
  72.9 29.7 %collective-permute-start.19 = (bf16[16,128,256]{2,1,0:T(8,128)(2,1)}, bf16[16,128,256]{2,1,0:T(8,128)(2,1)}, u32[]{:S(2)}, u32[]{:S(2)}) collective-permute-start(bf16[16,128,256]{2,1,0:T(8,128)(2,1)} %rest_0_.3), channel_id=1, source_target_pairs={{0,16},{8,24},{16,0},{24,8},{1,17},{9,25},{17,1},{25,9},{2,18},{10... | collective-permute-start | bytes 3145736 | tf_op jit(solution)/shard_map/ppermute | solution.py:75
  102.7 25.6 %collective-permute-start.20 = (bf16[16,256,128]{2,1,0:T(8,128)(2,1)S(1)}, bf16[16,256,128]{2,1,0:T(8,128)(2,1)S(1)}, u32[]{:S(2)}, u32[]{:S(2)}) collective-permute-start(bf16[16,256,128]{2,1,0:T(8,128)(2,1)S(1)} %copy-done.2), channel_id=1, source_target_pairs={{0,16},{8,24},{16,0},{24,8},{1,17},{9,25},{17,1},{25,9},{2,18},{10... | collective-permute-start | bytes 3145736 | tf_op jit(solution)/shard_map/ppermute | solution.py:75
  104.2 11.1 %collective-permute-start.15 = (bf16[128,1152]{1,0:T(8,128)(2,1)}, bf16[128,1152]{1,0:T(8,128)(2,1)S(1)}, u32[]{:S(2)}, u32[]{:S(2)}) collective-permute-start(bf16[128,1152]{1,0:T(8,128)(2,1)} %get-tuple-element.152.rest_0_), channel_id=1, source_target_pairs={{0,2},{1,3},{2,4},{3,5},{4,6},{5,7},{6,0},{7,1},{8,10},{9,11},{10,... | collective-permute-start | bytes 884744 | tf_op jit(solution)/shard_map/ppermute | solution.py:83
  105.9 9.5 %collective-permute-start.16 = (bf16[128,1152]{1,0:T(8,128)(2,1)}, bf16[128,1152]{1,0:T(8,128)(2,1)S(1)}, u32[]{:S(2)}, u32[]{:S(2)}) collective-permute-start(bf16[128,1152]{1,0:T(8,128)(2,1)} %get-tuple-element.152.rest_0_), channel_id=1, source_target_pairs={{0,1},{1,0},{2,3},{3,2},{4,5},{5,4},{6,7},{7,6},{8,9},{9,8},{10,11... | collective-permute-start | bytes 884744 | tf_op jit(solution)/shard_map/ppermute | solution.py:83
  115.3 10.2 %collective-permute-start.17 = (bf16[128,1152]{1,0:T(8,128)(2,1)S(1)}, bf16[128,1152]{1,0:T(8,128)(2,1)S(1)}, u32[]{:S(2)}, u32[]{:S(2)}) collective-permute-start(bf16[128,1152]{1,0:T(8,128)(2,1)S(1)} %collective-permute-done.15.rest_1_), channel_id=1, source_target_pairs={{0,2},{1,3},{2,4},{3,5},{4,6},{5,7},{6,0},{7,1},{8,10},{9,11},{10,... | collective-permute-start | bytes 884744 | tf_op jit(solution)/shard_map/ppermute | solution.py:83
  115.8 9.7 %collective-permute-start.18 = (bf16[128,1152]{1,0:T(8,128)(2,1)S(1)}, bf16[128,1152]{1,0:T(8,128)(2,1)S(1)}, u32[]{:S(2)}, u32[]{:S(2)}) collective-permute-start(bf16[128,1152]{1,0:T(8,128)(2,1)S(1)} %collective-permute-done.15.rest_1_), channel_id=1, source_target_pairs={{0,1},{1,0},{2,3},{3,2},{4,5},{5,4},{6,7},{7,6},{8,9},{9,8},{10,11... | collective-permute-start | bytes 884744 | tf_op jit(solution)/shard_map/ppermute | solution.py:83
  131.0 103.2 %all-gather.10.cloned.1.call-start = ((), (), s32[]{:S(2)}) async-start(), calls=%async_computation.3 | async-start | bytes 3932160 | tf_op jit(solution)/shard_map/all_gather | solution.py:1080
  131.9 13.5 %collective-permute-start.22 = (bf16[128,1152]{1,0:T(8,128)(2,1)S(1)}, bf16[128,1152]{1,0:T(8,128)(2,1)S(1)}, u32[]{:S(2)}, u32[]{:S(2)}) collective-permute-start(bf16[128,1152]{1,0:T(8,128)(2,1)S(1)} %collective-permute-done.17.rest_2_), channel_id=1, source_target_pairs={{0,2},{1,3},{2,4},{3,5},{4,6},{5,7},{6,0},{7,1},{8,10},{9,11},{10,... | collective-permute-start | bytes 884744 | tf_op jit(solution)/shard_map/ppermute | solution.py:83
  134.1 11.3 %collective-permute-start.23 = (bf16[128,1152]{1,0:T(8,128)(2,1)S(1)}, bf16[128,1152]{1,0:T(8,128)(2,1)S(1)}, u32[]{:S(2)}, u32[]{:S(2)}) collective-permute-start(bf16[128,1152]{1,0:T(8,128)(2,1)S(1)} %collective-permute-done.17.rest_2_), channel_id=1, source_target_pairs={{0,1},{1,0},{2,3},{3,2},{4,5},{5,4},{6,7},{7,6},{8,9},{9,8},{10,11... | collective-permute-start | bytes 884744 | tf_op jit(solution)/shard_map/ppermute | solution.py:83
  171.6 18.0 %collective-permute-start.26 = (bf16[4,64,1152]{2,1,0:T(8,128)(2,1)}, bf16[4,64,1152]{2,1,0:T(8,128)(2,1)S(1)}, u32[]{:S(2)}, u32[]{:S(2)}) collective-permute-start(bf16[4,64,1152]{2,1,0:T(8,128)(2,1)} %get-tuple-element.167), channel_id=1, source_target_pairs={{0,1},{1,0},{2,3},{3,2},{4,5},{5,4},{6,7},{7,6},{8,9},{9,8},{10,11... | collective-permute-start | bytes 1769480 | tf_op jit(solution)/shard_map/ppermute | solution.py:83
  188.4 18.9 %collective-permute-start.30 = (bf16[4,64,1152]{2,1,0:T(8,128)(2,1)}, bf16[4,64,1152]{2,1,0:T(8,128)(2,1)S(1)}, u32[]{:S(2)}, u32[]{:S(2)}) collective-permute-start(bf16[4,64,1152]{2,1,0:T(8,128)(2,1)} %get-tuple-element.178), channel_id=1, source_target_pairs={{0,1},{1,0},{2,3},{3,2},{4,5},{5,4},{6,7},{7,6},{8,9},{9,8},{10,11... | collective-permute-start | bytes 1769480 | tf_op jit(solution)/shard_map/ppermute | solution.py:83
  192.5 14.6 %collective-permute-start.27 = (bf16[64,1152]{1,0:T(8,128)(2,1)}, bf16[64,1152]{1,0:T(8,128)(2,1)S(1)}, u32[]{:S(2)}, u32[]{:S(2)}) collective-permute-start(bf16[64,1152]{1,0:T(8,128)(2,1)} %get-tuple-element.174), channel_id=1, source_target_pairs={{0,2},{1,3},{2,4},{3,5},{4,6},{5,7},{6,0},{7,1},{8,10},{9,11},{10,... | collective-permute-start | bytes 442376 | tf_op jit(solution)/shard_map/ppermute | solution.py:83
  193.9 13.3 %collective-permute-start.28 = (bf16[64,1152]{1,0:T(8,128)(2,1)}, bf16[64,1152]{1,0:T(8,128)(2,1)S(1)}, u32[]{:S(2)}, u32[]{:S(2)}) collective-permute-start(bf16[64,1152]{1,0:T(8,128)(2,1)} %get-tuple-element.175), channel_id=1, source_target_pairs={{0,4},{1,5},{2,6},{3,7},{4,0},{5,1},{6,2},{7,3},{8,12},{9,13},{10,... | collective-permute-start | bytes 442376 | tf_op jit(solution)/shard_map/ppermute | solution.py:83
  194.8 12.4 %collective-permute-start.29 = (bf16[64,1152]{1,0:T(8,128)(2,1)}, bf16[64,1152]{1,0:T(8,128)(2,1)S(1)}, u32[]{:S(2)}, u32[]{:S(2)}) collective-permute-start(bf16[64,1152]{1,0:T(8,128)(2,1)} %get-tuple-element.176), channel_id=1, source_target_pairs={{0,6},{1,7},{2,0},{3,1},{4,2},{5,3},{6,4},{7,5},{8,14},{9,15},{10,... | collective-permute-start | bytes 442376 | tf_op jit(solution)/shard_map/ppermute | solution.py:83
  210.2 23.9 %collective-permute-start.31 = (bf16[64,1152]{1,0:T(8,128)(2,1)}, bf16[64,1152]{1,0:T(8,128)(2,1)S(1)}, u32[]{:S(2)}, u32[]{:S(2)}) collective-permute-start(bf16[64,1152]{1,0:T(8,128)(2,1)} %get-tuple-element.191), channel_id=1, source_target_pairs={{0,2},{1,3},{2,4},{3,5},{4,6},{5,7},{6,0},{7,1},{8,10},{9,11},{10,... | collective-permute-start | bytes 442376 | tf_op jit(solution)/shard_map/ppermute | solution.py:83
  211.5 22.7 %collective-permute-start.32 = (bf16[64,1152]{1,0:T(8,128)(2,1)}, bf16[64,1152]{1,0:T(8,128)(2,1)S(1)}, u32[]{:S(2)}, u32[]{:S(2)}) collective-permute-start(bf16[64,1152]{1,0:T(8,128)(2,1)} %get-tuple-element.192), channel_id=1, source_target_pairs={{0,4},{1,5},{2,6},{3,7},{4,0},{5,1},{6,2},{7,3},{8,12},{9,13},{10,... | collective-permute-start | bytes 442376 | tf_op jit(solution)/shard_map/ppermute | solution.py:83
  212.5 21.7 %collective-permute-start.33 = (bf16[64,1152]{1,0:T(8,128)(2,1)}, bf16[64,1152]{1,0:T(8,128)(2,1)S(1)}, u32[]{:S(2)}, u32[]{:S(2)}) collective-permute-start(bf16[64,1152]{1,0:T(8,128)(2,1)} %get-tuple-element.193), channel_id=1, source_target_pairs={{0,6},{1,7},{2,0},{3,1},{4,2},{5,3},{6,4},{7,5},{8,14},{9,15},{10,... | collective-permute-start | bytes 442376 | tf_op jit(solution)/shard_map/ppermute | solution.py:83
  238.3 74.9 %all-to-all-start = ((bf16[8,128,1024]{2,1,0:T(8,128)(2,1)}), bf16[8,128,1024]{2,1,0:T(8,128)(2,1)S(1)}, u32[]{:S(2)}, u32[]{:S(2)}) async-start(bf16[8,128,1024]{2,1,0:T(8,128)(2,1)} %out.1), calls=%async_computation | async-start | bytes 4194304 | tf_op jit(solution)/shard_map/all_to_all | solution.py:1112
  242.3 13.2 %collective-permute-start.34 = (bf16[2,16,128,256]{3,2,1,0:T(8,128)(2,1)}, bf16[2,16,128,256]{3,2,1,0:T(8,128)(2,1)}, u32[]{:S(2)}, u32[]{:S(2)}) collective-permute-start(bf16[2,16,128,256]{3,2,1,0:T(8,128)(2,1)} %get-tuple-element.204), channel_id=1, source_target_pairs={{0,8},{8,0},{16,24},{24,16},{1,9},{9,1},{17,25},{25,17},{2,10},{10... | collective-permute-start | bytes 6291464 | tf_op jit(solution)/shard_map/ppermute | solution.py:75
  242.4 16.5 %collective-permute-start.35 = (bf16[2,16,256,128]{3,2,1,0:T(8,128)(2,1)}, bf16[2,16,256,128]{3,2,1,0:T(8,128)(2,1)S(1)}, u32[]{:S(2)}, u32[]{:S(2)}) collective-permute-start(bf16[2,16,256,128]{3,2,1,0:T(8,128)(2,1)} %get-tuple-element.209), channel_id=1, source_target_pairs={{0,8},{8,0},{16,24},{24,16},{1,9},{9,1},{17,25},{25,17},{2,10},{10... | collective-permute-start | bytes 6291464 | tf_op jit(solution)/shard_map/ppermute | solution.py:75
  242.9 11.1 %collective-permute-start.36 = (bf16[128,256]{1,0:T(8,128)(2,1)S(1)}, bf16[128,256]{1,0:T(8,128)(2,1)S(1)}, u32[]{:S(2)}, u32[]{:S(2)}) collective-permute-start(bf16[128,256]{1,0:T(8,128)(2,1)S(1)} %copy-done.42), channel_id=1, source_target_pairs={{0,16},{8,24},{16,0},{24,8},{1,17},{9,25},{17,1},{25,9},{2,18},{10... | collective-permute-start | bytes 196616 | tf_op jit(solution)/shard_map/ppermute | solution.py:75
  244.3 9.7 %collective-permute-start.37 = (bf16[128,256]{1,0:T(8,128)(2,1)S(1)}, bf16[128,256]{1,0:T(8,128)(2,1)S(1)}, u32[]{:S(2)}, u32[]{:S(2)}) collective-permute-start(bf16[128,256]{1,0:T(8,128)(2,1)S(1)} %copy-done.41), channel_id=1, source_target_pairs={{0,8},{8,0},{16,24},{24,16},{1,9},{9,1},{17,25},{25,17},{2,10},{10... | collective-permute-start | bytes 196616 | tf_op jit(solution)/shard_map/ppermute | solution.py:75
  244.3 9.7 %collective-permute-start.38 = (bf16[128,256]{1,0:T(8,128)(2,1)S(1)}, bf16[128,256]{1,0:T(8,128)(2,1)S(1)}, u32[]{:S(2)}, u32[]{:S(2)}) collective-permute-start(bf16[128,256]{1,0:T(8,128)(2,1)S(1)} %copy-done.40), channel_id=1, source_target_pairs={{0,24},{8,16},{16,8},{24,0},{1,25},{9,17},{17,9},{25,1},{2,26},{10... | collective-permute-start | bytes 196616 | tf_op jit(solution)/shard_map/ppermute | solution.py:75
  254.0 13.8 %collective-permute-start.39 = (bf16[128,1792]{1,0:T(8,128)(2,1)}, bf16[128,1792]{1,0:T(8,128)(2,1)S(1)}, u32[]{:S(2)}, u32[]{:S(2)}) collective-permute-start(bf16[128,1792]{1,0:T(8,128)(2,1)} %get-tuple-element.233.refs_0_.late_ref), channel_id=1, source_target_pairs={{0,16},{8,24},{16,0},{24,8},{1,17},{9,25},{17,1},{25,9},{2,18},{10... | collective-permute-start | bytes 1376264 | tf_op jit(solution)/shard_map/ppermute | solution.py:75
  268.4 21.4 %collective-permute-start.42 = (bf16[4,32,2560]{2,1,0:T(8,128)(2,1)}, bf16[4,32,2560]{2,1,0:T(8,128)(2,1)S(1)}, u32[]{:S(2)}, u32[]{:S(2)}) collective-permute-start(bf16[4,32,2560]{2,1,0:T(8,128)(2,1)} %get-tuple-element.225), channel_id=1, source_target_pairs={{0,1},{1,0},{2,3},{3,2},{4,5},{5,4},{6,7},{7,6},{8,9},{9,8},{10,11... | collective-permute-start | bytes 1966088 | tf_op jit(solution)/shard_map/ppermute | solution.py:83
  277.9 35.3 %collective-permute-start.46 = (bf16[4,32,3840]{2,1,0:T(8,128)(2,1)}, bf16[4,32,3840]{2,1,0:T(8,128)(2,1)}, u32[]{:S(2)}, u32[]{:S(2)}) collective-permute-start(bf16[4,32,3840]{2,1,0:T(8,128)(2,1)} %get-tuple-element.231), channel_id=1, source_target_pairs={{0,1},{1,0},{2,3},{3,2},{4,5},{5,4},{6,7},{7,6},{8,9},{9,8},{10,11... | collective-permute-start | bytes 2949128 | tf_op jit(solution)/shard_map/ppermute | solution.py:83
  279.2 57.4 %collective-permute-start.47 = (bf16[16,128,256]{2,1,0:T(8,128)(2,1)}, bf16[16,128,256]{2,1,0:T(8,128)(2,1)}, u32[]{:S(2)}, u32[]{:S(2)}) collective-permute-start(bf16[16,128,256]{2,1,0:T(8,128)(2,1)} %get-tuple-element.238), channel_id=1, source_target_pairs={{0,16},{8,24},{16,0},{24,8},{1,17},{9,25},{17,1},{25,9},{2,18},{10... | collective-permute-start | bytes 3145736 | tf_op jit(solution)/shard_map/ppermute | solution.py:75
  279.8 59.4 %collective-permute-start.48 = (bf16[16,256,128]{2,1,0:T(8,128)(2,1)}, bf16[16,256,128]{2,1,0:T(8,128)(2,1)S(1)}, u32[]{:S(2)}, u32[]{:S(2)}) collective-permute-start(bf16[16,256,128]{2,1,0:T(8,128)(2,1)} %get-tuple-element.240), channel_id=1, source_target_pairs={{0,16},{8,24},{16,0},{24,8},{1,17},{9,25},{17,1},{25,9},{2,18},{10... | collective-permute-start | bytes 3145736 | tf_op jit(solution)/shard_map/ppermute | solution.py:75
  292.9 10.1 %collective-permute-start.43 = (bf16[32,2560]{1,0:T(8,128)(2,1)}, bf16[32,2560]{1,0:T(8,128)(2,1)S(1)}, u32[]{:S(2)}, u32[]{:S(2)}) collective-permute-start(bf16[32,2560]{1,0:T(8,128)(2,1)} %get-tuple-element.227), channel_id=1, source_target_pairs={{0,2},{1,3},{2,4},{3,5},{4,6},{5,7},{6,0},{7,1},{8,10},{9,11},{10,... | collective-permute-start | bytes 491528 | tf_op jit(solution)/shard_map/ppermute | solution.py:83
  296.6 11.9 %collective-permute-start.44 = (bf16[32,2560]{1,0:T(8,128)(2,1)}, bf16[32,2560]{1,0:T(8,128)(2,1)S(1)}, u32[]{:S(2)}, u32[]{:S(2)}) collective-permute-start(bf16[32,2560]{1,0:T(8,128)(2,1)} %get-tuple-element.228), channel_id=1, source_target_pairs={{0,4},{1,5},{2,6},{3,7},{4,0},{5,1},{6,2},{7,3},{8,12},{9,13},{10,... | collective-permute-start | bytes 491528 | tf_op jit(solution)/shard_map/ppermute | solution.py:83
  303.0 10.2 %collective-permute-start.45 = (bf16[32,2560]{1,0:T(8,128)(2,1)}, bf16[32,2560]{1,0:T(8,128)(2,1)}, u32[]{:S(2)}, u32[]{:S(2)}) collective-permute-start(bf16[32,2560]{1,0:T(8,128)(2,1)} %get-tuple-element.229), channel_id=1, source_target_pairs={{0,6},{1,7},{2,0},{3,1},{4,2},{5,3},{6,4},{7,5},{8,14},{9,15},{10,... | collective-permute-start | bytes 491528 | tf_op jit(solution)/shard_map/ppermute | solution.py:83
  316.6 26.3 %collective-permute-start.49 = (bf16[32,3840]{1,0:T(8,128)(2,1)}, bf16[32,3840]{1,0:T(8,128)(2,1)S(1)}, u32[]{:S(2)}, u32[]{:S(2)}) collective-permute-start(bf16[32,3840]{1,0:T(8,128)(2,1)} %get-tuple-element.242), channel_id=1, source_target_pairs={{0,2},{1,3},{2,4},{3,5},{4,6},{5,7},{6,0},{7,1},{8,10},{9,11},{10,... | collective-permute-start | bytes 737288 | tf_op jit(solution)/shard_map/ppermute | solution.py:83
  318.9 23.9 %collective-permute-start.50 = (bf16[32,3840]{1,0:T(8,128)(2,1)}, bf16[32,3840]{1,0:T(8,128)(2,1)S(1)}, u32[]{:S(2)}, u32[]{:S(2)}) collective-permute-start(bf16[32,3840]{1,0:T(8,128)(2,1)} %get-tuple-element.243), channel_id=1, source_target_pairs={{0,4},{1,5},{2,6},{3,7},{4,0},{5,1},{6,2},{7,3},{8,12},{9,13},{10,... | collective-permute-start | bytes 737288 | tf_op jit(solution)/shard_map/ppermute | solution.py:83
  320.4 22.5 %collective-permute-start.51 = (bf16[32,3840]{1,0:T(8,128)(2,1)}, bf16[32,3840]{1,0:T(8,128)(2,1)S(1)}, u32[]{:S(2)}, u32[]{:S(2)}) collective-permute-start(bf16[32,3840]{1,0:T(8,128)(2,1)} %get-tuple-element.244), channel_id=1, source_target_pairs={{0,6},{1,7},{2,0},{3,1},{4,2},{5,3},{6,4},{7,5},{8,14},{9,15},{10,... | collective-permute-start | bytes 737288 | tf_op jit(solution)/shard_map/ppermute | solution.py:83
  (51 other events, 533.9 us)
Sparse Core Ops, SparseCore 0:
  13.1 57.9 all-gather.5
  131.1 17.4 all-gather.7
  150.1 28.5 all-gather.9

commit v3 on v2

--- a/solution.py
+++ b/solution.py
@@ -821,9 +821,8 @@
         else:
             d_y = to_y(down_weight, *done)
             swap_u = swap(up_weight, *done)
-            new.append(swap_u)
+            new += [swap_u, g_gathered]
         if i == len(STARTS) - 2:
-            new.append(g_gathered)
             swap_d = swap(down_weight, *done)
             new.append(swap_d)
         over_x_too.append(spread_x(over_y[i], *done))
@@ -833,9 +832,6 @@
             swap_x.append([swap_all(by_j[1:], *done) for by_j in over_x_too[i - 1]])
             new += flat(swap_x[-1])
         done = new
-    swap_x.append([swap_all(by_j[1:], *done) for by_j in over_x_too[-1]])
-    done = flat(swap_x[-1])
-
     def weight_pieces(own, swapped, chunks):
         arrays, tags = [own, swapped], [(0, 0, None, 0, 0), (0, 1, None, 0, 0)]
         for column, got, others in chunks:
@@ -846,12 +842,13 @@
                     tags += [(k, 0, split, j, column), (k, 1, split, j, column)]
         return arrays, tags
 
-    chunks = [
-        (low, got, [[v] + more for v, more in zip(ys, xs)])
-        for low, got, ys, xs in zip(STARTS, over_x_too, swap_y, swap_x)
-    ]
-    first_pieces, first_tags = weight_pieces(block_w, swap_w, chunks[:1])
-    a_pieces, a_tags = weight_pieces(block_w, swap_w, chunks)
+    def all_chunks():
+        return [
+            (low, got, [[v] + more for v, more in zip(ys, xs)])
+            for low, got, ys, xs in zip(STARTS, over_x_too, swap_y, swap_x)
+        ]
+
+    first_pieces, first_tags = weight_pieces(block_w, swap_w, all_chunks()[:1])
 
     n1, qk, sig, mask, probs, wmr = call(
         "attend",
@@ -876,6 +873,8 @@
         [pltpu.VMEM((width, COL_VALUES), BF), dma(len(first_pieces))],
         us=4,
     )
+    swap_x.append([swap_all(by_j[1:], n1, *done) for by_j in over_x_too[-1]])
+    a_pieces, a_tags = weight_pieces(block_w, swap_w, all_chunks())
     v_pieces, v_tags = window(a_pieces, a_tags, COL_VALUES, COL_OUT)
     o_pieces, o_tags = window(a_pieces, a_tags, COL_OUT, COL_A)
     vals, va, early, res, router, picked, xg, cols = call(

time: 360 us -> 354 us (0.983)
  waiting for transfers between devices: 110 us -> 101 us
    all_gather x1, waiting for transfers between devices: 21 us -> 0.02 us  [per_device(): g_gathered = lax.all_gather(g_all, 'expert', axis=0, tiled=True)]
    ppermute x26, waiting for transfers between devices: 18 us -> 31.5 us  [_dp(): return lax.ppermute(v, 'dp', pairs)]
    unnamed x90 -> x104, local copies, waits for them, and re-layouts: 11.1 us -> 12.5 us
  transfers between devices with their start and end apart: 56 -> 56, of which waited for: 15 -> 16; matrix products, arithmetic and copies ran while one was open for 1% -> 1% of each run, Pallas kernels for 40% -> 40%
where the time goes in v3:
time: 354 us; the launch traced here: 348 us
  Pallas kernels  150 us (42%)
  waiting for transfers between devices  101 us (29%)
  starting transfers between devices  66.2 us (19%)
  local copies, waits for them, and re-layouts  14.7 us (4%)
  between operations  14.7 us (4%)
    pallas_call x19, Pallas kernels, call(): pl.pallas_call(kernel, out_shape=tuple((pltpu.HBM(o[0].shape, o[0].dtype)...  118 us
    ppermute x26, waiting for transfers between devices, _ex(): return lax.ppermute(v, 'expert', pairs)  68.4 us
    ppermute x26, starting transfers between devices, _ex(): return lax.ppermute(v, 'expert', pairs)  44.7 us
    ppermute x26, waiting for transfers between devices, _dp(): return lax.ppermute(v, 'dp', pairs)  31.5 us
    pallas_call x2, Pallas kernels, expert_grad(): pl.pallas_call(functools.partial(kernel, grid), out_shape=[pltpu.HBM((Y,...  19.7 us
    ppermute x26, starting transfers between devices, _dp(): return lax.ppermute(v, 'dp', pairs)  17.5 us
    unnamed x104, local copies, waits for them, and re-layouts  12.5 us
    pallas_call x4, Pallas kernels, added_blocks(): pl.pallas_call(kernel, out_shape=[pltpu.HBM(dims, dtype)] * results, grid...  11.9 us
  transfers between devices with their start and end apart: 56, of which 16 were waited for; matrix products, arithmetic and copies ran while one was open for 1% of the time, Pallas kernels for 40%

profile of v3, /device:TPU:0, one launch (start us, length us, event | category | flops | bytes accessed | tf_op | source)
XLA Modules:
  0.0 347.5 jit_solution(9762180021193007181)
XLA Ops:
  7.9 4.6 %pack.1 = (bf16[256,6400]{1,0:T(8,128)(2,1)}, bf16[256,1280]{1,0:T(8,128)(2,1)}, bf16[128,2176]{1,0:T(8,128)(2,1)}, bf16[128,2176]{1,0:T(8,128)(2,1)}, bf16[128,2048]{1,0:T(8,128)(2,1)}) custom-call(s32[4]{0:T(128)} %pad_add_fusion.idx, bf16[256,512]{1,0:T(8,128)(2,1)} %q.1, bf16[256,512]{1,0:T(8,128)(2,1)} %k.1, bf16[20,256]{1,0:T(8,128)(2,1)} %bitcast.35, ...), custom_call_target="tpu_custom_call" | custom-call | flops 3 | bytes 3 | tf_op jit(solution)/shard_map/pack/pallas_call | solution.py:701
  13.0 2.6 collective-permute-start.1
  18.2 11.0 %collective-permute-done.1.rest_2_ = bf16[128,2176]{1,0:T(8,128)(2,1)} collective-permute-done((bf16[128,2176]{1,0:T(8,128)(2,1)}, bf16[128,2176]{1,0:T(8,128)(2,1)}, u32[]{:S(2)}, u32[]{:S(2)}) %collective-permute-start.1) | collective-permute-done | bytes 557088 | tf_op jit(solution)/shard_map/ppermute | solution.py:75
  32.5 13.2 %collective-permute-done.3.rest_4_ = bf16[128,2176]{1,0:T(8,128)(2,1)S(1)} collective-permute-done((bf16[128,2176]{1,0:T(8,128)(2,1)}, bf16[128,2176]{1,0:T(8,128)(2,1)S(1)}, u32[]{:S(2)}, u32[]{:S(2)}) %collective-permute-start.3) | collective-permute-done | bytes 557088 | tf_op jit(solution)/shard_map/ppermute | solution.py:83
  46.8 2.2 collective-permute-start.7
  50.3 12.8 %collective-permute-done.8.rest_16_.rest_6_.rest_10_ = bf16[128,2048]{1,0:T(8,128)(2,1)} collective-permute-done((bf16[128,2048]{1,0:T(8,128)(2,1)}, bf16[128,2048]{1,0:T(8,128)(2,1)}, u32[]{:S(2)}, u32[]{:S(2)}) %collective-permute-start.8) | collective-permute-done | bytes 524320 | tf_op jit(solution)/shard_map/ppermute | solution.py:75
  63.1 4.6 %collective-permute-done.7.rest_8_.rest_14_.rest_4_ = bf16[128,2176]{1,0:T(8,128)(2,1)} collective-permute-done((bf16[128,2176]{1,0:T(8,128)(2,1)S(1)}, bf16[128,2176]{1,0:T(8,128)(2,1)}, u32[]{:S(2)}, u32[]{:S(2)}) %collective-permute-start.7) | collective-permute-done | bytes 557088 | tf_op jit(solution)/shard_map/ppermute | solution.py:83
  73.4 4.5 %attend.1 = (bf16[128,1024]{1,0:T(8,128)(2,1)}, bf16[128,1024]{1,0:T(8,128)(2,1)}, f32[128,128]{1,0:T(8,128)}, f32[128,128]{1,0:T(8,128)}, f32[128,512]{1,0:T(8,128)}, /*index=5*/bf16[1024,256]{1,0:T(8,128)(2,1)}) custom-call(s32[4]{0:T(128)} %pad_add_fusion.idx, bf16[128,1024]{1,0:T(8,128)(2,1)} %bitcast.27, s32[1,128]{1,0:T(1,128)} %reshape.62.seg_ref, ...), custom_call_target="tpu_custom_call" | custom-call | flops 4 | bytes 4 | tf_op jit(solution)/shard_map/attend/pallas_call | solution.py:701
  77.9 5.5 %collective-permute-done.12.rest_18_.rest_8_.rest_12_ = bf16[128,2048]{1,0:T(8,128)(2,1)} collective-permute-done((bf16[128,2048]{1,0:T(8,128)(2,1)}, bf16[128,2048]{1,0:T(8,128)(2,1)}, u32[]{:S(2)}, u32[]{:S(2)}) %collective-permute-start.12) | collective-permute-done | bytes 524320 | tf_op jit(solution)/shard_map/ppermute | solution.py:83
  83.4 2.1 collective-permute-done.14.rest_19_.rest_9_.rest_13_
  86.3 10.3 %route.1 = (bf16[128,512]{1,0:T(8,128)(2,1)}, f32[128,2560]{1,0:T(8,128)}, f32[128,640]{1,0:T(8,128)}, f32[128,1024]{1,0:T(8,128)}, f32[128,128]{1,0:T(8,128)}, ...) custom-call(s32[4]{0:T(128)} %pad_add_fusion.idx, bf16[128,1024]{1,0:T(8,128)(2,1)} %bitcast.28, ...), custom_call_target="tpu_custom_call" | custom-call | flops 8 | bytes 8 | tf_op jit(solution)/shard_map/route/pallas_call | solution.py:701
  101.4 7.8 %collective-permute-done.15.rest_1_ = bf16[128,1152]{1,0:T(8,128)(2,1)S(1)} collective-permute-done((bf16[128,1152]{1,0:T(8,128)(2,1)}, bf16[128,1152]{1,0:T(8,128)(2,1)S(1)}, u32[]{:S(2)}, u32[]{:S(2)}) %collective-permute-start.15) | collective-permute-done | bytes 294944 | tf_op jit(solution)/shard_map/ppermute | solution.py:83
  111.7 7.3 %collective-permute-done.17.rest_2_ = bf16[128,1152]{1,0:T(8,128)(2,1)S(1)} collective-permute-done((bf16[128,1152]{1,0:T(8,128)(2,1)S(1)}, bf16[128,1152]{1,0:T(8,128)(2,1)S(1)}, u32[]{:S(2)}, u32[]{:S(2)}) %collective-permute-start.17) | collective-permute-done | bytes 294944 | tf_op jit(solution)/shard_map/ppermute | solution.py:83
  119.1 2.8 collective-permute-done.20.rest_10_
  121.8 2.7 collective-permute-done.25.rest_11_
  125.5 2.3 collective-permute-start.22
  130.2 9.2 %ahead.1.gh_ref = bf16[1024,2048]{1,0:T(8,128)(2,1)} custom-call(s32[4]{0:T(128)} %pad_add_fusion.idx, bf16[8,2,64,1024]{3,2,1,0:T(8,128)(2,1)} %bitcast.22, bf16[16,128,256]{2,1,0:T(8,128)(2,1)} %rest_0_.3, bf16[16,128,256]{2,1,0:T(8,128)(2,1)} %copy-done.11, bf16[16,128,256]{2,1,0:T(8,128)(2,1)} %collective-permute-done.19.rest_2_, ...), custom_call_target="tpu_custom_call" | custom-call | flops 9 | bytes 9 | tf_op jit(solution)/shard_map/ahead/pallas_call | solution.py:701
  140.1 8.2 %collective-permute-done.24.rest_7_ = bf16[128,1152]{1,0:T(8,128)(2,1)S(1)} collective-permute-done((bf16[128,1152]{1,0:T(8,128)(2,1)S(1)}, bf16[128,1152]{1,0:T(8,128)(2,1)S(1)}, u32[]{:S(2)}, u32[]{:S(2)}) %collective-permute-start.24) | collective-permute-done | bytes 294944 | tf_op jit(solution)/shard_map/ppermute | solution.py:83
  149.0 16.2 %experts.2 = (bf16[1024,2048]{1,0:T(8,128)(2,1)}, bf16[1024,2048]{1,0:T(8,128)(2,1)}, bf16[1024,1152]{1,0:T(8,128)(2,1)}, bf16[4,64,1152]{2,1,0:T(8,128)(2,1)}, bf16[4,64,1152]{2,1,0:T(8,128)(2,1)}) custom-call(s32[4]{0:T(128)} %pad_add_fusion.idx, bf16[1024,2048]{1,0:T(8,128)(2,1)} %ahead.1.gh_ref, bf16[128,1152]{1,0:T(8,128)(2,1)} %get-tuple-element.152.rest_0_, ...), custom_call_target="tpu_custom_call" | custom-call | flops 12 | bytes 12 | tf_op jit(solution)/shard_map/experts/pallas_call | solution.py:701
  165.6 15.8 %experts.3 = (bf16[1024,2048]{1,0:T(8,128)(2,1)}, bf16[1024,2048]{1,0:T(8,128)(2,1)}, bf16[1024,1152]{1,0:T(8,128)(2,1)}, bf16[4,64,1152]{2,1,0:T(8,128)(2,1)}, bf16[4,64,1152]{2,1,0:T(8,128)(2,1)}) custom-call(s32[4]{0:T(128)} %pad_add_fusion.idx, bf16[1024,2048]{1,0:T(8,128)(2,1)} %ahead.1.gh_ref, ...), custom_call_target="tpu_custom_call", output_to_operand_aliasing={{0}: (14, {}), {1}: (15, {}), {2}: (16, {})} | custom-call | flops 12 | bytes 12 | tf_op jit(solution)/shard_map/experts/pallas_call | solution.py:701
  183.9 2.1 fold.2
  189.3 2.4 collective-permute-start.29
  191.7 9.9 %out.1 = bf16[8,128,1024]{2,1,0:T(8,128)(2,1)} custom-call(s32[4]{0:T(128)} %pad_add_fusion.idx, bf16[1024,2048]{1,0:T(8,128)(2,1)} %get-tuple-element.169.hg_ref, bf16[16,128,256]{2,1,0:T(8,128)(2,1)} %rest_0_.3, bf16[16,128,256]{2,1,0:T(8,128)(2,1)} %copy-done.11, bf16[16,128,256]{2,1,0:T(8,128)(2,1)} %collective-permute-done.19.rest_2_, ...), custom_call_target="tpu_custom_call" | custom-call | flops 10 | bytes 10 | tf_op jit(solution)/shard_map/out/pallas_call | solution.py:701
  202.5 2.1 fold.3
  206.1 2.4 collective-permute-start.33
  208.5 10.0 %down_grad.1 = (bf16[2,16,128,256]{3,2,1,0:T(8,128)(2,1)}, bf16[2,16,128,256]{3,2,1,0:T(8,128)(2,1)}) custom-call(s32[4]{0:T(128)} %pad_add_fusion.idx, bf16[8,2,64,1024]{3,2,1,0:T(8,128)(2,1)} %bitcast.23, bf16[1024,2048]{1,0:T(8,128)(2,1)} %get-tuple-element.169.hg_ref), custom_call_target="tpu_custom_call" | custom-call | flops 4 | bytes 12 | tf_op jit(solution)/shard_map/down_grad/pallas_call | solution.py:1017
  218.5 9.7 %up_grad.1 = (bf16[2,16,256,128]{3,2,1,0:T(8,128)(2,1)}, bf16[2,16,256,128]{3,2,1,0:T(8,128)(2,1)}) custom-call(s32[4]{0:T(128)} %pad_add_fusion.idx, bf16[1024,1152]{1,0:T(8,128)(2,1)} %get-tuple-element.182.x_ref, bf16[1024,2048]{1,0:T(8,128)(2,1)} %get-tuple-element.183.pg_ref), custom_call_target="tpu_custom_call" | custom-call | flops 4 | bytes 12 | tf_op jit(solution)/shard_map/up_grad/pallas_call | solution.py:1017
  229.1 3.3 back_norm.1
  232.4 4.0 %all-to-all-start = ((bf16[8,128,1024]{2,1,0:T(8,128)(2,1)}), bf16[8,128,1024]{2,1,0:T(8,128)(2,1)S(1)}, u32[]{:S(2)}, u32[]{:S(2)}) async-start(bf16[8,128,1024]{2,1,0:T(8,128)(2,1)} %out.1), calls=%async_computation | async-start | bytes 4194304 | tf_op jit(solution)/shard_map/all_to_all | solution.py:1111
  239.1 8.9 %back_attend.1 = (bf16[128,1792]{1,0:T(8,128)(2,1)}, bf16[128,2560]{1,0:T(8,128)(2,1)}) custom-call(s32[4]{0:T(128)} %pad_add_fusion.idx, bf16[128,1024]{1,0:T(8,128)(2,1)} %get-tuple-element.194.bg_ref, bf16[128,128]{1,0:T(8,128)(2,1)} %get-tuple-element.197.rg_ref, f32[128,128]{1,0:T(8,128)} %get-tuple-element.140.sig_ref, ...), custom_call_target="tpu_custom_call" | custom-call | flops 8 | bytes 8 | tf_op jit(solution)/shard_map/back_attend/pallas_call | solution.py:701
  249.7 3.3 core_sum.2
  254.4 3.4 core_sum.3
  257.8 4.3 %grad_out.1 = (bf16[4,32,2560]{2,1,0:T(8,128)(2,1)}, bf16[4,32,2560]{2,1,0:T(8,128)(2,1)}) custom-call(s32[4]{0:T(128)} %pad_add_fusion.idx, f32[4,128,640]{2,1,0:T(8,128)} %bitcast.24, bf16[128,256]{1,0:T(8,128)(2,1)} %get-tuple-element.213.refs_0_, bf16[128,256]{1,0:T(8,128)(2,1)} %copy-done.40, bf16[128,256]{1,0:T(8,128)(2,1)} %copy-done.41, ...), custom_call_target="tpu_custom_call" | custom-call | flops 3 | bytes 3 | tf_op jit(solution)/shard_map/grad_out/pallas_call | solution.py:701
  265.5 6.5 %grad_rest.1 = (bf16[4,32,3840]{2,1,0:T(8,128)(2,1)}, bf16[4,32,3840]{2,1,0:T(8,128)(2,1)}) custom-call(s32[4]{0:T(128)} %pad_add_fusion.idx, bf16[4,128,3072]{2,1,0:T(8,128)(2,1)} %bitcast.26, f32[4,128,640]{2,1,0:T(8,128)} %bitcast.25, bf16[256,1280]{1,0:T(8,128)(2,1)} %get-tuple-element.219.a_ref, bf16[128,1792]{1,0:T(8,128)(2,1)} %get-tuple-element.233.refs_0_.late_ref, ...), custom_call_target="tpu_custom_call" | custom-call | flops 3 | bytes 3 | tf_op jit(solution)/shard_map/grad_rest/pallas_call | solution.py:701
  275.4 8.3 %collective-permute-done.42.refs_0_ = bf16[4,32,2560]{2,1,0:T(8,128)(2,1)S(1)} collective-permute-done((bf16[4,32,2560]{2,1,0:T(8,128)(2,1)}, bf16[4,32,2560]{2,1,0:T(8,128)(2,1)S(1)}, u32[]{:S(2)}, u32[]{:S(2)}) %collective-permute-start.42) | collective-permute-done | bytes 655392 | tf_op jit(solution)/shard_map/ppermute | solution.py:83
  284.6 2.2 fold_at.2
  286.8 3.9 %collective-permute-start.43 = (bf16[32,2560]{1,0:T(8,128)(2,1)}, bf16[32,2560]{1,0:T(8,128)(2,1)S(1)}, u32[]{:S(2)}, u32[]{:S(2)}) collective-permute-start(bf16[32,2560]{1,0:T(8,128)(2,1)} %get-tuple-element.227), channel_id=1, source_target_pairs={{0,2},{1,3},{2,4},{3,5},{4,6},{5,7},{6,0},{7,1},{8,10},{9,11},{10,... | collective-permute-start | bytes 491528 | tf_op jit(solution)/shard_map/ppermute | solution.py:83
  292.3 4.5 %collective-permute-done.43.refs_1_ = bf16[32,2560]{1,0:T(8,128)(2,1)S(1)} collective-permute-done((bf16[32,2560]{1,0:T(8,128)(2,1)}, bf16[32,2560]{1,0:T(8,128)(2,1)S(1)}, u32[]{:S(2)}, u32[]{:S(2)}) %collective-permute-start.43) | collective-permute-done | bytes 163872 | tf_op jit(solution)/shard_map/ppermute | solution.py:83
  298.4 4.0 %collective-permute-done.44.refs_2_ = bf16[32,2560]{1,0:T(8,128)(2,1)S(1)} collective-permute-done((bf16[32,2560]{1,0:T(8,128)(2,1)}, bf16[32,2560]{1,0:T(8,128)(2,1)S(1)}, u32[]{:S(2)}, u32[]{:S(2)}) %collective-permute-start.44) | collective-permute-done | bytes 163872 | tf_op jit(solution)/shard_map/ppermute | solution.py:83
  302.4 5.0 %collective-permute-done.45.refs_3_ = bf16[32,2560]{1,0:T(8,128)(2,1)} collective-permute-done((bf16[32,2560]{1,0:T(8,128)(2,1)}, bf16[32,2560]{1,0:T(8,128)(2,1)}, u32[]{:S(2)}, u32[]{:S(2)}) %collective-permute-start.45) | collective-permute-done | bytes 163872 | tf_op jit(solution)/shard_map/ppermute | solution.py:83
  307.4 3.4 fold_at.3
  310.7 2.4 collective-permute-start.49
  314.6 3.2 collective-permute-start.51
  317.7 8.3 %back_token.1 = f32[128,1024]{1,0:T(8,128)} custom-call(s32[4]{0:T(128)} %pad_add_fusion.idx, bf16[128,1024]{1,0:T(8,128)(2,1)} %bitcast.29, f32[128,1024]{1,0:T(8,128)} %get-tuple-element.196.rg_ref, bf16[128,1792]{1,0:T(8,128)(2,1)} %get-tuple-element.233.refs_0_.late_ref, bf16[128,2560]{1,0:T(8,128)(2,1)} %get-tuple-element.234.vag_ref, ...), custom_call_target="tpu_custom_call" | custom-call | flops 8 | bytes 8 | tf_op jit(solution)/shard_map/back_token/pallas_call | solution.py:701
  326.1 2.7 add_out.1
  330.8 2.6 last_sum.2
  334.4 2.6 last_sum.3
  338.5 2.2 finish.1
  (203 shorter events, 59.8 us)
Async XLA Ops:
  7.2 70.7 %all-gather.6.cloned.1.call-start = ((), (), s32[]{:S(2)}) async-start(), calls=%async_computation.1 | async-start | bytes 2359296 | tf_op jit(solution)/shard_map/all_gather | solution.py:806
  12.5 16.7 %collective-permute-start = (bf16[256,6400]{1,0:T(8,128)(2,1)}, bf16[256,6400]{1,0:T(8,128)(2,1)S(1)}, u32[]{:S(2)}, u32[]{:S(2)}) collective-permute-start(bf16[256,6400]{1,0:T(8,128)(2,1)} %get-tuple-element.133.rest_0_.rest_10_), channel_id=1, source_target_pairs={{0,8},{8,0},{16,24},{24,16},{1,9},{9,1},{17,25},{25,17},{2,10},{10... | collective-permute-start | bytes 9830408 | tf_op jit(solution)/shard_map/ppermute | solution.py:75
  12.9 215.3 %all-gather.8.cloned.1.call-start = ((), (), s32[]{:S(2)}) async-start(), calls=%async_computation.2 | async-start | bytes 1638400 | tf_op jit(solution)/shard_map/all_gather | solution.py:1078
  13.0 16.2 %collective-permute-start.1 = (bf16[128,2176]{1,0:T(8,128)(2,1)}, bf16[128,2176]{1,0:T(8,128)(2,1)}, u32[]{:S(2)}, u32[]{:S(2)}) collective-permute-start(bf16[128,2176]{1,0:T(8,128)(2,1)} %get-tuple-element.134), channel_id=1, source_target_pairs={{0,16},{8,24},{16,0},{24,8},{1,17},{9,25},{17,1},{25,9},{2,18},{10... | collective-permute-start | bytes 1671176 | tf_op jit(solution)/shard_map/ppermute | solution.py:75
  29.2 16.5 %collective-permute-start.3 = (bf16[128,2176]{1,0:T(8,128)(2,1)}, bf16[128,2176]{1,0:T(8,128)(2,1)S(1)}, u32[]{:S(2)}, u32[]{:S(2)}) collective-permute-start(bf16[128,2176]{1,0:T(8,128)(2,1)} %collective-permute-done.1.rest_2_), channel_id=1, source_target_pairs={{0,1},{1,0},{2,3},{3,2},{4,5},{5,4},{6,7},{7,6},{8,9},{9,8},{10,11... | collective-permute-start | bytes 1671176 | tf_op jit(solution)/shard_map/ppermute | solution.py:83
  31.0 14.9 %collective-permute-start.4 = (bf16[128,2176]{1,0:T(8,128)(2,1)}, bf16[128,2176]{1,0:T(8,128)(2,1)S(1)}, u32[]{:S(2)}, u32[]{:S(2)}) collective-permute-start(bf16[128,2176]{1,0:T(8,128)(2,1)} %get-tuple-element.137), channel_id=1, source_target_pairs={{0,16},{8,24},{16,0},{24,8},{1,17},{9,25},{17,1},{25,9},{2,18},{10... | collective-permute-start | bytes 1671176 | tf_op jit(solution)/shard_map/ppermute | solution.py:75
  45.9 21.9 %collective-permute-start.9 = (bf16[16,128,256]{2,1,0:T(8,128)(2,1)}, bf16[16,128,256]{2,1,0:T(8,128)(2,1)S(1)}, u32[]{:S(2)}, u32[]{:S(2)}) collective-permute-start(bf16[16,128,256]{2,1,0:T(8,128)(2,1)} %rest_0_.3), channel_id=1, source_target_pairs={{0,8},{8,0},{16,24},{24,16},{1,9},{9,1},{17,25},{25,17},{2,10},{10... | collective-permute-start | bytes 3145736 | tf_op jit(solution)/shard_map/ppermute | solution.py:75
  45.9 17.2 %collective-permute-start.5 = (bf16[128,2176]{1,0:T(8,128)(2,1)S(1)}, bf16[128,2176]{1,0:T(8,128)(2,1)S(1)}, u32[]{:S(2)}, u32[]{:S(2)}) collective-permute-start(bf16[128,2176]{1,0:T(8,128)(2,1)S(1)} %collective-permute-done.3.rest_4_), channel_id=1, source_target_pairs={{0,8},{8,0},{16,24},{24,16},{1,9},{9,1},{17,25},{25,17},{2,10},{10... | collective-permute-start | bytes 1671176 | tf_op jit(solution)/shard_map/ppermute | solution.py:75
  46.4 16.7 %collective-permute-start.6 = (bf16[128,2176]{1,0:T(8,128)(2,1)S(1)}, bf16[128,2176]{1,0:T(8,128)(2,1)S(1)}, u32[]{:S(2)}, u32[]{:S(2)}) collective-permute-start(bf16[128,2176]{1,0:T(8,128)(2,1)S(1)} %collective-permute-done.4.rest_6_.rest_12_.rest_2_), channel_id=1, source_target_pairs={{0,8},{8,0},{16,24},{24,16},{1,9},{9,1},{17,25},{25,17},{2,10},{10... | collective-permute-start | bytes 1671176 | tf_op jit(solution)/shard_map/ppermute | solution.py:75
  46.8 21.0 %collective-permute-start.7 = (bf16[128,2176]{1,0:T(8,128)(2,1)S(1)}, bf16[128,2176]{1,0:T(8,128)(2,1)}, u32[]{:S(2)}, u32[]{:S(2)}) collective-permute-start(bf16[128,2176]{1,0:T(8,128)(2,1)S(1)} %collective-permute-done.4.rest_6_.rest_12_.rest_2_), channel_id=1, source_target_pairs={{0,1},{1,0},{2,3},{3,2},{4,5},{5,4},{6,7},{7,6},{8,9},{9,8},{10,11... | collective-permute-start | bytes 1671176 | tf_op jit(solution)/shard_map/ppermute | solution.py:83
  49.0 14.1 %collective-permute-start.8 = (bf16[128,2048]{1,0:T(8,128)(2,1)}, bf16[128,2048]{1,0:T(8,128)(2,1)}, u32[]{:S(2)}, u32[]{:S(2)}) collective-permute-start(bf16[128,2048]{1,0:T(8,128)(2,1)} %get-tuple-element.146), channel_id=1, source_target_pairs={{0,16},{8,24},{16,0},{24,8},{1,17},{9,25},{17,1},{25,9},{2,18},{10... | collective-permute-start | bytes 1572872 | tf_op jit(solution)/shard_map/ppermute | solution.py:75
  67.7 15.6 %collective-permute-start.13 = (bf16[16,256,128]{2,1,0:T(8,128)(2,1)}, bf16[16,256,128]{2,1,0:T(8,128)(2,1)}, u32[]{:S(2)}, u32[]{:S(2)}) collective-permute-start(bf16[16,256,128]{2,1,0:T(8,128)(2,1)} %rest_8_.3), channel_id=1, source_target_pairs={{0,8},{8,0},{16,24},{24,16},{1,9},{9,1},{17,25},{25,17},{2,10},{10... | collective-permute-start | bytes 3145736 | tf_op jit(solution)/shard_map/ppermute | solution.py:75
  67.8 15.5 %collective-permute-start.10 = (bf16[128,2176]{1,0:T(8,128)(2,1)}, bf16[128,2176]{1,0:T(8,128)(2,1)}, u32[]{:S(2)}, u32[]{:S(2)}) collective-permute-start(bf16[128,2176]{1,0:T(8,128)(2,1)} %collective-permute-done.7.rest_8_.rest_14_.rest_4_), channel_id=1, source_target_pairs={{0,8},{8,0},{16,24},{24,16},{1,9},{9,1},{17,25},{25,17},{2,10},{10... | collective-permute-start | bytes 1671176 | tf_op jit(solution)/shard_map/ppermute | solution.py:75
  68.7 9.2 %collective-permute-start.11 = (bf16[128,2048]{1,0:T(8,128)(2,1)}, bf16[128,2048]{1,0:T(8,128)(2,1)}, u32[]{:S(2)}, u32[]{:S(2)}) collective-permute-start(bf16[128,2048]{1,0:T(8,128)(2,1)} %collective-permute-done.8.rest_16_.rest_6_.rest_10_), channel_id=1, source_target_pairs={{0,8},{8,0},{16,24},{24,16},{1,9},{9,1},{17,25},{25,17},{2,10},{10... | collective-permute-start | bytes 1572872 | tf_op jit(solution)/shard_map/ppermute | solution.py:75
  68.7 14.7 %collective-permute-start.12 = (bf16[128,2048]{1,0:T(8,128)(2,1)}, bf16[128,2048]{1,0:T(8,128)(2,1)}, u32[]{:S(2)}, u32[]{:S(2)}) collective-permute-start(bf16[128,2048]{1,0:T(8,128)(2,1)} %collective-permute-done.8.rest_16_.rest_6_.rest_10_), channel_id=1, source_target_pairs={{0,1},{1,0},{2,3},{3,2},{4,5},{5,4},{6,7},{7,6},{8,9},{9,8},{10,11... | collective-permute-start | bytes 1572872 | tf_op jit(solution)/shard_map/ppermute | solution.py:83
  70.4 26.1 %collective-permute-start.19 = (bf16[16,128,256]{2,1,0:T(8,128)(2,1)}, bf16[16,128,256]{2,1,0:T(8,128)(2,1)}, u32[]{:S(2)}, u32[]{:S(2)}) collective-permute-start(bf16[16,128,256]{2,1,0:T(8,128)(2,1)} %rest_0_.3), channel_id=1, source_target_pairs={{0,16},{8,24},{16,0},{24,8},{1,17},{9,25},{17,1},{25,9},{2,18},{10... | collective-permute-start | bytes 3145736 | tf_op jit(solution)/shard_map/ppermute | solution.py:75
  96.6 25.3 %collective-permute-start.20 = (bf16[16,256,128]{2,1,0:T(8,128)(2,1)S(1)}, bf16[16,256,128]{2,1,0:T(8,128)(2,1)S(1)}, u32[]{:S(2)}, u32[]{:S(2)}) collective-permute-start(bf16[16,256,128]{2,1,0:T(8,128)(2,1)S(1)} %copy-done.8), channel_id=1, source_target_pairs={{0,16},{8,24},{16,0},{24,8},{1,17},{9,25},{17,1},{25,9},{2,18},{10... | collective-permute-start | bytes 3145736 | tf_op jit(solution)/shard_map/ppermute | solution.py:75
  98.4 10.9 %collective-permute-start.15 = (bf16[128,1152]{1,0:T(8,128)(2,1)}, bf16[128,1152]{1,0:T(8,128)(2,1)S(1)}, u32[]{:S(2)}, u32[]{:S(2)}) collective-permute-start(bf16[128,1152]{1,0:T(8,128)(2,1)} %get-tuple-element.152.rest_0_), channel_id=1, source_target_pairs={{0,2},{1,3},{2,4},{3,5},{4,6},{5,7},{6,0},{7,1},{8,10},{9,11},{10,... | collective-permute-start | bytes 884744 | tf_op jit(solution)/shard_map/ppermute | solution.py:83
  100.0 9.3 %collective-permute-start.16 = (bf16[128,1152]{1,0:T(8,128)(2,1)}, bf16[128,1152]{1,0:T(8,128)(2,1)S(1)}, u32[]{:S(2)}, u32[]{:S(2)}) collective-permute-start(bf16[128,1152]{1,0:T(8,128)(2,1)} %get-tuple-element.152.rest_0_), channel_id=1, source_target_pairs={{0,1},{1,0},{2,3},{3,2},{4,5},{5,4},{6,7},{7,6},{8,9},{9,8},{10,11... | collective-permute-start | bytes 884744 | tf_op jit(solution)/shard_map/ppermute | solution.py:83
  109.2 9.8 %collective-permute-start.17 = (bf16[128,1152]{1,0:T(8,128)(2,1)S(1)}, bf16[128,1152]{1,0:T(8,128)(2,1)S(1)}, u32[]{:S(2)}, u32[]{:S(2)}) collective-permute-start(bf16[128,1152]{1,0:T(8,128)(2,1)S(1)} %collective-permute-done.15.rest_1_), channel_id=1, source_target_pairs={{0,2},{1,3},{2,4},{3,5},{4,6},{5,7},{6,0},{7,1},{8,10},{9,11},{10,... | collective-permute-start | bytes 884744 | tf_op jit(solution)/shard_map/ppermute | solution.py:83
  124.5 103.7 %all-gather.10.cloned.1.call-start = ((), (), s32[]{:S(2)}) async-start(), calls=%async_computation.3 | async-start | bytes 3932160 | tf_op jit(solution)/shard_map/all_gather | solution.py:1079
  125.5 14.0 %collective-permute-start.22 = (bf16[128,1152]{1,0:T(8,128)(2,1)S(1)}, bf16[128,1152]{1,0:T(8,128)(2,1)S(1)}, u32[]{:S(2)}, u32[]{:S(2)}) collective-permute-start(bf16[128,1152]{1,0:T(8,128)(2,1)S(1)} %collective-permute-done.17.rest_2_), channel_id=1, source_target_pairs={{0,2},{1,3},{2,4},{3,5},{4,6},{5,7},{6,0},{7,1},{8,10},{9,11},{10,... | collective-permute-start | bytes 884744 | tf_op jit(solution)/shard_map/ppermute | solution.py:83
  127.8 11.7 %collective-permute-start.23 = (bf16[128,1152]{1,0:T(8,128)(2,1)S(1)}, bf16[128,1152]{1,0:T(8,128)(2,1)S(1)}, u32[]{:S(2)}, u32[]{:S(2)}) collective-permute-start(bf16[128,1152]{1,0:T(8,128)(2,1)S(1)} %collective-permute-done.17.rest_2_), channel_id=1, source_target_pairs={{0,1},{1,0},{2,3},{3,2},{4,5},{5,4},{6,7},{7,6},{8,9},{9,8},{10,11... | collective-permute-start | bytes 884744 | tf_op jit(solution)/shard_map/ppermute | solution.py:83
  165.2 17.9 %collective-permute-start.26 = (bf16[4,64,1152]{2,1,0:T(8,128)(2,1)}, bf16[4,64,1152]{2,1,0:T(8,128)(2,1)S(1)}, u32[]{:S(2)}, u32[]{:S(2)}) collective-permute-start(bf16[4,64,1152]{2,1,0:T(8,128)(2,1)} %get-tuple-element.167), channel_id=1, source_target_pairs={{0,1},{1,0},{2,3},{3,2},{4,5},{5,4},{6,7},{7,6},{8,9},{9,8},{10,11... | collective-permute-start | bytes 1769480 | tf_op jit(solution)/shard_map/ppermute | solution.py:83
  181.4 20.3 %collective-permute-start.30 = (bf16[4,64,1152]{2,1,0:T(8,128)(2,1)}, bf16[4,64,1152]{2,1,0:T(8,128)(2,1)S(1)}, u32[]{:S(2)}, u32[]{:S(2)}) collective-permute-start(bf16[4,64,1152]{2,1,0:T(8,128)(2,1)} %get-tuple-element.178), channel_id=1, source_target_pairs={{0,1},{1,0},{2,3},{3,2},{4,5},{5,4},{6,7},{7,6},{8,9},{9,8},{10,11... | collective-permute-start | bytes 1769480 | tf_op jit(solution)/shard_map/ppermute | solution.py:83
  186.0 15.6 %collective-permute-start.27 = (bf16[64,1152]{1,0:T(8,128)(2,1)}, bf16[64,1152]{1,0:T(8,128)(2,1)S(1)}, u32[]{:S(2)}, u32[]{:S(2)}) collective-permute-start(bf16[64,1152]{1,0:T(8,128)(2,1)} %get-tuple-element.174), channel_id=1, source_target_pairs={{0,2},{1,3},{2,4},{3,5},{4,6},{5,7},{6,0},{7,1},{8,10},{9,11},{10,... | collective-permute-start | bytes 442376 | tf_op jit(solution)/shard_map/ppermute | solution.py:83
  187.5 14.1 %collective-permute-start.28 = (bf16[64,1152]{1,0:T(8,128)(2,1)}, bf16[64,1152]{1,0:T(8,128)(2,1)S(1)}, u32[]{:S(2)}, u32[]{:S(2)}) collective-permute-start(bf16[64,1152]{1,0:T(8,128)(2,1)} %get-tuple-element.175), channel_id=1, source_target_pairs={{0,4},{1,5},{2,6},{3,7},{4,0},{5,1},{6,2},{7,3},{8,12},{9,13},{10,... | collective-permute-start | bytes 442376 | tf_op jit(solution)/shard_map/ppermute | solution.py:83
  189.3 12.4 %collective-permute-start.29 = (bf16[64,1152]{1,0:T(8,128)(2,1)}, bf16[64,1152]{1,0:T(8,128)(2,1)S(1)}, u32[]{:S(2)}, u32[]{:S(2)}) collective-permute-start(bf16[64,1152]{1,0:T(8,128)(2,1)} %get-tuple-element.176), channel_id=1, source_target_pairs={{0,6},{1,7},{2,0},{3,1},{4,2},{5,3},{6,4},{7,5},{8,14},{9,15},{10,... | collective-permute-start | bytes 442376 | tf_op jit(solution)/shard_map/ppermute | solution.py:83
  204.7 23.6 %collective-permute-start.31 = (bf16[64,1152]{1,0:T(8,128)(2,1)}, bf16[64,1152]{1,0:T(8,128)(2,1)S(1)}, u32[]{:S(2)}, u32[]{:S(2)}) collective-permute-start(bf16[64,1152]{1,0:T(8,128)(2,1)} %get-tuple-element.191), channel_id=1, source_target_pairs={{0,2},{1,3},{2,4},{3,5},{4,6},{5,7},{6,0},{7,1},{8,10},{9,11},{10,... | collective-permute-start | bytes 442376 | tf_op jit(solution)/shard_map/ppermute | solution.py:83
  204.7 23.6 %collective-permute-start.32 = (bf16[64,1152]{1,0:T(8,128)(2,1)}, bf16[64,1152]{1,0:T(8,128)(2,1)S(1)}, u32[]{:S(2)}, u32[]{:S(2)}) collective-permute-start(bf16[64,1152]{1,0:T(8,128)(2,1)} %get-tuple-element.192), channel_id=1, source_target_pairs={{0,4},{1,5},{2,6},{3,7},{4,0},{5,1},{6,2},{7,3},{8,12},{9,13},{10,... | collective-permute-start | bytes 442376 | tf_op jit(solution)/shard_map/ppermute | solution.py:83
  206.1 22.2 %collective-permute-start.33 = (bf16[64,1152]{1,0:T(8,128)(2,1)}, bf16[64,1152]{1,0:T(8,128)(2,1)S(1)}, u32[]{:S(2)}, u32[]{:S(2)}) collective-permute-start(bf16[64,1152]{1,0:T(8,128)(2,1)} %get-tuple-element.193), channel_id=1, source_target_pairs={{0,6},{1,7},{2,0},{3,1},{4,2},{5,3},{6,4},{7,5},{8,14},{9,15},{10,... | collective-permute-start | bytes 442376 | tf_op jit(solution)/shard_map/ppermute | solution.py:83
  232.4 75.0 %all-to-all-start = ((bf16[8,128,1024]{2,1,0:T(8,128)(2,1)}), bf16[8,128,1024]{2,1,0:T(8,128)(2,1)S(1)}, u32[]{:S(2)}, u32[]{:S(2)}) async-start(bf16[8,128,1024]{2,1,0:T(8,128)(2,1)} %out.1), calls=%async_computation | async-start | bytes 4194304 | tf_op jit(solution)/shard_map/all_to_all | solution.py:1111
  236.4 13.4 %collective-permute-start.34 = (bf16[2,16,128,256]{3,2,1,0:T(8,128)(2,1)}, bf16[2,16,128,256]{3,2,1,0:T(8,128)(2,1)}, u32[]{:S(2)}, u32[]{:S(2)}) collective-permute-start(bf16[2,16,128,256]{3,2,1,0:T(8,128)(2,1)} %get-tuple-element.204), channel_id=1, source_target_pairs={{0,8},{8,0},{16,24},{24,16},{1,9},{9,1},{17,25},{25,17},{2,10},{10... | collective-permute-start | bytes 6291464 | tf_op jit(solution)/shard_map/ppermute | solution.py:75
  236.4 16.6 %collective-permute-start.35 = (bf16[2,16,256,128]{3,2,1,0:T(8,128)(2,1)}, bf16[2,16,256,128]{3,2,1,0:T(8,128)(2,1)S(1)}, u32[]{:S(2)}, u32[]{:S(2)}) collective-permute-start(bf16[2,16,256,128]{3,2,1,0:T(8,128)(2,1)} %get-tuple-element.209), channel_id=1, source_target_pairs={{0,8},{8,0},{16,24},{24,16},{1,9},{9,1},{17,25},{25,17},{2,10},{10... | collective-permute-start | bytes 6291464 | tf_op jit(solution)/shard_map/ppermute | solution.py:75
  236.9 11.1 %collective-permute-start.36 = (bf16[128,256]{1,0:T(8,128)(2,1)S(1)}, bf16[128,256]{1,0:T(8,128)(2,1)S(1)}, u32[]{:S(2)}, u32[]{:S(2)}) collective-permute-start(bf16[128,256]{1,0:T(8,128)(2,1)S(1)} %copy-done.49), channel_id=1, source_target_pairs={{0,16},{8,24},{16,0},{24,8},{1,17},{9,25},{17,1},{25,9},{2,18},{10... | collective-permute-start | bytes 196616 | tf_op jit(solution)/shard_map/ppermute | solution.py:75
  238.5 9.6 %collective-permute-start.37 = (bf16[128,256]{1,0:T(8,128)(2,1)S(1)}, bf16[128,256]{1,0:T(8,128)(2,1)S(1)}, u32[]{:S(2)}, u32[]{:S(2)}) collective-permute-start(bf16[128,256]{1,0:T(8,128)(2,1)S(1)} %copy-done.48), channel_id=1, source_target_pairs={{0,8},{8,0},{16,24},{24,16},{1,9},{9,1},{17,25},{25,17},{2,10},{10... | collective-permute-start | bytes 196616 | tf_op jit(solution)/shard_map/ppermute | solution.py:75
  238.5 9.6 %collective-permute-start.38 = (bf16[128,256]{1,0:T(8,128)(2,1)S(1)}, bf16[128,256]{1,0:T(8,128)(2,1)S(1)}, u32[]{:S(2)}, u32[]{:S(2)}) collective-permute-start(bf16[128,256]{1,0:T(8,128)(2,1)S(1)} %copy-done.47), channel_id=1, source_target_pairs={{0,24},{8,16},{16,8},{24,0},{1,25},{9,17},{17,9},{25,1},{2,26},{10... | collective-permute-start | bytes 196616 | tf_op jit(solution)/shard_map/ppermute | solution.py:75
  248.1 14.0 %collective-permute-start.39 = (bf16[128,1792]{1,0:T(8,128)(2,1)}, bf16[128,1792]{1,0:T(8,128)(2,1)S(1)}, u32[]{:S(2)}, u32[]{:S(2)}) collective-permute-start(bf16[128,1792]{1,0:T(8,128)(2,1)} %get-tuple-element.233.refs_0_.late_ref), channel_id=1, source_target_pairs={{0,16},{8,24},{16,0},{24,8},{1,17},{9,25},{17,1},{25,9},{2,18},{10... | collective-permute-start | bytes 1376264 | tf_op jit(solution)/shard_map/ppermute | solution.py:75
  262.7 21.1 %collective-permute-start.42 = (bf16[4,32,2560]{2,1,0:T(8,128)(2,1)}, bf16[4,32,2560]{2,1,0:T(8,128)(2,1)S(1)}, u32[]{:S(2)}, u32[]{:S(2)}) collective-permute-start(bf16[4,32,2560]{2,1,0:T(8,128)(2,1)} %get-tuple-element.225), channel_id=1, source_target_pairs={{0,1},{1,0},{2,3},{3,2},{4,5},{5,4},{6,7},{7,6},{8,9},{9,8},{10,11... | collective-permute-start | bytes 1966088 | tf_op jit(solution)/shard_map/ppermute | solution.py:83
  272.1 35.3 %collective-permute-start.46 = (bf16[4,32,3840]{2,1,0:T(8,128)(2,1)}, bf16[4,32,3840]{2,1,0:T(8,128)(2,1)}, u32[]{:S(2)}, u32[]{:S(2)}) collective-permute-start(bf16[4,32,3840]{2,1,0:T(8,128)(2,1)} %get-tuple-element.231), channel_id=1, source_target_pairs={{0,1},{1,0},{2,3},{3,2},{4,5},{5,4},{6,7},{7,6},{8,9},{9,8},{10,11... | collective-permute-start | bytes 2949128 | tf_op jit(solution)/shard_map/ppermute | solution.py:83
  273.4 57.4 %collective-permute-start.47 = (bf16[16,128,256]{2,1,0:T(8,128)(2,1)}, bf16[16,128,256]{2,1,0:T(8,128)(2,1)}, u32[]{:S(2)}, u32[]{:S(2)}) collective-permute-start(bf16[16,128,256]{2,1,0:T(8,128)(2,1)} %get-tuple-element.238), channel_id=1, source_target_pairs={{0,16},{8,24},{16,0},{24,8},{1,17},{9,25},{17,1},{25,9},{2,18},{10... | collective-permute-start | bytes 3145736 | tf_op jit(solution)/shard_map/ppermute | solution.py:75
  273.9 59.6 %collective-permute-start.48 = (bf16[16,256,128]{2,1,0:T(8,128)(2,1)}, bf16[16,256,128]{2,1,0:T(8,128)(2,1)S(1)}, u32[]{:S(2)}, u32[]{:S(2)}) collective-permute-start(bf16[16,256,128]{2,1,0:T(8,128)(2,1)} %get-tuple-element.240), channel_id=1, source_target_pairs={{0,16},{8,24},{16,0},{24,8},{1,17},{9,25},{17,1},{25,9},{2,18},{10... | collective-permute-start | bytes 3145736 | tf_op jit(solution)/shard_map/ppermute | solution.py:75
  286.8 10.0 %collective-permute-start.43 = (bf16[32,2560]{1,0:T(8,128)(2,1)}, bf16[32,2560]{1,0:T(8,128)(2,1)S(1)}, u32[]{:S(2)}, u32[]{:S(2)}) collective-permute-start(bf16[32,2560]{1,0:T(8,128)(2,1)} %get-tuple-element.227), channel_id=1, source_target_pairs={{0,2},{1,3},{2,4},{3,5},{4,6},{5,7},{6,0},{7,1},{8,10},{9,11},{10,... | collective-permute-start | bytes 491528 | tf_op jit(solution)/shard_map/ppermute | solution.py:83
  290.7 11.7 %collective-permute-start.44 = (bf16[32,2560]{1,0:T(8,128)(2,1)}, bf16[32,2560]{1,0:T(8,128)(2,1)S(1)}, u32[]{:S(2)}, u32[]{:S(2)}) collective-permute-start(bf16[32,2560]{1,0:T(8,128)(2,1)} %get-tuple-element.228), channel_id=1, source_target_pairs={{0,4},{1,5},{2,6},{3,7},{4,0},{5,1},{6,2},{7,3},{8,12},{9,13},{10,... | collective-permute-start | bytes 491528 | tf_op jit(solution)/shard_map/ppermute | solution.py:83
  296.8 10.6 %collective-permute-start.45 = (bf16[32,2560]{1,0:T(8,128)(2,1)}, bf16[32,2560]{1,0:T(8,128)(2,1)}, u32[]{:S(2)}, u32[]{:S(2)}) collective-permute-start(bf16[32,2560]{1,0:T(8,128)(2,1)} %get-tuple-element.229), channel_id=1, source_target_pairs={{0,6},{1,7},{2,0},{3,1},{4,2},{5,3},{6,4},{7,5},{8,14},{9,15},{10,... | collective-permute-start | bytes 491528 | tf_op jit(solution)/shard_map/ppermute | solution.py:83
  310.7 26.3 %collective-permute-start.49 = (bf16[32,3840]{1,0:T(8,128)(2,1)}, bf16[32,3840]{1,0:T(8,128)(2,1)S(1)}, u32[]{:S(2)}, u32[]{:S(2)}) collective-permute-start(bf16[32,3840]{1,0:T(8,128)(2,1)} %get-tuple-element.242), channel_id=1, source_target_pairs={{0,2},{1,3},{2,4},{3,5},{4,6},{5,7},{6,0},{7,1},{8,10},{9,11},{10,... | collective-permute-start | bytes 737288 | tf_op jit(solution)/shard_map/ppermute | solution.py:83
  313.1 23.9 %collective-permute-start.50 = (bf16[32,3840]{1,0:T(8,128)(2,1)}, bf16[32,3840]{1,0:T(8,128)(2,1)S(1)}, u32[]{:S(2)}, u32[]{:S(2)}) collective-permute-start(bf16[32,3840]{1,0:T(8,128)(2,1)} %get-tuple-element.243), channel_id=1, source_target_pairs={{0,4},{1,5},{2,6},{3,7},{4,0},{5,1},{6,2},{7,3},{8,12},{9,13},{10,... | collective-permute-start | bytes 737288 | tf_op jit(solution)/shard_map/ppermute | solution.py:83
  314.6 22.5 %collective-permute-start.51 = (bf16[32,3840]{1,0:T(8,128)(2,1)}, bf16[32,3840]{1,0:T(8,128)(2,1)S(1)}, u32[]{:S(2)}, u32[]{:S(2)}) collective-permute-start(bf16[32,3840]{1,0:T(8,128)(2,1)} %get-tuple-element.244), channel_id=1, source_target_pairs={{0,6},{1,7},{2,0},{3,1},{4,2},{5,3},{6,4},{7,5},{8,14},{9,15},{10,... | collective-permute-start | bytes 737288 | tf_op jit(solution)/shard_map/ppermute | solution.py:83
  (58 other events, 569.8 us)
Sparse Core Ops, SparseCore 0:
  13.1 58.1 all-gather.5
  124.7 19.6 all-gather.7
  145.9 28.5 all-gather.9
